TPU v7x, 32 devices: a whole 2x2x4 slice. The times are simulated.
32 devices in a mesh: tensor: 4 (over z), dp: 2 (over x), context: 4 (over y, core).
Axes of the slice: x: 2, y: 2, z: 4, core: 2. Of those that a mesh axis runs over, the one named last changes fastest.
Arguments:
- tokens: bfloat16 [4, 1024, 2048], P('dp', 'context'), may hold values from -6 to 6
- segments: int32 [4, 1024], P('dp'), may hold values from 0 to 510, as said below
- expert_ids: int32 [4, 1024, 6], P('dp', 'context'), may hold values from 0 to 15, all different within a row; in each aligned block of 256 rows (0 to 255, 256 to 511, ..., all dimensions but the last counted through in order) at most 192 rows name the same one
- norm_attn: bfloat16 [2048], replicated, may hold values from 0.5 to 1.5
- w_query: bfloat16 [2048, 3072], P(None, 'tensor'), may hold values from -0.125 to 0.125
- w_kv_down: bfloat16 [2048, 576], replicated, may hold values from -0.125 to 0.125
- norm_latent: bfloat16 [512], replicated, may hold values from 0.5 to 1.5
- w_kv_up: bfloat16 [512, 4096], P(None, 'tensor'), may hold values from -0.25 to 0.25
- w_out: bfloat16 [2048, 2048], P('tensor'), may hold values from -1 to 1
- norm_ffn: bfloat16 [2048], replicated, may hold values from 0.5 to 1.5
- w_router: bfloat16 [2048, 16], replicated, may hold values from -0.0625 to 0.0625
- w_shared_gate: bfloat16 [2048, 2816], P(None, 'tensor'), may hold values from -0.125 to 0.125
- w_shared_up: bfloat16 [2048, 2816], P(None, 'tensor'), may hold values from -0.125 to 0.125
- w_shared_down: bfloat16 [2816, 2048], P('tensor'), may hold values from -0.15625 to 0.15625
- w_expert_gate: bfloat16 [16, 2048, 1408], P(('dp', 'context'), None, 'tensor'), may hold values from -0.125 to 0.125
- w_expert_up: bfloat16 [16, 2048, 1408], P(('dp', 'context'), None, 'tensor'), may hold values from -0.125 to 0.125
- w_expert_down: bfloat16 [16, 1408, 2048], P(('dp', 'context'), 'tensor'), may hold values from -2.5 to 2.5
- cotangent: bfloat16 [4, 1024, 2048], P('dp', 'context'), may hold values from -6 to 6
Outputs:
- output: bfloat16 [4, 1024, 2048], P('dp', 'context')
- grad_tokens: bfloat16 [4, 1024, 2048], P('dp', 'context')
- grad_norm_attn: float32 [2048], replicated
- grad_w_query: float32 [2048, 3072], P(None, 'tensor')
- grad_w_kv_down: float32 [2048, 576], replicated
- grad_norm_latent: float32 [512], replicated
- grad_w_kv_up: float32 [512, 4096], P(None, 'tensor')
- grad_w_out: float32 [2048, 2048], P('tensor')
- grad_norm_ffn: float32 [2048], replicated
- grad_w_router: float32 [2048, 16], replicated
- grad_w_shared_gate: float32 [2048, 2816], P(None, 'tensor')
- grad_w_shared_up: float32 [2048, 2816], P(None, 'tensor')
- grad_w_shared_down: float32 [2816, 2048], P('tensor')
- grad_w_expert_gate: float32 [16, 2048, 1408], P(('dp', 'context'), None, 'tensor')
- grad_w_expert_up: float32 [16, 2048, 1408], P(('dp', 'context'), None, 'tensor')
- grad_w_expert_down: float32 [16, 1408, 2048], P(('dp', 'context'), 'tensor')
Inputs may be any that keep to these rules, and one draw needn't show every extreme that they name: `segments`: segment numbers start at 0 in every sequence and rise by 0 or 1 from one position to the next; in every sequence one document begins among the first 256 positions and ends among the last 256; the largest segment number, 510, is reached by some sequence in every draw. `expert_ids`: each token names 6 different experts. Within the rows of one device for one sequence (aligned blocks of 256 positions), no expert is named by more than 192 rows, and in some block an expert is named by exactly 192.
All inputs are finite; a program needn't handle non-finite values.
Results may differ from a plain program's by a relative error of at most 0.025.
Values may be sent and summed in bfloat16 or wider, within the bound.
A program may use at most 512 MiB of HBM per device.

v0:
```python
import jax
import jax.numpy as jnp
from jax import lax
from jax.sharding import PartitionSpec as P

D = 2048
NOPE = 128
ROPE = 64
VDIM = 128
LATENT = 512
TOP = 6
EXP_DEV = 2


EPS = 1e-06


def rms_scale(rows):
    return lax.rsqrt(jnp.mean(rows * rows, axis=-1, keepdims=True) + EPS)


def norm_back(grad_out, normed, inverse):
    return inverse * (grad_out - normed * jnp.mean(grad_out * normed, axis=-1, keepdims=True))


def angles(positions, rope_dim):
    frequency = 10000.0 ** (-(jnp.arange(rope_dim // 2).astype(jnp.float32) * 2.0) / rope_dim)
    turned = positions[:, None] * frequency[None, :]
    return (jnp.cos(turned), jnp.sin(turned))


def rotate(vectors, cosine, sine):
    half_dim = vectors.shape[-1] // 2
    front_part = vectors[..., :half_dim]
    back_part = vectors[..., half_dim:]
    return jnp.concatenate(
        [front_part * cosine - back_part * sine, front_part * sine + back_part * cosine], axis=-1
    )


def unrotate(vectors, cosine, sine):
    half_dim = vectors.shape[-1] // 2
    front_part = vectors[..., :half_dim]
    back_part = vectors[..., half_dim:]
    return jnp.concatenate(
        [front_part * cosine + back_part * sine, back_part * cosine - front_part * sine], axis=-1
    )


def silu_grad(pre):
    sigma_val = jax.nn.sigmoid(pre)
    return sigma_val * (1.0 + pre * (1.0 - sigma_val))


def per_device(
    tokens,
    segments,
    expert_ids,
    norm_attn,
    w_query,
    w_kv_down,
    norm_latent,
    w_kv_up,
    w_out,
    norm_ffn,
    w_router,
    w_shared_gate,
    w_shared_up,
    w_shared_down,
    w_expert_gate,
    w_expert_up,
    w_expert_down,
    cotangent,
):
    micro_count = tokens.shape[0]
    block_rows = tokens.shape[1]
    seq_len = segments.shape[1]
    groups = lax.axis_size("dp") * lax.axis_size("context")
    experts = EXP_DEV * groups
    capacity = 2 * block_rows * TOP // experts
    pair_count = block_rows * TOP
    heads_local = w_query.shape[1] // (NOPE + ROPE)
    fe_local = w_expert_gate.shape[2]
    scale_factor = (NOPE + ROPE) ** (-0.5)
    start_row = lax.axis_index("context") * block_rows
    query_index = start_row + jnp.arange(block_rows)
    key_index = jnp.arange(seq_len)
    cos_query, sin_query = angles(query_index.astype(jnp.float32), ROPE)
    gain_attn = norm_attn.astype(jnp.float32)
    gain_latent = norm_latent.astype(jnp.float32)
    gain_ffn = norm_ffn.astype(jnp.float32)
    router_wide = w_router.astype(jnp.float32)
    expert_range = jnp.arange(experts)
    zero_row = jnp.zeros((1, D), jnp.bfloat16)
    gate_all, up_all, down_all = (
        lax.all_gather(w_expert_gate, ("dp", "context"), axis=0, tiled=True),
        lax.all_gather(w_expert_up, ("dp", "context"), axis=0, tiled=True),
        lax.all_gather(w_expert_down, ("dp", "context"), axis=0, tiled=True),
    )
    gate_use = gate_all.reshape(groups, EXP_DEV, D, fe_local)
    up_use = up_all.reshape(groups, EXP_DEV, D, fe_local)
    down_use = down_all.reshape(groups, EXP_DEV, fe_local, D)
    weight_letters = "ji"
    acc_norm_attn = jnp.zeros(norm_attn.shape, jnp.float32)
    acc_query = jnp.zeros(w_query.shape, jnp.float32)
    acc_kv_down = jnp.zeros(w_kv_down.shape, jnp.float32)
    acc_norm_latent = jnp.zeros(norm_latent.shape, jnp.float32)
    acc_kv_up = jnp.zeros(w_kv_up.shape, jnp.float32)
    acc_out = jnp.zeros(w_out.shape, jnp.float32)
    acc_norm_ffn = jnp.zeros(norm_ffn.shape, jnp.float32)
    acc_router = jnp.zeros(w_router.shape, jnp.float32)
    acc_shared_gate = jnp.zeros(w_shared_gate.shape, jnp.float32)
    acc_shared_up = jnp.zeros(w_shared_up.shape, jnp.float32)
    acc_shared_down = jnp.zeros(w_shared_down.shape, jnp.float32)
    acc_expert_gate = jnp.zeros(gate_use.shape, jnp.float32)
    acc_expert_up = jnp.zeros(up_use.shape, jnp.float32)
    acc_expert_down = jnp.zeros(down_use.shape, jnp.float32)
    output_rows = []
    input_grads = []
    for micro_step in range(micro_count):
        x_rows = tokens[micro_step].astype(jnp.float32)
        inv_attn = rms_scale(x_rows)
        normed_attn = x_rows * inv_attn
        x_attn = (normed_attn * gain_attn).astype(jnp.bfloat16)
        query = jnp.dot(x_attn, w_query, preferred_element_type=jnp.float32).reshape(
            block_rows, heads_local, NOPE + ROPE
        )
        query_rot = jnp.concatenate(
            [
                query[..., :NOPE],
                rotate(query[..., NOPE:], cos_query[:, None, :], sin_query[:, None, :]),
            ],
            axis=-1,
        ).astype(jnp.bfloat16)
        kv_raw = jnp.dot(x_attn, w_kv_down, preferred_element_type=jnp.float32)
        latent_raw = kv_raw[:, :LATENT]
        inv_latent = rms_scale(latent_raw)
        normed_latent = latent_raw * inv_latent
        latent = (normed_latent * gain_latent).astype(jnp.bfloat16)
        key_rope = rotate(kv_raw[:, LATENT:], cos_query, sin_query).astype(jnp.bfloat16)
        latent_all, key_rope_all = (
            lax.all_gather(latent, "context", axis=0, tiled=True),
            lax.all_gather(key_rope, "context", axis=0, tiled=True),
        )
        expanded = jnp.dot(latent_all, w_kv_up, preferred_element_type=jnp.float32).astype(
            jnp.bfloat16
        )
        expanded = expanded.reshape(seq_len, heads_local, NOPE + VDIM)
        key_nope = expanded[..., :NOPE]
        head_values = expanded[..., NOPE:]
        seg_all = segments[micro_step]
        seg_query = lax.dynamic_slice_in_dim(seg_all, start_row, block_rows)
        allowed = (seg_query[:, None] == seg_all[None, :]) & (
            key_index[None, :] <= query_index[:, None]
        )
        raw = jnp.einsum(
            "chd,lhd->hcl", query_rot[..., :NOPE], key_nope, preferred_element_type=jnp.float32
        )
        raw = raw + jnp.einsum(
            "chd,ld->hcl", query_rot[..., NOPE:], key_rope_all, preferred_element_type=jnp.float32
        )
        scores = jnp.where(allowed[None], raw * scale_factor, -1e30)
        top_score = jnp.max(scores, axis=-1, keepdims=True)
        weights_exp = jnp.where(allowed[None], jnp.exp(scores - top_score), 0.0)
        row_total = jnp.sum(weights_exp, axis=-1, keepdims=True)
        log_total = top_score + jnp.log(row_total)
        probs_low = (weights_exp / row_total).astype(jnp.bfloat16)
        attended = jnp.einsum(
            "hcl,lhd->chd", probs_low, head_values, preferred_element_type=jnp.float32
        )
        attended = attended.astype(jnp.bfloat16).reshape(block_rows, heads_local * VDIM)
        attn_part = jnp.dot(attended, w_out, preferred_element_type=jnp.float32)
        attn_sum = lax.psum(attn_part.astype(jnp.bfloat16), "tensor").astype(jnp.float32)
        hidden_one = x_rows + attn_sum
        inv_ffn = rms_scale(hidden_one)
        normed_ffn = hidden_one * inv_ffn
        x_ffn = (normed_ffn * gain_ffn).astype(jnp.bfloat16)
        logits = jnp.dot(x_ffn, w_router, preferred_element_type=jnp.float32)
        router_probs = jax.nn.softmax(logits, axis=-1)
        ids_here = expert_ids[micro_step]
        gates = jnp.take_along_axis(router_probs, ids_here, axis=1)
        flat_ids = ids_here.reshape(pair_count)
        onehot_ids = (flat_ids[:, None] == expert_range[None, :]).astype(jnp.int32)
        earlier = jnp.cumsum(onehot_ids, axis=0) - onehot_ids
        rank_slot = jnp.sum(earlier * onehot_ids, axis=1)
        slot_index = (
            flat_ids % EXP_DEV * (groups * capacity) + flat_ids // EXP_DEV * capacity + rank_slot
        )
        source_pair = (
            jnp.full((experts * capacity,), pair_count, jnp.int32)
            .at[slot_index]
            .set(jnp.arange(pair_count, dtype=jnp.int32))
        )
        source_token = source_pair // TOP
        shared_gate = jnp.dot(x_ffn, w_shared_gate, preferred_element_type=jnp.float32)
        shared_up = jnp.dot(x_ffn, w_shared_up, preferred_element_type=jnp.float32)
        shared_hidden = (jax.nn.silu(shared_gate) * shared_up).astype(jnp.bfloat16)
        shared_out = jnp.dot(shared_hidden, w_shared_down, preferred_element_type=jnp.float32)
        x_padded = jnp.concatenate([x_ffn, zero_row], axis=0)
        send_rows = jnp.take(x_padded, source_token, axis=0).reshape(EXP_DEV, groups, capacity, D)
        form_in = "ijcd," + weight_letters + "df->ijcf"
        gate_pre = jnp.einsum(form_in, send_rows, gate_use, preferred_element_type=jnp.float32)
        up_pre = jnp.einsum(form_in, send_rows, up_use, preferred_element_type=jnp.float32)
        expert_hidden = (jax.nn.silu(gate_pre) * up_pre).astype(jnp.bfloat16)
        expert_result = jnp.einsum(
            "ijcf," + weight_letters + "fd->ijcd",
            expert_hidden,
            down_use,
            preferred_element_type=jnp.float32,
        )
        routed_rows = jnp.take(
            expert_result.reshape(experts * capacity, D), slot_index, axis=0
        ).reshape(block_rows, TOP, D)
        moe_part = jnp.sum(gates[:, :, None] * routed_rows, axis=1) + shared_out
        moe_sum = lax.psum(moe_part.astype(jnp.bfloat16), "tensor").astype(jnp.float32)
        hidden_two = hidden_one + moe_sum
        output_rows.append(hidden_two.astype(jnp.bfloat16))
        grad_two = cotangent[micro_step].astype(jnp.float32)
        grad_two_low = grad_two.astype(jnp.bfloat16)
        acc_shared_down = acc_shared_down + jnp.dot(
            shared_hidden.T, grad_two_low, preferred_element_type=jnp.float32
        )
        grad_shared_hidden = jnp.dot(
            grad_two_low, w_shared_down.T, preferred_element_type=jnp.float32
        )
        grad_shared_gate = (grad_shared_hidden * shared_up * silu_grad(shared_gate)).astype(
            jnp.bfloat16
        )
        grad_shared_up = (grad_shared_hidden * jax.nn.silu(shared_gate)).astype(jnp.bfloat16)
        acc_shared_gate = acc_shared_gate + jnp.dot(
            x_ffn.T, grad_shared_gate, preferred_element_type=jnp.float32
        )
        acc_shared_up = acc_shared_up + jnp.dot(
            x_ffn.T, grad_shared_up, preferred_element_type=jnp.float32
        )
        grad_x_shared = jnp.dot(
            grad_shared_gate, w_shared_gate.T, preferred_element_type=jnp.float32
        )
        grad_x_shared = grad_x_shared + jnp.dot(
            grad_shared_up, w_shared_up.T, preferred_element_type=jnp.float32
        )
        grad_pairs = (
            (gates[:, :, None] * grad_two[:, None, :]).astype(jnp.bfloat16).reshape(pair_count, D)
        )
        grad_padded = jnp.concatenate([grad_pairs, zero_row], axis=0)
        grad_send = jnp.take(grad_padded, source_pair, axis=0).reshape(EXP_DEV, groups, capacity, D)
        grad_hidden = jnp.einsum(
            "ijcd," + weight_letters + "fd->ijcf",
            grad_send,
            down_use,
            preferred_element_type=jnp.float32,
        )
        acc_expert_down = acc_expert_down + jnp.einsum(
            "ijcf,ijcd->" + weight_letters + "fd",
            expert_hidden,
            grad_send,
            preferred_element_type=jnp.float32,
        )
        grad_gate_pre = (grad_hidden * up_pre * silu_grad(gate_pre)).astype(jnp.bfloat16)
        grad_up_pre = (grad_hidden * jax.nn.silu(gate_pre)).astype(jnp.bfloat16)
        acc_expert_gate = acc_expert_gate + jnp.einsum(
            "ijcd,ijcf->" + weight_letters + "df",
            send_rows,
            grad_gate_pre,
            preferred_element_type=jnp.float32,
        )
        acc_expert_up = acc_expert_up + jnp.einsum(
            "ijcd,ijcf->" + weight_letters + "df",
            send_rows,
            grad_up_pre,
            preferred_element_type=jnp.float32,
        )
        form_back = "ijcf," + weight_letters + "df->ijcd"
        grad_rows = jnp.einsum(
            form_back, grad_gate_pre, gate_use, preferred_element_type=jnp.float32
        )
        grad_rows = grad_rows + jnp.einsum(
            form_back, grad_up_pre, up_use, preferred_element_type=jnp.float32
        )
        grad_routed = jnp.take(
            grad_rows.reshape(experts * capacity, D), slot_index, axis=0
        ).reshape(block_rows, TOP, D)
        grad_x_routed = jnp.sum(grad_routed, axis=1)
        grad_gate_sum = jnp.sum(grad_two[:, None, :] * routed_rows, axis=-1)
        onehot_float = onehot_ids.reshape(block_rows, TOP, experts).astype(jnp.float32)
        grad_combine = jnp.sum(onehot_float * grad_gate_sum[:, :, None], axis=1)
        grad_logits = router_probs * (
            grad_combine - jnp.sum(router_probs * grad_combine, axis=-1, keepdims=True)
        )
        grad_x_router = jnp.dot(grad_logits, router_wide.T, precision=lax.Precision.HIGHEST)
        router_part = jnp.dot(
            x_ffn.astype(jnp.float32).T, grad_logits, precision=lax.Precision.HIGHEST
        )
        grad_x_part = grad_x_shared + grad_x_routed + grad_x_router
        grad_x_ffn, router_grad = (
            lax.psum(grad_x_part.astype(jnp.bfloat16), "tensor").astype(jnp.float32),
            lax.psum(router_part.astype(jnp.bfloat16), "tensor").astype(jnp.float32),
        )
        acc_router = acc_router + router_grad
        acc_norm_ffn = acc_norm_ffn + jnp.sum(grad_x_ffn * normed_ffn, axis=0)
        grad_one = grad_two + norm_back(grad_x_ffn * gain_ffn, normed_ffn, inv_ffn)
        grad_attn_low = grad_one.astype(jnp.bfloat16)
        acc_out = acc_out + jnp.dot(attended.T, grad_attn_low, preferred_element_type=jnp.float32)
        grad_attended = jnp.dot(grad_attn_low, w_out.T, preferred_element_type=jnp.float32)
        grad_attended = grad_attended.astype(jnp.bfloat16).reshape(block_rows, heads_local, VDIM)
        probs = jnp.where(allowed[None], jnp.exp(scores - log_total), 0.0)
        probs_again = probs.astype(jnp.bfloat16)
        grad_probs = jnp.einsum(
            "chd,lhd->hcl", grad_attended, head_values, preferred_element_type=jnp.float32
        )
        grad_scores = (
            probs * (grad_probs - jnp.sum(probs * grad_probs, axis=-1, keepdims=True))
        ).astype(jnp.bfloat16)
        grad_values = jnp.einsum(
            "hcl,chd->lhd", probs_again, grad_attended, preferred_element_type=jnp.float32
        )
        grad_key_nope = scale_factor * jnp.einsum(
            "hcl,chd->lhd", grad_scores, query_rot[..., :NOPE], preferred_element_type=jnp.float32
        )
        grad_key_rope = scale_factor * jnp.einsum(
            "hcl,chd->ld", grad_scores, query_rot[..., NOPE:], preferred_element_type=jnp.float32
        )
        grad_query_nope = scale_factor * jnp.einsum(
            "hcl,lhd->chd", grad_scores, key_nope, preferred_element_type=jnp.float32
        )
        grad_query_rope = scale_factor * jnp.einsum(
            "hcl,ld->chd", grad_scores, key_rope_all, preferred_element_type=jnp.float32
        )
        grad_expanded_all = jnp.concatenate([grad_key_nope, grad_values], axis=-1).reshape(
            seq_len, heads_local * (NOPE + VDIM)
        )
        grad_expanded, grad_rope_part = (
            lax.psum_scatter(
                grad_expanded_all.astype(jnp.bfloat16), "context", scatter_dimension=0, tiled=True
            ).astype(jnp.float32),
            lax.psum_scatter(
                grad_key_rope.astype(jnp.bfloat16), "context", scatter_dimension=0, tiled=True
            ).astype(jnp.float32),
        )
        grad_expanded_low = grad_expanded.astype(jnp.bfloat16)
        acc_kv_up = acc_kv_up + jnp.dot(
            latent.T, grad_expanded_low, preferred_element_type=jnp.float32
        )
        grad_latent_part = jnp.dot(grad_expanded_low, w_kv_up.T, preferred_element_type=jnp.float32)
        grad_query_raw = jnp.concatenate(
            [
                grad_query_nope,
                unrotate(grad_query_rope, cos_query[:, None, :], sin_query[:, None, :]),
            ],
            axis=-1,
        )
        grad_query_raw = grad_query_raw.astype(jnp.bfloat16).reshape(
            block_rows, heads_local * (NOPE + ROPE)
        )
        acc_query = acc_query + jnp.dot(
            x_attn.T, grad_query_raw, preferred_element_type=jnp.float32
        )
        grad_x_query = jnp.dot(grad_query_raw, w_query.T, preferred_element_type=jnp.float32)
        grad_x_heads, grad_latent, grad_rope_key = (
            lax.psum(grad_x_query.astype(jnp.bfloat16), "tensor").astype(jnp.float32),
            lax.psum(grad_latent_part.astype(jnp.bfloat16), "tensor").astype(jnp.float32),
            lax.psum(grad_rope_part.astype(jnp.bfloat16), "tensor").astype(jnp.float32),
        )
        acc_norm_latent = acc_norm_latent + jnp.sum(grad_latent * normed_latent, axis=0)
        grad_latent_raw = norm_back(grad_latent * gain_latent, normed_latent, inv_latent)
        grad_kv_raw = jnp.concatenate(
            [grad_latent_raw, unrotate(grad_rope_key, cos_query, sin_query)], axis=-1
        ).astype(jnp.bfloat16)
        acc_kv_down = acc_kv_down + jnp.dot(
            x_attn.T, grad_kv_raw, preferred_element_type=jnp.float32
        )
        grad_x_attn = grad_x_heads + jnp.dot(
            grad_kv_raw, w_kv_down.T, preferred_element_type=jnp.float32
        )
        acc_norm_attn = acc_norm_attn + jnp.sum(grad_x_attn * normed_attn, axis=0)
        grad_input = grad_one + norm_back(grad_x_attn * gain_attn, normed_attn, inv_attn)
        input_grads.append(grad_input.astype(jnp.bfloat16))
    dense_sums = (
        lax.psum(acc_norm_attn.astype(jnp.bfloat16), ("dp", "context")).astype(jnp.float32),
        lax.psum(acc_query.astype(jnp.bfloat16), ("dp", "context")).astype(jnp.float32),
        lax.psum(acc_kv_down.astype(jnp.bfloat16), ("dp", "context")).astype(jnp.float32),
        lax.psum(acc_norm_latent.astype(jnp.bfloat16), ("dp", "context")).astype(jnp.float32),
        lax.psum(acc_kv_up.astype(jnp.bfloat16), ("dp", "context")).astype(jnp.float32),
        lax.psum(acc_out.astype(jnp.bfloat16), ("dp", "context")).astype(jnp.float32),
        lax.psum(acc_norm_ffn.astype(jnp.bfloat16), ("dp", "context")).astype(jnp.float32),
        lax.psum(acc_router.astype(jnp.bfloat16), ("dp", "context")).astype(jnp.float32),
        lax.psum(acc_shared_gate.astype(jnp.bfloat16), ("dp", "context")).astype(jnp.float32),
        lax.psum(acc_shared_up.astype(jnp.bfloat16), ("dp", "context")).astype(jnp.float32),
        lax.psum(acc_shared_down.astype(jnp.bfloat16), ("dp", "context")).astype(jnp.float32),
    )
    expert_sums = (
        lax.psum_scatter(
            acc_expert_gate.reshape(experts, D, fe_local).astype(jnp.bfloat16),
            ("dp", "context"),
            scatter_dimension=0,
            tiled=True,
        ).astype(jnp.float32),
        lax.psum_scatter(
            acc_expert_up.reshape(experts, D, fe_local).astype(jnp.bfloat16),
            ("dp", "context"),
            scatter_dimension=0,
            tiled=True,
        ).astype(jnp.float32),
        lax.psum_scatter(
            acc_expert_down.reshape(experts, fe_local, D).astype(jnp.bfloat16),
            ("dp", "context"),
            scatter_dimension=0,
            tiled=True,
        ).astype(jnp.float32),
    )
    return (
        jnp.stack(output_rows),
        jnp.stack(input_grads),
        dense_sums[0],
        dense_sums[1],
        dense_sums[2],
        dense_sums[3],
        dense_sums[4],
        dense_sums[5],
        dense_sums[6],
        dense_sums[7],
        dense_sums[8],
        dense_sums[9],
        dense_sums[10],
        expert_sums[0],
        expert_sums[1],
        expert_sums[2],
    )


def solution(mesh):
    return jax.shard_map(
        per_device,
        mesh=mesh,
        in_specs=(
            P("dp", "context", None),
            P("dp", None),
            P("dp", "context", None),
            P(),
            P(None, "tensor"),
            P(),
            P(),
            P(None, "tensor"),
            P("tensor", None),
            P(),
            P(),
            P(None, "tensor"),
            P(None, "tensor"),
            P("tensor", None),
            P(("dp", "context"), None, "tensor"),
            P(("dp", "context"), None, "tensor"),
            P(("dp", "context"), "tensor", None),
            P("dp", "context", None),
        ),
        out_specs=(
            P("dp", "context", None),
            P("dp", "context", None),
            P(),
            P(None, "tensor"),
            P(),
            P(),
            P(None, "tensor"),
            P("tensor", None),
            P(),
            P(),
            P(None, "tensor"),
            P(None, "tensor"),
            P("tensor", None),
            P(("dp", "context"), None, "tensor"),
            P(("dp", "context"), None, "tensor"),
            P(("dp", "context"), "tensor", None),
        ),
        check_vma=False,
    )
```

profile of v0, /device:TPU:0, one launch (start us, length us, event | category | flops | bytes accessed | tf_op | source)
XLA Modules:
  0.0 2107.2 jit_solution(15852512389078090490)
XLA Ops:
  93.8 15.8 mul.912
  115.6 12.1 mul.858
  127.7 16.4 mul.859
  171.1 25.4 %gather_fusion.4 = bf16[3072,2048]{1,0:T(8,128)(2,1)} fusion(bf16[257,2048]{1,0:T(8,128)(2,1)} %concatenate.57, s32[3072]{0:T(1024)S(1)} %get-tuple-element.124), kind=kCustom, calls=%fused_computation.5.clone | custom fusion | bytes 25178112 | tf_op jit(solution)/shard_map/jit(_take)/gather | solution.py:200
  196.5 25.2 %gather_fusion.1 = bf16[3072,2048]{1,0:T(8,128)(2,1)} fusion(bf16[257,2048]{1,0:T(8,128)(2,1)} %concatenate.54, s32[3072]{0:T(1024)S(1)} %get-tuple-element.120), kind=kCustom, calls=%fused_computation.1.clone | custom fusion | bytes 25178112 | tf_op jit(solution)/shard_map/jit(_take)/gather | solution.py:200
  258.1 17.1 fusion.20
  275.2 34.4 %all-gather.10.cloned.1.call-done = bf16[16,2048,352]{1,2,0:T(8,128)(2,1)} async-done(((bf16[2,2048,352]{1,2,0:T(8,128)(2,1)}), bf16[16,2048,352]{1,2,0:T(8,128)(2,1)}) %all-gather.10.cloned.1.call-update) | async-done | bytes 23068688 | tf_op jit(solution)/shard_map/all_gather | solution.py:97
  309.5 25.6 %multiply_convert_fusion.6 = (bf16[2,8,192,352]{3,2,1,0:T(8,128)(2,1)}, f32[2,8,192,352]{3,2,1,0:T(8,128)}) fusion(f32[2,8,192,352]{3,2,1,0:T(8,128)} %fusion.20, bf16[2,8,192,2048]{3,2,1,0:T(8,128)(2,1)} %bitcast.398, bf16[8,2,2048,352]{2,3,1,0:T(8,128)(2,1)} %bitcast.389), kind=kOutput, calls=%fused_computation.73 | convolution fusion | flops 4435673088 | bytes 46465024 | tf_op jit(solution)/shard_map/ijcd,jidf->ijcf/dot_general | solution.py:203
  335.1 92.6 %all-gather.12.cloned.1.call-done = bf16[16,352,2048]{2,1,0:T(8,128)(2,1)} async-done(((bf16[2,352,2048]{2,1,0:T(8,128)(2,1)}), bf16[16,352,2048]{2,1,0:T(8,128)(2,1)}) %all-gather.12.cloned.1.call-update) | async-done | bytes 23068688 | tf_op jit(solution)/shard_map/all_gather | solution.py:98
  427.8 16.5 fusion.4
  444.2 20.7 gather_fusion.5
  464.9 14.0 multiply_reduce_fusion.2
  479.8 13.1 gather_fusion.3
  508.0 27.4 %gather_fusion.8 = bf16[3072,2048]{1,0:T(8,128)(2,1)} fusion(bf16[1537,2048]{1,0:T(8,128)(2,1)} %concatenate.62, s32[3072]{0:T(1024)S(1)} %copy-done.150), kind=kCustom, calls=%fused_computation.9.clone | custom fusion | bytes 25178112 | tf_op jit(solution)/shard_map/jit(_take)/gather | solution.py:246
  546.5 24.2 %multiply_convert_fusion.3 = (bf16[2,8,192,352]{3,2,1,0:T(8,128)(2,1)}, bf16[2,8,192,352]{3,2,1,0:T(8,128)(2,1)}) fusion(f32[2,8,192,352]{3,2,1,0:T(8,128)} %fusion.20, f32[2,8,192,352]{3,2,1,0:T(8,128)} %get-tuple-element.145, bf16[2,8,192,2048]{3,2,1,0:T(8,128)(2,1)} %bitcast.412, bf16[8,2,352,2048]{3,2,1,0:T(8,128)(2,1)} %bitcast.394), kind=kOutput, calls=%fused_computation.70 | convolution fusion | flops 4443242496 | bytes 48627712 | tf_op jit(solution)/shard_map/ijcd,jifd->ijcf/dot_general | solution.py:247
  570.7 16.5 fusion.8
  587.1 26.4 %fusion.36 = f32[2,8,192,2048]{3,2,1,0:T(8,128)} fusion(f32[2,8,192,2048]{3,2,1,0:T(8,128)} %fusion.8, bf16[2,8,192,352]{3,2,1,0:T(8,128)(2,1)} %get-tuple-element.79, bf16[8,2,2048,352]{2,3,1,0:T(8,128)(2,1)} %bitcast.409), kind=kOutput, calls=%fused_computation.59 | convolution fusion | flops 4435476480 | bytes 75563008 | tf_op jit(solution)/shard_map/ijcf,jidf->ijcd/dot_general | solution.py:274
  613.5 20.9 gather_fusion.9
  644.4 15.0 reshape.814
  659.4 16.5 fusion.22
  675.9 23.9 %multiply_convert_fusion.7 = (bf16[2,8,192,352]{3,2,1,0:T(8,128)(2,1)}, f32[2,8,192,352]{3,2,1,0:T(8,128)}) fusion(f32[2,8,192,352]{3,2,1,0:T(8,128)} %fusion.22, bf16[2,8,192,2048]{3,2,1,0:T(8,128)(2,1)} %bitcast.402, bf16[8,2,2048,352]{2,3,1,0:T(8,128)(2,1)} %bitcast.391), kind=kOutput, calls=%fused_computation.76 | convolution fusion | flops 4435673088 | bytes 46465024 | tf_op jit(solution)/shard_map/ijcd,jidf->ijcf/dot_general | solution.py:203
  699.7 16.5 fusion.6
  716.2 20.9 gather_fusion.2
  737.2 14.1 multiply_reduce_fusion.3
  752.1 12.7 gather_fusion
  779.9 27.4 %gather_fusion.6 = bf16[3072,2048]{1,0:T(8,128)(2,1)} fusion(bf16[1537,2048]{1,0:T(8,128)(2,1)} %concatenate.58, s32[3072]{0:T(1024)S(1)} %copy-done.149), kind=kCustom, calls=%fused_computation.3.clone | custom fusion | bytes 25178112 | tf_op jit(solution)/shard_map/jit(_take)/gather | solution.py:246
  818.4 24.2 %multiply_convert_fusion.5 = (bf16[2,8,192,352]{3,2,1,0:T(8,128)(2,1)}, bf16[2,8,192,352]{3,2,1,0:T(8,128)(2,1)}) fusion(f32[2,8,192,352]{3,2,1,0:T(8,128)} %fusion.22, f32[2,8,192,352]{3,2,1,0:T(8,128)} %get-tuple-element.149, bf16[2,8,192,2048]{3,2,1,0:T(8,128)(2,1)} %bitcast.414, bf16[8,2,352,2048]{3,2,1,0:T(8,128)(2,1)} %bitcast.396), kind=kOutput, calls=%fused_computation.72 | convolution fusion | flops 4443242496 | bytes 48627712 | tf_op jit(solution)/shard_map/ijcd,jifd->ijcf/dot_general | solution.py:247
  842.6 16.9 fusion.10
  859.5 26.4 %fusion.33 = f32[2,8,192,2048]{3,2,1,0:T(8,128)} fusion(f32[2,8,192,2048]{3,2,1,0:T(8,128)} %fusion.10, bf16[2,8,192,352]{3,2,1,0:T(8,128)(2,1)} %get-tuple-element.77, bf16[8,2,2048,352]{2,3,1,0:T(8,128)(2,1)} %bitcast.411), kind=kOutput, calls=%fused_computation.58 | convolution fusion | flops 4435476480 | bytes 75563008 | tf_op jit(solution)/shard_map/ijcf,jidf->ijcd/dot_general | solution.py:274
  885.9 20.7 gather_fusion.7
  916.5 15.0 reshape.810
  961.2 87.1 %all-reduce.22.cloned.1.call-done = (bf16[256,2048]{1,0:T(8,128)(2,1)}, bf16[256,2048]{1,0:T(8,128)(2,1)}) async-done(((bf16[256,2048]{1,0:T(8,128)(2,1)}, bf16[256,2048]{1,0:T(8,128)(2,1)}), (bf16[256,2048]{1,0:T(8,128)(2,1)}, bf16[256,2048]{1,0:T(8,128)(2,1)})) %all-reduce.22.cloned.1.call-update) | async-done | bytes 2097168 | tf_op jit(solution)/shard_map/psum | solution.py:296
  1091.1 15.1 reshape.807
  1123.6 15.3 reshape.801
  1168.1 20.6 reduce-scatter.8.cloned.1.call-done
  1212.6 12.7 all-reduce.18.cloned.1.call-done
  1230.1 177.7 %all-reduce.20.cloned.1.call-done = (bf16[256,2048]{1,0:T(8,128)(2,1)}, bf16[256,2048]{1,0:T(8,128)(2,1)}, bf16[256,2048]{1,0:T(8,128)(2,1)}, bf16[256,512]{0,1:...) async-done(((bf16[256,2048]{1,0:T(8,128)(2,1)}, bf16[256,2048]{1,0:T(8,128)(2,1)}, ...) | async-done | bytes 4849680 | tf_op jit(solution)/shard_map/psum | solution.py:215
  1417.6 21.9 %fusion.31 = f32[8,2,2048,352]{2,3,1,0:T(8,128)} fusion(bf16[2,8,192,2048]{3,2,1,0:T(8,128)(2,1)} %bitcast.403, bf16[2,8,192,352]{3,2,1,0:T(8,128)(2,1)} %get-tuple-element.77), kind=kOutput, calls=%fused_computation.56 | convolution fusion | flops 4429185024 | bytes 60882944 | tf_op jit(solution)/shard_map/ijcd,ijcf->jidf/dot_general | solution.py:261
  1439.5 30.5 %add_convert_fusion.2 = bf16[8,2,2048,352]{2,3,1,0:T(8,128)(2,1)} fusion(f32[8,2,2048,352]{2,3,1,0:T(8,128)} %fusion.31, bf16[2,8,192,2048]{3,2,1,0:T(8,128)(2,1)} %bitcast.399, bf16[2,8,192,352]{3,2,1,0:T(8,128)(2,1)} %get-tuple-element.79), kind=kOutput, calls=%fused_computation.14 | convolution fusion | flops 4452253696 | bytes 83951616 | tf_op jit(solution)/shard_map/ijcd,ijcf->jidf/dot_general | solution.py:261
  1470.1 22.2 %fusion.29 = f32[8,2,2048,352]{2,3,1,0:T(8,128)} fusion(bf16[2,8,192,2048]{3,2,1,0:T(8,128)(2,1)} %bitcast.404, bf16[2,8,192,352]{3,2,1,0:T(8,128)(2,1)} %get-tuple-element.78), kind=kOutput, calls=%fused_computation.54 | convolution fusion | flops 4429185024 | bytes 60882944 | tf_op jit(solution)/shard_map/ijcd,ijcf->jidf/dot_general | solution.py:267
  1492.3 29.8 %add_convert_fusion.1 = bf16[8,2,2048,352]{2,3,1,0:T(8,128)(2,1)} fusion(f32[8,2,2048,352]{2,3,1,0:T(8,128)} %fusion.29, bf16[2,8,192,2048]{3,2,1,0:T(8,128)(2,1)} %bitcast.400, bf16[2,8,192,352]{3,2,1,0:T(8,128)(2,1)} %get-tuple-element.80), kind=kOutput, calls=%fused_computation.13 | convolution fusion | flops 4452253696 | bytes 83951616 | tf_op jit(solution)/shard_map/ijcd,ijcf->jidf/dot_general | solution.py:267
  1522.5 22.8 %fusion.25 = f32[8,2,352,2048]{3,2,1,0:T(8,128)} fusion(bf16[2,8,192,2048]{3,2,1,0:T(8,128)(2,1)} %bitcast.415, bf16[2,8,192,352]{3,2,1,0:T(8,128)(2,1)} %get-tuple-element.148), kind=kOutput, calls=%fused_computation.42 | convolution fusion | flops 4429185024 | bytes 60882944 | tf_op jit(solution)/shard_map/ijcf,ijcd->jifd/dot_general | solution.py:253
  1545.3 30.1 %add_convert_fusion = bf16[8,2,352,2048]{3,2,1,0:T(8,128)(2,1)} fusion(f32[8,2,352,2048]{3,2,1,0:T(8,128)} %fusion.25, bf16[2,8,192,2048]{3,2,1,0:T(8,128)(2,1)} %bitcast.413, bf16[2,8,192,352]{3,2,1,0:T(8,128)(2,1)} %get-tuple-element.144), kind=kOutput, calls=%fused_computation.12 | convolution fusion | flops 4452253696 | bytes 83951616 | tf_op jit(solution)/shard_map/ijcf,ijcd->jifd/dot_general | solution.py:253
  1583.1 15.7 all-reduce.4
  1610.3 34.7 %all-reduce.16.cloned.1.call-done = (bf16[2048,768]{1,0:T(8,128)(2,1)}, bf16[2048,576]{0,1:T(8,128)(2,1)}, bf16[512,1024]{1,0:T(8,128)(2,1)}, bf16[512,2048]{1,0...) async-done(((bf16[2048,768]{1,0:T(8,128)(2,1)}, bf16[2048,576]{0,1:T(8,128)(2,1)}, ...) | async-done | bytes 17367056 | tf_op jit(solution)/shard_map/psum | solution.py:380
  1671.9 122.9 %reduce-scatter.16.cloned.1.call-done = bf16[2,2048,352]{1,2,0:T(8,128)(2,1)} async-done(((bf16[16,2048,352]{1,2,0:T(8,128)(2,1)}), bf16[2,2048,352]{1,2,0:T(8,128)(2,1)}) %reduce-scatter.16.cloned.1.call-update) | async-done | bytes 2883600 | tf_op jit(solution)/shard_map/reduce_scatter | solution.py:392
  1799.9 144.7 %reduce-scatter.18.cloned.1.call-done = bf16[2,2048,352]{1,2,0:T(8,128)(2,1)} async-done(((bf16[16,2048,352]{1,2,0:T(8,128)(2,1)}), bf16[2,2048,352]{1,2,0:T(8,128)(2,1)}) %reduce-scatter.18.cloned.1.call-update) | async-done | bytes 2883600 | tf_op jit(solution)/shard_map/reduce_scatter | solution.py:398
  1949.7 144.5 %reduce-scatter.20.cloned.1.call-done = bf16[2,352,2048]{2,1,0:T(8,128)(2,1)} async-done(((bf16[16,352,2048]{2,1,0:T(8,128)(2,1)}), bf16[2,352,2048]{2,1,0:T(8,128)(2,1)}) %reduce-scatter.20.cloned.1.call-update) | async-done | bytes 2883600 | tf_op jit(solution)/shard_map/reduce_scatter | solution.py:404
  (668 shorter events, 446.3 us)
Async XLA Ops:
  8.0 225.5 %copy-start = (bf16[704,2048]{1,0:T(8,128)(2,1)S(1)}, bf16[704,2048]{1,0:T(8,128)(2,1)}, u32[]{:S(2)}) copy-start(bf16[704,2048]{1,0:T(8,128)(2,1)} %param.39) | copy-start | bytes 8650756
  8.0 40.5 %all-gather.14.cloned.1.call-start = ((), (), s32[]{:S(2)}) async-start(), calls=%async_computation.11 | async-start | bytes 1310720 | tf_op jit(solution)/shard_map/all_gather | solution.py:142
  8.9 17.9 copy-start.120
  11.6 15.2 copy-start.159
  17.0 41.6 %all-gather.6.cloned.1.call-start = ((), (), s32[]{:S(2)}) async-start(), calls=%async_computation.7 | async-start | bytes 1310720 | tf_op jit(solution)/shard_map/all_gather | solution.py:142
  17.8 145.5 %all-reduce.24.cloned.1.call-start = ((), (), s32[]{:S(2)}) async-start(), calls=%async_computation.23 | async-start | bytes 4194304 | tf_op jit(solution)/shard_map/psum | solution.py:173
  48.5 16.8 copy-start.47
  70.9 187.1 %all-gather.8.cloned.1.call-start = ((), (), s32[]{:S(2)}) async-start(), calls=%async_computation.8 | async-start | bytes 25952256 | tf_op jit(solution)/shard_map/all_gather | solution.py:96
  71.5 238.0 %all-gather.10.cloned.1.call-start = ((), (), s32[]{:S(2)}) async-start(), calls=%async_computation.9 | async-start | bytes 25952256 | tf_op jit(solution)/shard_map/all_gather | solution.py:97
  72.1 355.6 %all-gather.12.cloned.1.call-start = ((), (), s32[]{:S(2)}) async-start(), calls=%async_computation.10 | async-start | bytes 25952256 | tf_op jit(solution)/shard_map/all_gather | solution.py:98
  72.7 975.7 %all-reduce.22.cloned.1.call-start = ((), (), s32[]{:S(2)}) async-start(), calls=%async_computation.22 | async-start | bytes 4194304 | tf_op jit(solution)/shard_map/psum | solution.py:296
  72.8 88.7 %copy-start.128 = (s32[1,256,6]{1,0,2:T(1,128)}, s32[1,256,6]{1,0,2:T(1,128)S(1)}, u32[]{:S(2)}) copy-start(s32[1,256,6]{1,0,2:T(1,128)S(1)} %get-tuple-element.125) | copy-start | bytes 18436
  72.8 88.7 %copy-start.130 = (s32[1,256,6]{1,0,2:T(1,128)}, s32[1,256,6]{1,0,2:T(1,128)S(1)}, u32[]{:S(2)}) copy-start(s32[1,256,6]{1,0,2:T(1,128)S(1)} %get-tuple-element.126) | copy-start | bytes 18436
  74.0 92.5 %copy-start.134 = (f32[2048]{0:T(1024)}, f32[2048]{0:T(1024)S(1)}, u32[]{:S(2)}) copy-start(f32[2048]{0:T(1024)S(1)} %convert_element_type.466) | copy-start | bytes 24580
  196.5 25.2 %copy-start.105 = (bf16[2048,16]{0,1:T(8,128)(2,1)S(1)}, bf16[2048,16]{0,1:T(8,128)(2,1)}, u32[]{:S(2)}) copy-start(bf16[2048,16]{0,1:T(8,128)(2,1)} %param.36) | copy-start | bytes 196612
  427.8 16.5 copy-start.138
  444.2 20.7 copy-start.166
  508.0 27.4 %copy-start.182 = (pred[3072]{0:T(1024)(128)(4,1)S(1)}, pred[3072]{0:T(1024)(128)(4,1)}, u32[]{:S(2)}) copy-start(pred[3072]{0:T(1024)(128)(4,1)} %get-tuple-element.121) | copy-start | bytes 9220
  587.1 26.4 %copy-start.139 = (s32[2048]{0:T(1024)S(1)}, s32[2048]{0:T(1024)}, u32[]{:S(2)}) copy-start(s32[2048]{0:T(1024)} %pad_clamp_fusion) | copy-start | bytes 24580
  613.5 20.9 copy-start.167
  699.7 16.5 copy-start.136
  716.2 20.9 copy-start.164
  737.1 15.0 copy-start.12
  779.9 27.4 %copy-start.181 = (pred[3072]{0:T(1024)(128)(4,1)S(1)}, pred[3072]{0:T(1024)(128)(4,1)}, u32[]{:S(2)}) copy-start(pred[3072]{0:T(1024)(128)(4,1)} %get-tuple-element.117) | copy-start | bytes 9220
  859.5 26.4 %copy-start.137 = (s32[2048]{0:T(1024)S(1)}, s32[2048]{0:T(1024)}, u32[]{:S(2)}) copy-start(s32[2048]{0:T(1024)} %pad_clamp_fusion.1) | copy-start | bytes 24580
  885.9 20.7 copy-start.165
  959.0 89.4 %copy-start.135 = (f32[2048]{0:T(1024)S(1)}, f32[2048]{0:T(1024)}, u32[]{:S(2)}) copy-start(f32[2048]{0:T(1024)} %copy-done.134) | copy-start | bytes 24580
  959.0 89.4 %copy-start.178 = (f32[256]{0:T(256)S(1)}, f32[256]{0:T(256)}, u32[]{:S(2)}) copy-start(f32[256]{0:T(256)} %copy-done.177) | copy-start | bytes 3076
  959.0 89.4 %copy-start.180 = (f32[256]{0:T(256)S(1)}, f32[256]{0:T(256)}, u32[]{:S(2)}) copy-start(f32[256]{0:T(256)} %copy-done.179) | copy-start | bytes 3076
  961.1 204.4 %reduce-scatter.14.cloned.1.call-start = ((), (), s32[]{:S(2)}) async-start(), calls=%async_computation.15 | async-start | bytes 163840 | tf_op jit(solution)/shard_map/reduce_scatter | solution.py:336
  1078.7 86.8 %reduce-scatter.10.cloned.1.call-start = ((), (), s32[]{:S(2)}) async-start(), calls=%async_computation.13 | async-start | bytes 163840 | tf_op jit(solution)/shard_map/reduce_scatter | solution.py:336
  1087.1 78.5 %reduce-scatter.12.cloned.1.call-start = ((), (), s32[]{:S(2)}) async-start(), calls=%async_computation.14 | async-start | bytes 2621440 | tf_op jit(solution)/shard_map/reduce_scatter | solution.py:333
  1091.0 97.8 %reduce-scatter.8.cloned.1.call-start = ((), (), s32[]{:S(2)}) async-start(), calls=%async_computation.12 | async-start | bytes 2621440 | tf_op jit(solution)/shard_map/reduce_scatter | solution.py:333
  1091.0 15.1 copy-start.99
  1120.8 104.5 %all-reduce.18.cloned.1.call-start = ((), (), s32[]{:S(2)}) async-start(), calls=%async_computation.20 | async-start | bytes 131072 | tf_op jit(solution)/shard_map/psum | solution.py:362
  1123.6 17.9 copy-start.90
  1165.5 242.3 %all-reduce.20.cloned.1.call-start = ((), (), s32[]{:S(2)}) async-start(), calls=%async_computation.21 | async-start | bytes 9699328 | tf_op jit(solution)/shard_map/psum | solution.py:215
  1191.3 453.6 %all-reduce.16.cloned.1.call-start = ((), (), s32[]{:S(2)}) async-start(), calls=%async_computation.19 | async-start | bytes 34734080 | tf_op jit(solution)/shard_map/psum | solution.py:380
  1209.7 17.2 copy-start.185
  1209.7 17.2 copy-start.195
  1209.7 17.4 copy-start.69
  1227.1 186.9 %copy-start.140 = (bf16[256,32]{0,1:T(8,128)(2,1)}, bf16[256,32]{0,1:T(8,128)(2,1)S(1)}, u32[]{:S(2)}) copy-start(bf16[256,32]{0,1:T(8,128)(2,1)S(1)} %get-tuple-element.109) | copy-start | bytes 49156
  1227.1 186.9 %copy-start.142 = (bf16[256,32]{0,1:T(8,128)(2,1)}, bf16[256,32]{0,1:T(8,128)(2,1)S(1)}, u32[]{:S(2)}) copy-start(bf16[256,32]{0,1:T(8,128)(2,1)S(1)} %get-tuple-element.110) | copy-start | bytes 49156
  1227.1 180.7 %copy-start.148 = (f32[512]{0:T(512)S(1)}, f32[512]{0:T(512)}, u32[]{:S(2)}) copy-start(f32[512]{0:T(512)} %copy-done.147) | copy-start | bytes 6148
  1228.7 181.3 %copy-start.55 = (f32[256,576]{0,1:T(8,128)S(1)}, f32[256,576]{0,1:T(8,128)}, u32[]{:S(2)}) copy-start(f32[256,576]{0,1:T(8,128)} %copy-done.54) | copy-start | bytes 1769476
  1417.6 377.2 %reduce-scatter.16.cloned.1.call-start = ((), (), s32[]{:S(2)}) async-start(), calls=%async_computation.16 | async-start | bytes 25952256 | tf_op jit(solution)/shard_map/reduce_scatter | solution.py:392
  1470.0 474.6 %reduce-scatter.18.cloned.1.call-start = ((), (), s32[]{:S(2)}) async-start(), calls=%async_computation.17 | async-start | bytes 25952256 | tf_op jit(solution)/shard_map/reduce_scatter | solution.py:398
  1522.2 572.1 %reduce-scatter.20.cloned.1.call-start = ((), (), s32[]{:S(2)}) async-start(), calls=%async_computation.18 | async-start | bytes 25952256 | tf_op jit(solution)/shard_map/reduce_scatter | solution.py:404
  (172 other events, 711.4 us)
Sparse Core Ops, SparseCore 0:
  17.2 19.5 all-gather.13
  38.3 16.8 all-gather.5
  71.0 88.7 all-reduce.23
  961.2 87.0 all-reduce.21
  1078.8 18.5 reduce-scatter.13
  1099.8 19.5 reduce-scatter.9
  1122.6 31.4 reduce-scatter.11
  1157.3 31.4 reduce-scatter.7
  1191.1 34.0 all-reduce.17
  1229.5 178.3 all-reduce.19
Sparse Core Ops, SparseCore 1:
  73.5 117.8 all-gather.7
  193.2 116.3 all-gather.9
  311.4 116.3 all-gather.11
  1417.6 227.3 all-reduce.15
  1649.0 145.7 reduce-scatter.15
  1798.9 145.7 reduce-scatter.17
  1948.5 145.7 reduce-scatter.19
where the time goes:
time: 2120 us; the launch traced here: 2110 us
  waiting for transfers between devices  874 us (41%)
  matrix products  537 us (25%)
  local copies, waits for them, and re-layouts  390 us (18%)
  other arithmetic  257 us (12%)
  blocking collectives  28.6 us (1%)
    psum x1, waiting for transfers between devices, per_device(): lax.psum(moe_part.astype(jnp.bfloat16), 'tensor').astype(jnp.float32)  178 us
    reduce_scatter x1, waiting for transfers between devices, per_device(): lax.psum_scatter(acc_expert_up.reshape(experts, D, fe_local).astype(jnp.b...  145 us
    reduce_scatter x1, waiting for transfers between devices, per_device(): lax.psum_scatter(acc_expert_down.reshape(experts, fe_local, D).astype(jnp...  145 us
    reduce_scatter x1, waiting for transfers between devices, per_device(): lax.psum_scatter(acc_expert_gate.reshape(experts, D, fe_local).astype(jnp...  123 us
    all_gather x1, waiting for transfers between devices, per_device(): lax.all_gather(w_expert_down, ('dp', 'context'), axis=0, tiled=True)  92.6 us
    psum x1, waiting for transfers between devices, per_device(): lax.psum(grad_x_part.astype(jnp.bfloat16), 'tensor').astype(jnp.float32)  87.1 us
    gather x2, local copies, waits for them, and re-layouts, per_device(): jnp.take(grad_padded, source_pair, axis=0)  54.9 us
    mul x4, local copies, waits for them, and re-layouts, per_device(): gates[:, :, None] * grad_two[:, None, :]  54.4 us
  transfers between devices with their start and end apart: 17, of which 10 were waited for; matrix products, arithmetic and copies ran while one was open for 27% of the time, Pallas kernels for 0%

commit v1 on v0

v1 whole, which is shorter than its diff:
```python
import functools

import jax
import jax.numpy as jnp
from jax import lax
from jax.experimental import pallas as pl
from jax.experimental.pallas import tpu as pltpu
from jax.sharding import PartitionSpec as P

D = 2048
NOPE = 128
ROPE = 64
VDIM = 128
LATENT = 512
TOP = 6
EXP_DEV = 2
LANES = 128
GROUP = ("dp", "context")
EVERY = ("dp", "context", "tensor")
BF16 = jnp.bfloat16
F32 = jnp.float32
MESH = pl.DeviceIdType.MESH
MIB = 1024 * 1024

EPS = 1e-06


def rms_scale(rows):
    return lax.rsqrt(jnp.mean(rows * rows, axis=-1, keepdims=True) + EPS)


def norm_back(grad_out, normed, inverse):
    return inverse * (grad_out - normed * jnp.mean(grad_out * normed, axis=-1, keepdims=True))


def angles(positions, rope_dim):
    frequency = 10000.0 ** (-(jnp.arange(rope_dim // 2).astype(jnp.float32) * 2.0) / rope_dim)
    turned = positions[:, None] * frequency[None, :]
    return (jnp.cos(turned), jnp.sin(turned))


def rotate(vectors, cosine, sine):
    half_dim = vectors.shape[-1] // 2
    front_part = vectors[..., :half_dim]
    back_part = vectors[..., half_dim:]
    return jnp.concatenate(
        [front_part * cosine - back_part * sine, front_part * sine + back_part * cosine], axis=-1
    )


def unrotate(vectors, cosine, sine):
    half_dim = vectors.shape[-1] // 2
    front_part = vectors[..., :half_dim]
    back_part = vectors[..., half_dim:]
    return jnp.concatenate(
        [front_part * cosine + back_part * sine, back_part * cosine - front_part * sine], axis=-1
    )


def mm(left, right):
    return jnp.dot(left, right, preferred_element_type=F32)


def mm_nt(left, right):
    return lax.dot_general(left, right, (((1,), (1,)), ((), ())), preferred_element_type=F32)


def mm_tn(left, right):
    return lax.dot_general(left, right, (((0,), (0,)), ((), ())), preferred_element_type=F32)


def ring(axes, sizes):
    place = 0
    total = 1
    for axis, size in zip(axes, sizes):
        place = place * size + lax.axis_index(axis)
        total *= size

    def coordinates(index):
        found = {}
        for axis, size in reversed(list(zip(axes, sizes))):
            found[axis] = lax.rem(index, size)
            index = lax.div(index, size)
        return found

    return place, total, coordinates


def meet(devices):
    barrier = pltpu.get_barrier_semaphore()
    for device in devices:
        pl.semaphore_signal(barrier, inc=1, device_id=device, device_id_type=MESH)
    pl.semaphore_wait(barrier, len(devices))


def link_cost(values, times=1):
    sent = sum(v.size * v.dtype.itemsize for v in values) * times
    return pl.CostEstimate(flops=0, bytes_accessed=20 * sent, transcendentals=0)


def gather_kernel(axes, sizes, columns, v_ref, out_ref, send_sem, recv_sem, own_sem):
    place, total, coordinates = ring(axes, sizes)

    def part(index):
        if columns:
            width = v_ref.shape[1]
            return out_ref.at[:, pl.ds(pl.multiple_of(index * width, LANES), width)]
        return out_ref.at[:, index]

    peers = [lax.rem(place + step, total) for step in range(1, total)]
    meet([coordinates(peer) for peer in peers])
    copies = []
    for step in range(1, total):
        copy = pltpu.make_async_remote_copy(
            src_ref=v_ref,
            dst_ref=part(place),
            send_sem=send_sem.at[step - 1],
            recv_sem=recv_sem.at[step - 1],
            device_id=coordinates(peers[step - 1]),
            device_id_type=MESH,
        )
        copy.start()
        copies.append(copy)
    own = pltpu.make_async_copy(v_ref, part(place), own_sem)
    own.start()
    own.wait()
    for copy in copies:
        copy.wait_send()
    for step in range(1, total):
        source = lax.rem(place - step + total, total)
        pltpu.make_async_remote_copy(
            src_ref=v_ref,
            dst_ref=part(source),
            send_sem=send_sem.at[step - 1],
            recv_sem=recv_sem.at[step - 1],
            device_id=coordinates(peers[step - 1]),
            device_id_type=MESH,
        ).wait_recv()


def push_gather(v, axes, collective_id, columns=False):
    sizes = tuple(lax.axis_size(axis) for axis in axes)
    total = 1
    for size in sizes:
        total *= size
    if columns:
        shape = (v.shape[0], total * v.shape[1])
    else:
        shape = (v.shape[0], total) + v.shape[1:]
    return pl.pallas_call(
        functools.partial(gather_kernel, axes, sizes, columns),
        out_shape=jax.ShapeDtypeStruct(shape, v.dtype),
        in_specs=[pl.BlockSpec(memory_space=pl.ANY)],
        out_specs=pl.BlockSpec(memory_space=pl.ANY),
        scratch_shapes=[
            pltpu.SemaphoreType.DMA((total - 1,)),
            pltpu.SemaphoreType.DMA((total - 1,)),
            pltpu.SemaphoreType.DMA,
        ],
        compiler_params=pltpu.CompilerParams(collective_id=collective_id, has_side_effects=True),
        cost_estimate=link_cost([v], 4 * total),
        name="push_gather",
    )(v)


def scatter_kernel(axes, sizes, v_ref, out_ref, held, send_sem, recv_sem, own_sem):
    place, total, coordinates = ring(axes, sizes)
    peers = [lax.rem(place + step, total) for step in range(1, total)]
    meet([coordinates(peer) for peer in peers])
    copies = []
    for step in range(1, total):
        copy = pltpu.make_async_remote_copy(
            src_ref=v_ref.at[:, peers[step - 1]],
            dst_ref=held.at[step],
            send_sem=send_sem.at[step - 1],
            recv_sem=recv_sem.at[step - 1],
            device_id=coordinates(peers[step - 1]),
            device_id_type=MESH,
        )
        copy.start()
        copies.append(copy)
    own = pltpu.make_async_copy(v_ref.at[:, place], held.at[0], own_sem)
    own.start()
    own.wait()
    for copy in copies:
        copy.wait()
    for lead in range(out_ref.shape[0]):
        rows = out_ref.shape[1]
        chunk = min(rows, 16)

        def add(index, carry):
            at = pl.ds(pl.multiple_of(index * chunk, chunk), chunk)
            value = held[0, lead, at, :].astype(F32)
            for step in range(1, total):
                value = value + held[step, lead, at, :].astype(F32)
            out_ref[lead, at, :] = value
            return carry

        lax.fori_loop(0, rows // chunk, add, 0)


def push_scatter(v, axes, collective_id):
    sizes = tuple(lax.axis_size(axis) for axis in axes)
    lead, total, rows, width = v.shape
    return pl.pallas_call(
        functools.partial(scatter_kernel, axes, sizes),
        out_shape=jax.ShapeDtypeStruct((lead, rows, width), F32),
        in_specs=[pl.BlockSpec(memory_space=pl.ANY)],
        out_specs=pl.BlockSpec(memory_space=pltpu.VMEM),
        scratch_shapes=[
            pltpu.VMEM((total, lead, rows, width), v.dtype),
            pltpu.SemaphoreType.DMA((total - 1,)),
            pltpu.SemaphoreType.DMA((total - 1,)),
            pltpu.SemaphoreType.DMA,
        ],
        compiler_params=pltpu.CompilerParams(
            collective_id=collective_id, has_side_effects=True, vmem_limit_bytes=40 * MIB
        ),
        cost_estimate=link_cost([v], 4),
        name="push_scatter",
    )(v)


def flip(index, mask, bits):
    total = 0
    for bit in range(bits):
        weight = 1 << bit
        ours = lax.rem(lax.div(index, weight), 2)
        theirs = lax.rem(lax.div(mask, weight), 2)
        total = total + lax.rem(ours + theirs, 2) * weight
    return total


def group_layout(axes, sizes):
    place, _, coordinates = ring(axes, sizes)
    return lax.div(place, 2), lax.rem(place, 2), lambda chip, core: coordinates(chip * 2 + core)


def group_sizes(axes):
    sizes = tuple(lax.axis_size(axis) for axis in axes)
    pairs = 1
    for size in sizes:
        pairs *= size
    return sizes, pairs // 2


def group_scatter_kernel(count, pairs, axes, sizes, *refs):
    inputs, outputs, refs = refs[:count], refs[count : 2 * count], refs[2 * count :]
    mine, peer, summed, held = (refs[count * i : count * (i + 1)] for i in range(4))
    load_sem, swap_send, swap_recv, sum_send, sum_recv = refs[4 * count :]
    bits = pairs.bit_length() - 1
    chip, core, device = group_layout(axes, sizes)
    sibling = device(chip, 1 - core)
    meet([sibling] + [device(flip(chip, mask, bits), core) for mask in range(1, pairs)])
    loads = []
    swaps = []
    for i in range(count):
        swap = pltpu.make_async_remote_copy(
            src_ref=inputs[i].at[:, 1 - core],
            dst_ref=peer[i],
            send_sem=swap_send.at[i],
            recv_sem=swap_recv.at[i],
            device_id=sibling,
            device_id_type=MESH,
        )
        swap.start()
        swaps.append(swap)
        load = pltpu.make_async_copy(inputs[i].at[:, core], mine[i], load_sem.at[i])
        load.start()
        loads.append(load)
    pushes = []
    for i in range(count):
        loads[i].wait()
        swaps[i].wait()
        rows = mine[i].shape[1]
        for mask in list(range(1, pairs)) + [0]:
            target = flip(chip, mask, bits)

            def add(index, carry):
                at = pl.ds(pl.multiple_of(index * 16, 16), 16)
                value = mine[i][target, at, :].astype(F32) + peer[i][target, at, :].astype(F32)
                summed[i][mask, at, :] = value.astype(BF16)
                return carry

            lax.fori_loop(0, rows // 16, add, 0)
            if mask:
                push = pltpu.make_async_remote_copy(
                    src_ref=summed[i].at[mask],
                    dst_ref=held[i].at[mask - 1],
                    send_sem=sum_send.at[i, mask - 1],
                    recv_sem=sum_recv.at[i, mask - 1],
                    device_id=device(target, core),
                    device_id_type=MESH,
                )
                push.start()
                pushes.append(push)
    for push in pushes:
        push.wait()
    for i in range(count):
        rows = mine[i].shape[1]

        def total(index, carry):
            at = pl.ds(pl.multiple_of(index * 16, 16), 16)
            value = summed[i][0, at, :].astype(F32)
            for mask in range(1, pairs):
                value = value + held[i][mask - 1, at, :].astype(F32)
            outputs[i][at, :] = value.astype(BF16)
            return carry

        lax.fori_loop(0, rows // 16, total, 0)


def group_scatter(values, axes, collective_id):
    sizes, pairs = group_sizes(axes)
    count = len(values)
    values = [v.reshape((pairs, 2) + v.shape[1:]) for v in values]
    tails = [v.shape[2:] for v in values]
    dma = pltpu.SemaphoreType.DMA
    return pl.pallas_call(
        functools.partial(group_scatter_kernel, count, pairs, axes, sizes),
        out_shape=tuple(jax.ShapeDtypeStruct(tail, BF16) for tail in tails),
        in_specs=[pl.BlockSpec(memory_space=pl.ANY)] * count,
        out_specs=(pl.BlockSpec(memory_space=pltpu.VMEM),) * count,
        scratch_shapes=[pltpu.VMEM((pairs,) + tail, BF16) for tail in tails] * 3
        + [pltpu.VMEM((pairs - 1,) + tail, BF16) for tail in tails]
        + [
            dma((count,)),
            dma((count,)),
            dma((count,)),
            dma((count, pairs - 1)),
            dma((count, pairs - 1)),
        ],
        compiler_params=pltpu.CompilerParams(
            collective_id=collective_id, has_side_effects=True, vmem_limit_bytes=48 * MIB
        ),
        cost_estimate=link_cost(values),
        name="group_scatter",
    )(*values)


def group_gather_kernel(count, pairs, axes, sizes, *refs):
    inputs, outputs = refs[:count], refs[count : 2 * count]
    own_sem, push_send, push_recv, relay_send, relay_recv = refs[2 * count :]
    bits = pairs.bit_length() - 1
    chip, core, device = group_layout(axes, sizes)
    sibling = device(chip, 1 - core)
    meet([sibling] + [device(flip(chip, mask, bits), core) for mask in range(1, pairs)])

    def push(i, mask, source):
        return pltpu.make_async_remote_copy(
            src_ref=inputs[i],
            dst_ref=outputs[i].at[source, core],
            send_sem=push_send.at[i, mask],
            recv_sem=push_recv.at[i, mask],
            device_id=device(flip(chip, mask, bits), core),
            device_id_type=MESH,
        )

    def relay(i, mask, side):
        source = flip(chip, mask, bits)
        return pltpu.make_async_remote_copy(
            src_ref=inputs[i] if mask == 0 else outputs[i].at[source, side],
            dst_ref=outputs[i].at[source, side],
            send_sem=relay_send.at[i, mask],
            recv_sem=relay_recv.at[i, mask],
            device_id=sibling,
            device_id_type=MESH,
        )

    for mask in range(1, pairs):
        for i in range(count):
            push(i, mask, chip).start()
    owns = []
    for i in range(count):
        relay(i, 0, core).start()
        own = pltpu.make_async_copy(inputs[i], outputs[i].at[chip, core], own_sem.at[i])
        own.start()
        owns.append(own)
    for mask in range(1, pairs):
        for i in range(count):
            push(i, mask, flip(chip, mask, bits)).wait_recv()
            relay(i, mask, core).start()
    for own in owns:
        own.wait()
    for mask in range(pairs):
        for i in range(count):
            if mask:
                push(i, mask, chip).wait_send()
            relay(i, mask, core).wait_send()
            relay(i, mask, 1 - core).wait_recv()


def group_gather(values, axes, collective_id):
    sizes, pairs = group_sizes(axes)
    count = len(values)
    dma = pltpu.SemaphoreType.DMA
    gathered = pl.pallas_call(
        functools.partial(group_gather_kernel, count, pairs, axes, sizes),
        out_shape=tuple(jax.ShapeDtypeStruct((pairs, 2) + v.shape, v.dtype) for v in values),
        in_specs=[pl.BlockSpec(memory_space=pl.ANY)] * count,
        out_specs=(pl.BlockSpec(memory_space=pl.ANY),) * count,
        scratch_shapes=[
            dma((count,)),
            dma((count, pairs)),
            dma((count, pairs)),
            dma((count, pairs)),
            dma((count, pairs)),
        ],
        compiler_params=pltpu.CompilerParams(collective_id=collective_id, has_side_effects=True),
        cost_estimate=link_cost(values, 2 * pairs),
        name="group_gather",
    )(*values)
    return [g.reshape((2 * pairs,) + v.shape) for g, v in zip(gathered, values)]


def expert_kernel(
    pairs,
    context_size,
    fe,
    x_ref,
    cot_ref,
    gate_ref,
    up_ref,
    down_ref,
    out_ref,
    part_ref,
    gate_out,
    up_out,
    down_out,
    x_all,
    x_tile,
    cot_tile,
    out_tile,
    grad_tile,
    sum_tile,
    peer_tile,
    grad_gate,
    grad_up,
    hidden_low,
    gate_acc,
    up_acc,
    down_acc,
    x_send,
    x_recv,
    relay_send,
    relay_recv,
    pass_send,
    pass_recv,
    own_sem,
    x_load,
    cot_load,
    out_store,
    swap_send,
    swap_recv,
    sum_send,
    sum_recv,
    acc_store,
    credit,
):
    micro_count, rows = x_ref.shape[0], x_ref.shape[1]
    units = gate_ref.shape[1]
    half = units // EXP_DEV
    experts = 2 * pairs * EXP_DEV
    bits = pairs.bit_length() - 1
    steps = micro_count * pairs
    across = pairs == 4
    tile_rows = 2 * rows
    place = lax.axis_index("dp") * context_size + lax.axis_index("context")
    core = lax.rem(place, 2)
    chip = lax.div(place, 2)

    def device(chip_index, core_index):
        index = chip_index * 2 + core_index
        return {"dp": lax.div(index, context_size), "context": lax.rem(index, context_size)}

    sibling = device(chip, 1 - core)
    meet([sibling] + [device(flip(chip, mask, bits), core) for mask in range(1, pairs)])

    def step_of(step):
        micro = lax.div(step, pairs)
        turn = lax.rem(step, pairs)
        backward = lax.rem(micro, 2)
        return micro, lax.rem(turn + backward, pairs)

    def push_x(micro, mask):
        return pltpu.make_async_remote_copy(
            src_ref=x_ref.at[micro],
            dst_ref=x_all.at[micro, chip, core],
            send_sem=x_send.at[micro, mask],
            recv_sem=x_recv.at[micro, mask],
            device_id=device(flip(chip, mask, bits), core),
            device_id_type=MESH,
        )

    def relay(micro, mask):
        source = flip(chip, mask, bits)
        return pltpu.make_async_remote_copy(
            src_ref=x_all.at[micro, source, core],
            dst_ref=x_all.at[micro, source, core],
            send_sem=relay_send.at[micro, mask],
            recv_sem=relay_recv.at[micro, mask],
            device_id=sibling,
            device_id_type=MESH,
        )

    def relay_arrival(micro, mask):
        source = flip(chip, mask, bits)
        return pltpu.make_async_remote_copy(
            src_ref=x_all.at[micro, source, 1 - core],
            dst_ref=x_all.at[micro, source, 1 - core],
            send_sem=relay_send.at[micro, mask],
            recv_sem=relay_recv.at[micro, mask],
            device_id=sibling,
            device_id_type=MESH,
        )

    def x_arrival(micro, mask):
        return pltpu.make_async_remote_copy(
            src_ref=x_ref.at[micro],
            dst_ref=x_all.at[micro, flip(chip, mask, bits), core],
            send_sem=x_send.at[micro, mask],
            recv_sem=x_recv.at[micro, mask],
            device_id=device(flip(chip, mask, bits), core),
            device_id_type=MESH,
        )

    middle = rows // 2
    parts = (pl.ds(0, middle), pl.ds(middle, rows - middle))

    def pass_on(micro, mask, source, part):
        return pltpu.make_async_remote_copy(
            src_ref=x_all.at[micro, source, core, parts[part]],
            dst_ref=x_all.at[micro, source, core, parts[part]],
            send_sem=pass_send.at[micro, part],
            recv_sem=pass_recv.at[micro, part],
            device_id=device(flip(chip, mask, bits), core),
            device_id_type=MESH,
        )

    def load(step):
        micro, mask = step_of(step)
        slot = lax.rem(step, 2)
        source = flip(chip, mask, bits)
        return (
            pltpu.make_async_copy(x_all.at[micro, source], x_tile.at[slot], x_load.at[slot]),
            pltpu.make_async_copy(
                cot_ref.at[pl.ds(2 * source, 2), micro], cot_tile.at[slot], cot_load.at[slot]
            ),
        )

    def store(step):
        micro, mask = step_of(step)
        slot = lax.rem(step, 2)
        return pltpu.make_async_copy(
            out_tile.at[slot],
            out_ref.at[pl.ds(2 * flip(chip, mask, bits), 2), micro],
            out_store.at[slot],
        )

    def swap(step):
        slot = lax.rem(step, 2)
        return pltpu.make_async_remote_copy(
            src_ref=grad_tile.at[slot, 1 - core],
            dst_ref=peer_tile.at[slot],
            send_sem=swap_send.at[slot],
            recv_sem=swap_recv.at[slot],
            device_id=sibling,
            device_id_type=MESH,
        )

    def push_sum(step):
        micro, mask = step_of(step)
        slot = lax.rem(step, 2)
        return pltpu.make_async_remote_copy(
            src_ref=sum_tile.at[slot],
            dst_ref=part_ref.at[micro, mask],
            send_sem=sum_send.at[slot],
            recv_sem=sum_recv.at[micro, mask],
            device_id=device(flip(chip, mask, bits), core),
            device_id_type=MESH,
        )

    def keep_sum(step):
        micro, mask = step_of(step)
        slot = lax.rem(step, 2)
        return pltpu.make_async_copy(
            sum_tile.at[slot], part_ref.at[micro, mask], sum_send.at[slot]
        )

    def wait_sum_sent(step):
        mask = step_of(step)[1]

        @pl.when(mask > 0)
        def _():
            push_sum(step).wait_send()

        @pl.when(mask == 0)
        def _():
            keep_sum(step).wait()

    def fetch(step):
        micro, mask = step_of(step)

        if not across:

            @pl.when(mask > 0)
            def _():
                x_arrival(micro, mask).wait_recv()
                relay(micro, mask).start()

        else:

            @pl.when((mask == 1) | (mask == 2))
            def _():
                x_arrival(micro, mask).wait_recv()
                relay(micro, mask).start()

            for part in range(2):

                @pl.when(mask == part + 1)
                def _():
                    pass_on(micro, 2 - part, flip(chip, part + 1, bits), part).start()

            @pl.when(mask == 3)
            def _():
                for part in range(2):
                    pass_on(micro, part + 1, flip(chip, 3, bits), part).wait_recv()
                relay(micro, mask).start()

    def begin_load(step):
        micro, mask = step_of(step)
        relay_arrival(micro, mask).wait_recv()
        for copy in load(step):
            copy.start()

    def finish_sum(step):
        slot = lax.rem(step, 2)
        swap(step).wait()

        @pl.when(step >= 2)
        def _():
            wait_sum_sent(step - 2)

        def add(index, carry):
            at = pl.ds(pl.multiple_of(index * 16, 16), 16)
            value = grad_tile[slot, core, at, :].astype(F32) + peer_tile[slot, at, :].astype(F32)
            sum_tile[slot, at, :] = value.astype(BF16)
            return carry

        lax.fori_loop(0, rows // 16, add, 0)

        @pl.when(step < steps - 2)
        def _():
            pl.semaphore_signal(credit, inc=1, device_id=sibling, device_id_type=MESH)

        mask = step_of(step)[1]

        @pl.when(mask > 0)
        def _():
            push_sum(step).start()

        @pl.when(mask == 0)
        def _():
            keep_sum(step).start()

    direct = (1, 2) if across else tuple(range(1, pairs))
    for mask in direct:
        push_x(0, mask).start()
    own_copies = []
    for micro in range(micro_count):
        own = pltpu.make_async_copy(x_ref.at[micro], x_all.at[micro, chip, core], own_sem.at[micro])
        own.start()
        own_copies.append(own)
    for own in own_copies:
        own.wait()
    for micro in range(micro_count):
        relay(micro, 0).start()
    gate_acc[...] = jnp.zeros_like(gate_acc)
    up_acc[...] = jnp.zeros_like(up_acc)
    down_acc[...] = jnp.zeros_like(down_acc)
    begin_load(0)

    chunk = 256 if units % 256 == 0 else LANES
    out_chunk = 512
    slab = half - LANES
    first_lane = fe % LANES

    def work(step, carry):
        slot = lax.rem(step, 2)

        @pl.when(step == 1)
        def _():
            for micro in range(1, micro_count):
                for mask in direct:
                    push_x(micro, mask).start()

        for copy in load(step):
            copy.wait()

        @pl.when(step >= 2)
        def _():
            store(step - 2).wait()

        x_ext = x_tile[slot].reshape(tile_rows, D + LANES)
        x = x_ext[:, :D]
        chosen = x_ext[:, D:].astype(F32)
        cot = cot_tile[slot].reshape(tile_rows, D)
        lane = lax.broadcasted_iota(jnp.int32, (tile_rows, LANES), 1) - first_lane
        valid = (lane >= 0) & (lane < experts)

        slab_chunk = slab // chunk * chunk
        first_gate = mm(x, gate_ref[:, slab_chunk : slab_chunk + chunk])
        slab_gate = first_gate[:, slab - slab_chunk : slab - slab_chunk + LANES]
        logits = jnp.where(valid, slab_gate, -1e30)
        weights = jnp.where(
            valid, jnp.exp(logits - jnp.max(logits, axis=-1, keepdims=True)), 0.0
        )
        router_probs = weights / jnp.sum(weights, axis=-1, keepdims=True)
        named = router_probs * chosen
        picks = [lane == place * EXP_DEV + number for number in range(EXP_DEV)]
        scales = [
            jnp.sum(jnp.where(pick, named, 0.0), axis=-1, keepdims=True) for pick in picks
        ]
        flags = [
            jnp.sum(jnp.where(pick, chosen, 0.0), axis=-1, keepdims=True) for pick in picks
        ]
        dots = [jnp.zeros((tile_rows, 1), F32) for _ in picks]
        column = lax.broadcasted_iota(jnp.int32, (tile_rows, chunk), 1)
        starts = [slab_chunk] + [at for at in range(0, units, chunk) if at != slab_chunk]
        for start in starts:
            at = slice(start, start + chunk)
            gate = first_gate if start == slab_chunk else mm(x, gate_ref[:, at])
            up = mm(x, up_ref[:, at])
            back = mm_nt(cot, down_ref[at, :])
            first, last = start // half, (start + chunk - 1) // half
            scale = scales[first]
            if last > first:
                scale = jnp.where(column < last * half - start, scales[first], scales[last])
            sig = jax.nn.sigmoid(gate)
            act = gate * sig
            hidden = act * up
            grad_hidden = back * scale
            hidden_low[:, at] = (hidden * scale).astype(BF16)
            grad_gate[:, at] = (grad_hidden * up * (sig * (1.0 + gate * (1.0 - sig)))).astype(BF16)
            grad_up[:, at] = (grad_hidden * act).astype(BF16)
            product = hidden * back
            if last > first:
                split = last * half - start
                dots[first] = dots[first] + jnp.sum(product[:, :split], axis=-1, keepdims=True)
                dots[last] = dots[last] + jnp.sum(product[:, split:], axis=-1, keepdims=True)
            else:
                dots[first] = dots[first] + jnp.sum(product, axis=-1, keepdims=True)
        spread = jnp.zeros((tile_rows, LANES), F32)
        for pick, dot, flag in zip(picks, dots, flags):
            spread = spread + jnp.where(pick, dot * flag, 0.0)
        grad_logits = router_probs * (
            spread - jnp.sum(router_probs * spread, axis=-1, keepdims=True)
        )
        grad_gate[:, slab:half] = jnp.where(
            lane < 0, grad_gate[:, slab:half].astype(F32), grad_logits
        ).astype(BF16)

        @pl.when(step + 1 < steps)
        def _():
            fetch(step + 1)

        @pl.when(step >= 2)
        def _():
            pl.semaphore_wait(credit, 1)

        for start in range(0, D, out_chunk):
            at = slice(start, start + out_chunk)
            grad = mm_nt(grad_gate[...], gate_ref[at, :]) + mm_nt(grad_up[...], up_ref[at, :])
            grad_tile[slot, :, :, at] = grad.astype(BF16).reshape(2, rows, out_chunk)
        swap(step).start()

        @pl.when(step >= 1)
        def _():
            finish_sum(step - 1)

        for start in range(0, D, out_chunk):
            at = slice(start, start + out_chunk)
            out_tile[slot, :, :, at] = (
                mm(hidden_low[...], down_ref[:, at]).astype(BF16).reshape(2, rows, out_chunk)
            )
        store(step).start()
        for start in range(0, D, out_chunk):
            at = slice(start, start + out_chunk)
            x_part = x_tile[slot, :, :, at].reshape(tile_rows, out_chunk)
            gate_acc[at, :] += mm_tn(x_part, grad_gate[...])
            up_acc[at, :] += mm_tn(x_part, grad_up[...])

        @pl.when(step + 1 < steps)
        def _():
            begin_load(step + 1)

        for start in range(0, units, chunk):
            at = slice(start, start + chunk)
            down_acc[at, :] += mm_tn(hidden_low[:, at], cot)
        return carry

    lax.fori_loop(0, steps, work, 0)
    finals = []
    for number, (acc, target) in enumerate(
        ((gate_acc, gate_out), (up_acc, up_out), (down_acc, down_out))
    ):
        copy = pltpu.make_async_copy(acc, target, acc_store.at[number])
        copy.start()
        finals.append(copy)
    finish_sum(steps - 1)
    wait_sum_sent(steps - 2)
    wait_sum_sent(steps - 1)
    for copy in finals:
        copy.wait()
    store(steps - 2).wait()
    store(steps - 1).wait()
    for micro in range(micro_count):
        if across:
            for part in range(2):
                pass_on(micro, 2 - part, flip(chip, part + 1, bits), part).wait_send()
        for mask in range(pairs):
            relay(micro, mask).wait_send()
            if mask in direct:
                push_x(micro, mask).wait_send()
            if mask:
                pltpu.make_async_remote_copy(
                    src_ref=sum_tile.at[0],
                    dst_ref=part_ref.at[micro, mask],
                    send_sem=sum_send.at[0],
                    recv_sem=sum_recv.at[micro, mask],
                    device_id=device(flip(chip, mask, bits), core),
                    device_id_type=MESH,
                ).wait_recv()


def expert_pass(x_ext, cot_all, gate_w, up_w, down_w, fe, collective_id):
    micro_count, rows, width = x_ext.shape
    context_size = lax.axis_size("context")
    pairs = lax.axis_size("dp") * context_size // 2
    units = gate_w.shape[1]
    anywhere = pl.BlockSpec(memory_space=pl.ANY)
    weights = pl.BlockSpec(memory_space=pltpu.VMEM)
    dma = pltpu.SemaphoreType.DMA
    return pl.pallas_call(
        functools.partial(expert_kernel, pairs, context_size, fe),
        out_shape=(
            jax.ShapeDtypeStruct((2 * pairs, micro_count, rows, D), BF16),
            jax.ShapeDtypeStruct((micro_count, pairs, rows, D), BF16),
            jax.ShapeDtypeStruct((D, units), F32),
            jax.ShapeDtypeStruct((D, units), F32),
            jax.ShapeDtypeStruct((units, D), F32),
            jax.ShapeDtypeStruct((micro_count, pairs, 2, rows, width), BF16),
        ),
        in_specs=[anywhere, anywhere, weights, weights, weights],
        out_specs=(anywhere,) * 6,
        scratch_shapes=[
            pltpu.VMEM((2, 2, rows, width), BF16),
            pltpu.VMEM((2, 2, rows, D), BF16),
            pltpu.VMEM((2, 2, rows, D), BF16),
            pltpu.VMEM((2, 2, rows, D), BF16),
            pltpu.VMEM((2, rows, D), BF16),
            pltpu.VMEM((2, rows, D), BF16),
            pltpu.VMEM((2 * rows, units), BF16),
            pltpu.VMEM((2 * rows, units), BF16),
            pltpu.VMEM((2 * rows, units), BF16),
            pltpu.VMEM((D, units), F32),
            pltpu.VMEM((D, units), F32),
            pltpu.VMEM((units, D), F32),
            dma((micro_count, pairs)),
            dma((micro_count, pairs)),
            dma((micro_count, pairs)),
            dma((micro_count, pairs)),
            dma((micro_count, 2)),
            dma((micro_count, 2)),
            dma((micro_count,)),
            dma((2,)),
            dma((2,)),
            dma((2,)),
            dma((2,)),
            dma((2,)),
            dma((2,)),
            dma((micro_count, pairs)),
            dma((3,)),
            pltpu.SemaphoreType.REGULAR,
        ],
        compiler_params=pltpu.CompilerParams(
            collective_id=collective_id, has_side_effects=True, vmem_limit_bytes=62 * MIB
        ),
        cost_estimate=pl.CostEstimate(
            flops=36 * pairs * micro_count * rows * D * units,
            bytes_accessed=500_000_000,
            transcendentals=0,
        ),
        name="expert_pass",
    )(x_ext, cot_all, gate_w, up_w, down_w)[:5]


def swiglu_pass(x, cot, gate_w, up_w, down_w):
    gate = mm(x, gate_w)
    up = mm(x, up_w)
    sig = jax.nn.sigmoid(gate)
    act = gate * sig
    back = mm_nt(cot, down_w)
    hidden = (act * up).astype(BF16)
    out = mm(hidden, down_w)
    grad_gate = (back * up * (sig * (1.0 + gate * (1.0 - sig)))).astype(BF16)
    grad_up = (back * act).astype(BF16)
    grad_x = mm_nt(grad_gate, gate_w) + mm_nt(grad_up, up_w)
    weight_grads = [mm_tn(x, grad_gate), mm_tn(x, grad_up), mm_tn(cot, hidden)]
    return out, grad_x, [grad.astype(BF16) for grad in weight_grads]


def per_device(
    tokens,
    segments,
    expert_ids,
    norm_attn,
    w_query,
    w_kv_down,
    norm_latent,
    w_kv_up,
    w_out,
    norm_ffn,
    w_router,
    w_shared_gate,
    w_shared_up,
    w_shared_down,
    w_expert_gate,
    w_expert_up,
    w_expert_down,
    cotangent,
):
    micro_count, block_rows = tokens.shape[:2]
    rows = micro_count * block_rows
    seq_len = segments.shape[1]
    context_size = lax.axis_size("context")
    groups = lax.axis_size("dp") * context_size
    tensor_size = lax.axis_size("tensor")
    group_index = lax.axis_index("dp") * context_size + lax.axis_index("context")
    own_rows = block_rows // tensor_size
    own_start = lax.axis_index("tensor") * own_rows
    experts = EXP_DEV * groups
    heads_local = w_query.shape[1] // (NOPE + ROPE)
    fe_local = w_expert_gate.shape[2]
    half = -(-(fe_local + experts) // LANES) * LANES
    scale_factor = (NOPE + ROPE) ** (-0.5)
    start_row = lax.axis_index("context") * block_rows
    query_index = start_row + jnp.arange(block_rows)
    key_index = jnp.arange(seq_len)
    cos_block, sin_block = angles(query_index.astype(F32), ROPE)
    cos_query = jnp.tile(cos_block, (micro_count, 1))
    sin_query = jnp.tile(sin_block, (micro_count, 1))
    gain_attn = norm_attn.astype(F32)
    gain_latent = norm_latent.astype(F32)
    gain_ffn = norm_ffn.astype(F32)

    def own(values):
        values = values.reshape((micro_count, block_rows) + values.shape[1:])
        part = lax.dynamic_slice_in_dim(values, own_start, own_rows, axis=1)
        return part.reshape((micro_count * own_rows,) + values.shape[2:])

    def to_owner(values, collective_id):
        values = values.astype(BF16).reshape(micro_count, tensor_size, own_rows, values.shape[-1])
        summed = push_scatter(values, ("tensor",), collective_id)
        return summed.reshape(micro_count * own_rows, values.shape[-1])

    def from_owners(values, collective_id):
        values = values.reshape(micro_count, own_rows, values.shape[-1])
        return push_gather(values, ("tensor",), collective_id).reshape(rows, values.shape[-1])

    out_rows = w_out.shape[0] // groups
    out_full = lax.dynamic_slice_in_dim(w_out, group_index * out_rows, out_rows)
    out_full = lax.all_gather(out_full, "tensor", axis=0)
    out_full = lax.all_gather(out_full, GROUP, axis=0)
    out_full = out_full.transpose(1, 0, 2, 3).reshape(tensor_size * w_out.shape[0], D)
    cot_all = lax.all_gather(cotangent, GROUP, axis=0)
    zeros = jnp.zeros((D, half - fe_local - experts), BF16)
    more = jnp.zeros((D, half - fe_local), BF16)
    gate_wide = jnp.concatenate([w_expert_gate[0], w_router, zeros, w_expert_gate[1], more], axis=1)
    up_wide = jnp.concatenate([w_expert_up[0], more, w_expert_up[1], more], axis=1)
    down_wide = jnp.pad(w_expert_down, ((0, 0), (0, half - fe_local), (0, 0)))
    down_wide = down_wide.reshape(EXP_DEV * half, D)
    slots = jnp.arange(LANES) - fe_local % LANES
    named = jnp.any(expert_ids[..., None] == slots, axis=2).astype(BF16)

    x_rows = tokens.reshape(rows, D).astype(F32)
    cot_rows = cotangent.reshape(rows, D)
    inv_attn = rms_scale(x_rows)
    normed_attn = x_rows * inv_attn
    x_attn = (normed_attn * gain_attn).astype(BF16)
    kv_raw = mm(x_attn, w_kv_down)
    latent_raw = kv_raw[:, :LATENT]
    inv_latent = rms_scale(latent_raw)
    normed_latent = latent_raw * inv_latent
    latent = (normed_latent * gain_latent).astype(BF16)
    key_rope = rotate(kv_raw[:, LATENT:], cos_query, sin_query).astype(BF16)
    kv_own = jnp.concatenate([latent, key_rope], axis=1)
    kv_all = group_gather(list(jnp.split(kv_own, micro_count)), ("context",), 1)
    kv_all = jnp.concatenate(kv_all, axis=0).reshape(micro_count * seq_len, LATENT + ROPE)
    query = mm(x_attn, w_query).reshape(rows, heads_local, NOPE + ROPE)
    query_rot = jnp.concatenate(
        [
            query[..., :NOPE],
            rotate(query[..., NOPE:], cos_query[:, None, :], sin_query[:, None, :]),
        ],
        axis=-1,
    ).astype(BF16)
    latent_all = kv_all[:, :LATENT]
    expanded = mm(latent_all, w_kv_up).astype(BF16)
    expanded = expanded.reshape(micro_count, seq_len, heads_local, NOPE + VDIM)
    key_rope_all = kv_all[:, LATENT:].reshape(micro_count, seq_len, ROPE)
    query_rot = query_rot.reshape(micro_count, block_rows, heads_local, NOPE + ROPE)
    seg_query = lax.dynamic_slice_in_dim(segments, start_row, block_rows, axis=1)
    allowed = (seg_query[:, :, None] == segments[:, None, :]) & (
        key_index[None, None, :] <= query_index[None, :, None]
    )
    probs = []
    attended = []
    for m in range(micro_count):
        key_nope, head_values = expanded[m, ..., :NOPE], expanded[m, ..., NOPE:]
        raw = jnp.einsum(
            "chd,lhd->hcl", query_rot[m, ..., :NOPE], key_nope, preferred_element_type=F32
        )
        raw = raw + jnp.einsum(
            "chd,ld->hcl", query_rot[m, ..., NOPE:], key_rope_all[m], preferred_element_type=F32
        )
        scores = jnp.where(allowed[m][None], raw * scale_factor, -1e30)
        top_score = jnp.max(scores, axis=-1, keepdims=True)
        weights_exp = jnp.where(allowed[m][None], jnp.exp(scores - top_score), 0.0)
        probs.append(weights_exp / jnp.sum(weights_exp, axis=-1, keepdims=True))
        part = jnp.einsum(
            "hcl,lhd->chd", probs[m].astype(BF16), head_values, preferred_element_type=F32
        )
        attended.append(part.astype(BF16).reshape(block_rows, heads_local * VDIM))
    attended = jnp.concatenate(attended, axis=0)
    attended_all = push_gather(attended, ("tensor",), 2, columns=True)
    hidden_one = x_rows + mm(attended_all, out_full)
    inv_ffn = rms_scale(hidden_one)
    normed_ffn = hidden_one * inv_ffn
    x_ffn = (normed_ffn * gain_ffn).astype(BF16)
    x_ext = jnp.concatenate([x_ffn.reshape(micro_count, block_rows, D), named], axis=-1)

    shared_out, shared_grad_x, shared_grads = swiglu_pass(
        x_ffn, cot_rows, w_shared_gate, w_shared_up, w_shared_down
    )
    out_part, grad_part, gate_grad, up_grad, down_grad = expert_pass(
        x_ext, cot_all, gate_wide, up_wide, down_wide, fe_local, 3
    )
    router_grad = gate_grad[:, fe_local : fe_local + experts]

    def unit_columns(grad):
        return jnp.stack([grad[:, half * e : half * e + fe_local] for e in range(EXP_DEV)])

    down_grad = down_grad.reshape(EXP_DEV, half, D)[:, :fe_local]
    grad_sum = jnp.sum(grad_part.astype(F32), axis=1).reshape(rows, D) + shared_grad_x
    grad_x_ffn = to_owner(grad_sum, 4)
    out_sum = lax.psum_scatter(out_part, GROUP, scatter_dimension=0, tiled=False).reshape(rows, D)
    out_sum = lax.psum((out_sum.astype(F32) + shared_out).astype(BF16), "tensor")
    output = (hidden_one + out_sum.astype(F32)).astype(BF16)

    normed_own = own(normed_ffn)
    norm_ffn_grad = jnp.sum(grad_x_ffn * normed_own, axis=0)
    grad_one = own(cot_rows).astype(F32) + norm_back(
        grad_x_ffn * gain_ffn, normed_own, own(inv_ffn)
    )
    grad_attn_low = from_owners(grad_one.astype(BF16), 5)
    out_grad = mm_tn(grad_attn_low, attended).astype(BF16)
    early = jnp.concatenate(shared_grads + [out_grad], axis=1)
    early = lax.psum_scatter(early, GROUP, scatter_dimension=0, tiled=True)
    early = lax.all_gather(early, GROUP, axis=0, tiled=True)
    grad_attended = mm_nt(grad_attn_low, w_out).astype(BF16)
    grad_attended = grad_attended.reshape(micro_count, block_rows, heads_local, VDIM)
    grad_expanded = []
    grad_key_rope = []
    grad_query = []
    for m in range(micro_count):
        key_nope, head_values = expanded[m, ..., :NOPE], expanded[m, ..., NOPE:]
        grad_probs = jnp.einsum(
            "chd,lhd->hcl", grad_attended[m], head_values, preferred_element_type=F32
        )
        grad_scores = (
            probs[m] * (grad_probs - jnp.sum(probs[m] * grad_probs, axis=-1, keepdims=True))
        ).astype(BF16)
        grad_values = jnp.einsum(
            "hcl,chd->lhd", probs[m].astype(BF16), grad_attended[m], preferred_element_type=F32
        )
        grad_key_nope = scale_factor * jnp.einsum(
            "hcl,chd->lhd", grad_scores, query_rot[m, ..., :NOPE], preferred_element_type=F32
        )
        grad_key_rope.append(
            scale_factor
            * jnp.einsum(
                "hcl,chd->ld", grad_scores, query_rot[m, ..., NOPE:], preferred_element_type=F32
            )
        )
        grad_query_nope = scale_factor * jnp.einsum(
            "hcl,lhd->chd", grad_scores, key_nope, preferred_element_type=F32
        )
        grad_query_rope = scale_factor * jnp.einsum(
            "hcl,ld->chd", grad_scores, key_rope_all[m], preferred_element_type=F32
        )
        grad_expanded.append(
            jnp.concatenate([grad_key_nope, grad_values], axis=-1)
            .reshape(seq_len, heads_local * (NOPE + VDIM))
            .astype(BF16)
        )
        grad_query.append(
            jnp.concatenate(
                [
                    grad_query_nope,
                    unrotate(grad_query_rope, cos_block[:, None, :], sin_block[:, None, :]),
                ],
                axis=-1,
            ).reshape(block_rows, heads_local * (NOPE + ROPE))
        )
    grad_expanded = jnp.concatenate(grad_expanded, axis=0)
    grad_key_rope = jnp.concatenate(grad_key_rope, axis=0)
    grad_query_raw = jnp.concatenate(grad_query, axis=0).astype(BF16)
    kv_up_grad = mm_tn(latent_all, grad_expanded)
    grad_kv_part = jnp.concatenate([mm_nt(grad_expanded, w_kv_up), grad_key_rope], axis=1)
    grad_kv = group_scatter(
        [
            part.reshape(context_size, block_rows, LATENT + ROPE)
            for part in jnp.split(grad_kv_part.astype(BF16), micro_count)
        ],
        ("context",),
        6,
    )
    grad_kv = jnp.concatenate(grad_kv, axis=0)
    query_grad = mm_tn(x_attn, grad_query_raw).astype(BF16)
    grad_x_heads = mm_nt(grad_query_raw, w_query).astype(BF16)
    router_part = router_grad.astype(BF16).reshape(tensor_size, micro_count, own_rows, -1)
    router_part = router_part.transpose(1, 0, 2, 3).reshape(rows, -1)
    late = to_owner(jnp.concatenate([grad_x_heads, grad_kv, router_part], axis=1), 7)
    grad_x_heads, grad_latent, grad_rope_key, router_own = jnp.split(
        late, [D, D + LATENT, D + LATENT + ROPE], axis=1
    )
    normed_latent_own = own(normed_latent)
    norm_latent_grad = jnp.sum(grad_latent * normed_latent_own, axis=0)
    grad_latent_raw = norm_back(grad_latent * gain_latent, normed_latent_own, own(inv_latent))
    grad_kv_raw = jnp.concatenate(
        [grad_latent_raw, unrotate(grad_rope_key, own(cos_query), own(sin_query))], axis=-1
    ).astype(BF16)
    grad_x_attn = grad_x_heads + mm_nt(grad_kv_raw, w_kv_down)
    normed_attn_own = own(normed_attn)
    norm_attn_grad = jnp.sum(grad_x_attn * normed_attn_own, axis=0)
    grad_input = grad_one + norm_back(grad_x_attn * gain_attn, normed_attn_own, own(inv_attn))
    finished = from_owners(jnp.concatenate([grad_input.astype(BF16), grad_kv_raw], axis=1), 8)
    grad_tokens, grad_kv_raw = finished[:, :D], finished[:, D:]

    slice_rows = D // tensor_size
    x_slice = lax.dynamic_slice_in_dim(
        x_attn, lax.axis_index("tensor") * slice_rows, slice_rows, axis=1
    )
    kv_down_grad = mm_tn(x_slice, grad_kv_raw).astype(BF16)
    query_part, kv_up_part, kv_down_part, router_part = group_scatter(
        [
            query_grad.reshape(groups, D // groups, -1),
            kv_up_grad.astype(BF16).reshape(groups, LATENT // groups, -1),
            kv_down_grad.reshape(groups, slice_rows // groups, -1),
            router_own.astype(BF16).reshape(groups, 16, -1),
        ],
        GROUP,
        9,
    )
    router_width = router_part.shape[1]
    router_part = jnp.pad(router_part, ((0, 0), (0, LATENT + ROPE - router_width)))
    sliced = jnp.concatenate([kv_down_part, router_part], axis=0)
    sliced = push_gather(sliced[None], ("tensor",), 10)
    query_grad, kv_up_grad, sliced = group_gather(
        [query_part, kv_up_part, sliced.reshape(-1, LATENT + ROPE)], GROUP, 11
    )
    sliced = sliced.reshape(groups, tensor_size, -1, LATENT + ROPE).transpose(1, 0, 2, 3)
    kv_down_grad = sliced[:, :, :-16].reshape(D, LATENT + ROPE).astype(F32)
    router_grad = sliced[:, :, -16:, :router_width].reshape(D, experts).astype(F32)
    small = jnp.concatenate([norm_attn_grad, norm_ffn_grad, norm_latent_grad])
    small = jnp.sum(push_gather(small.reshape(1, -1, LANES), EVERY, 12), axis=(0, 1)).reshape(-1)
    ff_local = w_shared_gate.shape[1]
    early = early.astype(F32)
    return (
        output.reshape(tokens.shape),
        grad_tokens.reshape(tokens.shape),
        small[:D],
        query_grad.reshape(D, -1).astype(F32),
        kv_down_grad,
        small[D + D :],
        kv_up_grad.reshape(LATENT, -1).astype(F32),
        early[:, 3 * ff_local :].T,
        small[D : D + D],
        router_grad,
        early[:, :ff_local],
        early[:, ff_local : 2 * ff_local],
        early[:, 2 * ff_local : 3 * ff_local].T,
        unit_columns(gate_grad),
        unit_columns(up_grad),
        down_grad,
    )


def solution(mesh):
    return jax.shard_map(
        per_device,
        mesh=mesh,
        in_specs=(
            P("dp", "context", None),
            P("dp", None),
            P("dp", "context", None),
            P(),
            P(None, "tensor"),
            P(),
            P(),
            P(None, "tensor"),
            P("tensor", None),
            P(),
            P(),
            P(None, "tensor"),
            P(None, "tensor"),
            P("tensor", None),
            P(("dp", "context"), None, "tensor"),
            P(("dp", "context"), None, "tensor"),
            P(("dp", "context"), "tensor", None),
            P("dp", "context", None),
        ),
        out_specs=(
            P("dp", "context", None),
            P("dp", "context", None),
            P(),
            P(None, "tensor"),
            P(),
            P(),
            P(None, "tensor"),
            P("tensor", None),
            P(),
            P(),
            P(None, "tensor"),
            P(None, "tensor"),
            P("tensor", None),
            P(("dp", "context"), None, "tensor"),
            P(("dp", "context"), None, "tensor"),
            P(("dp", "context"), "tensor", None),
        ),
        check_vma=False,
    )
```

time: 2120 us -> 1200 us (0.57)
  waiting for transfers between devices: 874 us -> 117 us
  Pallas kernels: 0 us -> 678 us
  matrix products: 537 us -> 111 us
  local copies, waits for them, and re-layouts: 390 us -> 176 us
  other arithmetic: 257 us -> 92.4 us
  blocking collectives: 28.6 us -> 0 us
    pallas_call x0 -> x12, Pallas kernels: none -> 678 us  [the longest x1 257 us: expert_pass(): pl.pallas_call(functools.partial(expert_kernel, pairs, context_size, fe),...]
    dot_general x82 -> x35, matrix products: 535 us -> 95.5 us  [the longest x7 26.3 us: mm(): return jnp.dot(left, right, preferred_element_type=F32)]
    reduce_scatter x7 -> x2, waiting for transfers between devices: 433 us -> 85 us  [the longest x1 85 us: per_device(): early = lax.psum_scatter(early, GROUP, scatter_dimension=0, tiled=True)]
    psum x5 -> x1, waiting for transfers between devices: 312 us -> 0.01 us  [per_device(): lax.psum((out_sum.astype(F32) + shared_out).astype(BF16), 'tensor')]
    gather x18 -> x0, local copies, waits for them, and re-layouts: 217 us -> none  [the longest x2 54.9 us: per_device(): jnp.take(grad_padded, source_pair, axis=0)]
    all_gather x5 -> x4, waiting for transfers between devices: 127 us -> 31.7 us  [the longest x1 31.7 us: per_device(): out_full = lax.all_gather(out_full, 'tensor', axis=0)]
    reduce_sum x19 -> x4, other arithmetic: 82.2 us -> 6.13 us  [the longest x1 4.32 us: per_device(): jnp.sum(grad_part.astype(F32), axis=1).reshape(rows, D) + shared_grad_x]
    select_n x10 -> x0, other arithmetic: 55 us -> none  [the longest x2 22.1 us: per_device(): jnp.take(grad_padded, source_pair, axis=0)]
  transfers between devices with their start and end apart: 17 -> 7, of which waited for: 10 -> 2; matrix products, arithmetic and copies ran while one was open for 27% -> 27% of each run, Pallas kernels for 0% -> 35%
where the time goes in v1:
time: 1200 us; the launch traced here: 1190 us
  Pallas kernels  678 us (56%)
  local copies, waits for them, and re-layouts  176 us (15%)
  waiting for transfers between devices  117 us (10%)
  matrix products  111 us (9%)
  other arithmetic  92.4 us (8%)
  between operations  15.8 us (1%)
    pallas_call x1, Pallas kernels, expert_pass(): pl.pallas_call(functools.partial(expert_kernel, pairs, context_size, fe),...  257 us
    pallas_call x5, Pallas kernels, push_gather(): pl.pallas_call(functools.partial(gather_kernel, axes, sizes, columns), ou...  194 us
    pallas_call x2, Pallas kernels, push_scatter(): pl.pallas_call(functools.partial(scatter_kernel, axes, sizes), out_shape=...  96.3 us
    reduce_scatter x1, waiting for transfers between devices, per_device(): early = lax.psum_scatter(early, GROUP, scatter_dimension=0, tiled=True)  85 us
    pallas_call x2, Pallas kernels, group_gather(): pl.pallas_call(functools.partial(group_gather_kernel, count, pairs, axes,...  76 us
    unnamed x213, local copies, waits for them, and re-layouts  62.9 us
    pallas_call x2, Pallas kernels, group_scatter(): pl.pallas_call(functools.partial(group_scatter_kernel, count, pairs, axes...  54.9 us
    all_gather x1, waiting for transfers between devices, per_device(): out_full = lax.all_gather(out_full, 'tensor', axis=0)  31.7 us
  transfers between devices with their start and end apart: 7, of which 2 were waited for; matrix products, arithmetic and copies ran while one was open for 27% of the time, Pallas kernels for 35%

profile of v1, /device:TPU:0, one launch (start us, length us, event | category | flops | bytes accessed | tf_op | source)
XLA Modules:
  0.0 1191.5 jit_solution(15081509505354889229)
XLA Ops:
  9.2 31.7 %all-gather.10.cloned.1.call-done = bf16[256,2048]{1,0:T(8,128)(2,1)} async-done(((bf16[64,2048]{1,0:T(8,128)(2,1)}), bf16[256,2048]{1,0:T(8,128)(2,1)}) %all-gather.10.cloned.1.call-update) | async-done | bytes 1048592 | tf_op jit(solution)/shard_map/all_gather | solution.py:973
  48.7 30.2 %group_gather.2 = (bf16[2,2,256,576]{3,2,1,0:T(8,128)(2,1)}, bf16[2,2,256,576]{3,2,1,0:T(8,128)(2,1)}) custom-call(bf16[256,576]{1,0:T(8,128)(2,1)} %get-tuple-element.167.refs_0_, bf16[256,576]{1,0:T(8,128)(2,1)} %get-tuple-element.166.refs_1_), custom_call_target="tpu_custom_call" | custom-call | bytes 47185920 | tf_op jit(solution)/shard_map/group_gather/pallas_call | solution.py:397
  82.6 4.4 convolution_convert_fusion
  87.0 8.2 reshape.564
  95.2 4.7 copy.208
  102.4 4.1 fusion.90
  118.3 7.1 fusion.98
  125.4 4.1 convolution_convert_fusion.13
  133.7 4.1 fusion.53
  137.8 6.5 fusion.97
  144.9 4.1 convolution_convert_fusion.12
  152.7 38.6 %push_gather.5 = bf16[512,2048]{1,0:T(8,128)(2,1)} custom-call(bf16[512,512]{1,0:T(8,128)(2,1)} %pad_maximum_fusion.16.v_ref), custom_call_target="tpu_custom_call" | custom-call | bytes 167772160 | tf_op jit(solution)/shard_map/push_gather/pallas_call | solution.py:150
  192.0 3.8 fusion.92
  202.0 3.7 fusion.91
  210.8 3.9 pad.8
  216.5 6.8 concatenate.98.gate_ref
  223.3 4.6 pad_maximum_fusion.4.up_ref
  227.9 8.5 copy.222
  236.4 7.1 multiply_reduce_fusion.2
  249.7 256.9 %expert_pass.1 = (bf16[8,2,256,2048]{3,2,1,0:T(8,128)(2,1)}, bf16[2,4,256,2048]{3,2,1,0:T(8,128)(2,1)}, f32[2048,768]{1,0:T(8,128)}, f32[2048,768]{1,0:T(8,128)}...) custom-call(bf16[2,256,2176]{2,1,0:T(8,128)(2,1)} %pad_maximum_fusion.8.x_ref, ...), custom_call_target="tpu_custom_call" | custom-call | flops 115964116992 | bytes 500000000 | tf_op jit(solution)/shard_map/expert_pass/pallas_call | solution.py:844
  508.2 3.6 fusion.100
  526.4 4.2 fusion.102
  530.6 4.3 convert_reduce_fusion
  534.9 7.2 fusion.3
  542.1 47.1 %push_scatter.2 = f32[2,64,2048]{2,1,0:T(8,128)S(1)} custom-call(bf16[2,4,64,2048]{3,2,1,0:T(8,128)(2,1)S(1)} %bitcast.360), custom_call_target="tpu_custom_call" | custom-call | bytes 167772160 | tf_op jit(solution)/shard_map/push_scatter/pallas_call | solution.py:205
  592.0 48.8 %push_gather.6 = bf16[2,4,64,2048]{3,2,1,0:T(8,128)(2,1)} custom-call(bf16[2,64,2048]{2,1,0:T(8,128)(2,1)} %add_convert_fusion.1.v_ref), custom_call_target="tpu_custom_call" | custom-call | bytes 167772160 | tf_op jit(solution)/shard_map/push_gather/pallas_call | solution.py:150
  644.2 25.1 %pad_maximum_fusion = bf16[2048,2624]{0,1:T(8,128)(2,1)} fusion(bf16[2048,512]{0,1:T(8,128)(2,1)S(1)} %convolution_convert_fusion.6, bf16[2048,704]{0,1:T(8,128)(2,1)} %fusion.11, bf16[2048,704]{0,1:T(8,128)(2,1)S(1)} %copy-done.29, bf16[2048,704]{0,1:T(8,128)(2,1)S(1)} %copy-done.30), kind=kLoop, calls=%fused_computation.3 | loop fusion | flops 42991616 | bytes 21495808 | tf_op jit(solution)/shard_map/concatenate | solution.py:1068
  669.5 5.8 fusion.2
  675.6 85.0 %reduce-scatter.5.cloned.1.call-done = bf16[256,2624]{0,1:T(8,128)(2,1)} async-done(((bf16[2048,2624]{0,1:T(8,128)(2,1)}), bf16[256,2624]{0,1:T(8,128)(2,1)}) %reduce-scatter.5.cloned.1.call-update) | async-done | bytes 1343504 | tf_op jit(solution)/shard_map/reduce_scatter | solution.py:1069
  778.0 6.6 copy.242
  791.0 6.4 copy.243
  797.3 3.7 convolution_convert_fusion.11
  828.1 20.0 %group_scatter.2 = (bf16[256,576]{1,0:T(8,128)(2,1)S(1)}, bf16[256,576]{1,0:T(8,128)(2,1)S(1)}) custom-call(bf16[2,2,256,576]{3,2,1,0:T(8,128)(2,1)S(1)} %bitcast.356, bf16[2,2,256,576]{3,2,1,0:T(8,128)(2,1)S(1)} %bitcast.357), custom_call_target="tpu_custom_call" | custom-call | bytes 47185920 | tf_op jit(solution)/shard_map/group_scatter/pallas_call | solution.py:319
  859.9 5.2 concatenate.111.v_ref
  866.9 49.1 %push_scatter.3 = f32[2,64,2688]{2,1,0:T(8,128)S(1)} custom-call(bf16[2,4,64,2688]{3,2,1,0:T(8,128)(2,1)S(1)} %copy-done.1), custom_call_target="tpu_custom_call" | custom-call | bytes 220200960 | tf_op jit(solution)/shard_map/push_scatter/pallas_call | solution.py:205
  921.1 63.0 %push_gather.7 = bf16[2,4,64,2624]{3,2,1,0:T(8,128)(2,1)} custom-call(bf16[2,64,2624]{2,1,0:T(8,128)(2,1)} %bitcast.391), custom_call_target="tpu_custom_call" | custom-call | bytes 214958080 | tf_op jit(solution)/shard_map/push_gather/pallas_call | solution.py:150
  989.5 3.6 convolution_convert_fusion.1
  995.5 34.9 %group_scatter.3 = (bf16[256,768]{1,0:T(8,128)(2,1)S(1)}, bf16[64,1024]{1,0:T(8,128)(2,1)S(1)}, bf16[64,576]{1,0:T(8,128)(2,1)S(1)}, bf16[16,64]{1,0:T(8,128)(2,1)S(1)}) custom-call(bf16[4,2,256,768]{3,2,1,0:T(8,128)(2,1)S(1)} %bitcast.358, bf16[4,2,64,1024]{3,2,1,0:T(8,128)(2,1)S(1)} %bitcast.361, bf16[4,2,64,576]{3,2,1,0:T(8,128)(2,1)S(1)} %bitcast.359, ...), custom_call_target="tpu_custom_call" | custom-call | bytes 96010240 | tf_op jit(solution)/shard_map/group_scatter/pallas_call | solution.py:319
  1032.4 24.1 %push_gather.9 = bf16[1,4,80,576]{3,2,1,0:T(8,128)(2,1)} custom-call(bf16[1,80,576]{2,1,0:T(8,128)(2,1)} %fusion.76.v_ref), custom_call_target="tpu_custom_call" | custom-call | bytes 29491200 | tf_op jit(solution)/shard_map/push_gather/pallas_call | solution.py:150
  1056.5 45.9 %group_gather.3 = (bf16[4,2,256,768]{3,2,1,0:T(8,128)(2,1)}, bf16[4,2,64,1024]{3,2,1,0:T(8,128)(2,1)}, bf16[4,2,320,576]{3,2,1,0:T(8,128)(2,1)}) custom-call(bf16[256,768]{1,0:T(8,128)(2,1)} %copy-done.4, bf16[64,1024]{1,0:T(8,128)(2,1)} %copy-done.5, bf16[320,576]{1,0:T(8,128)(2,1)} %bitcast.404), custom_call_target="tpu_custom_call" | custom-call | bytes 142868480 | tf_op jit(solution)/shard_map/group_gather/pallas_call | solution.py:397
  1109.6 5.7 copy.240
  1118.1 19.7 %push_gather.8 = f32[1,32,36,128]{3,2,1,0:T(8,128)} custom-call(f32[1,36,128]{2,1,0:T(8,128)} %maximum_bitcast_fusion.v_ref), custom_call_target="tpu_custom_call" | custom-call | bytes 47185920 | tf_op jit(solution)/shard_map/push_gather/pallas_call | solution.py:150
  1137.9 6.0 slice.278
  1150.2 4.9 add_convert_fusion
  1155.1 12.4 %convert_element_type.261 = f32[2048,2624]{0,1:T(8,128)} convert(bf16[2048,2624]{0,1:T(8,128)(2,1)} %all-gather.8.cloned.1.call-done) | non-fusion elementwise | flops 5373952 | bytes 32243712 | tf_op jit(solution)/shard_map/convert_element_type | solution.py:1179
  1167.5 6.2 slice_bitcast_fusion
  1173.6 4.8 slice_bitcast_fusion.1
  1178.5 6.0 fusion.89
  (357 shorter events, 173.1 us)
Async XLA Ops:
  7.2 75.4 %copy-start = (bf16[512,1024]{1,0:T(8,128)(2,1)S(1)}, bf16[512,1024]{1,0:T(8,128)(2,1)}, u32[]{:S(2)}) copy-start(bf16[512,1024]{1,0:T(8,128)(2,1)} %param.25) | copy-start | bytes 3145732
  7.2 35.4 %copy-start.80 = (bf16[2048]{0:T(1024)(128)(2,1)S(1)}, bf16[2048]{0:T(1024)(128)(2,1)}, u32[]{:S(2)}) copy-start(bf16[2048]{0:T(1024)(128)(2,1)} %param.21) | copy-start | bytes 12292
  7.2 35.4 %copy-start.10 = (bf16[2,256,2048]{2,1,0:T(8,128)(2,1)S(1)}, bf16[2,256,2048]{2,1,0:T(8,128)(2,1)}, u32[]{:S(2)}) copy-start(bf16[2,256,2048]{2,1,0:T(8,128)(2,1)} %param.18) | copy-start | bytes 6291460
  7.2 33.6 %all-gather.10.cloned.1.call-start = ((), (), s32[]{:S(2)}) async-start(), calls=%async_computation.6 | async-start | bytes 1310720 | tf_op jit(solution)/shard_map/all_gather | solution.py:973
  9.1 34.1 %copy-start.84 = (bf16[512]{0:T(512)(128)(2,1)S(1)}, bf16[512]{0:T(512)(128)(2,1)}, u32[]{:S(2)}) copy-start(bf16[512]{0:T(512)(128)(2,1)} %param.24) | copy-start | bytes 3076
  9.1 218.8 %all-gather.12.cloned.1.call-start = ((), (), s32[]{:S(2)}) async-start(), calls=%async_computation.7 | async-start | bytes 9437184 | tf_op jit(solution)/shard_map/all_gather | solution.py:974
  40.9 208.8 %all-gather.14.cloned.1.call-start = ((), (), s32[]{:S(2)}) async-start(), calls=%async_computation.8 | async-start | bytes 18874368 | tf_op jit(solution)/shard_map/all_gather | solution.py:976
  41.6 627.8 %reduce-scatter.3.cloned.1.call-start = ((), (), s32[]{:S(2)}) async-start(), calls=%async_computation.2 | async-start | bytes 18874368 | tf_op jit(solution)/shard_map/reduce_scatter | solution.py:1057
  42.7 66.3 %copy-start.62 = (f32[2048]{0:T(1024)}, f32[2048]{0:T(1024)S(1)}, u32[]{:S(2)}) copy-start(f32[2048]{0:T(1024)S(1)} %convert_element_type.208) | copy-start | bytes 24580
  43.2 65.8 %copy-start.71 = (f32[2,256]{1,0:T(2,128)}, f32[2,256]{1,0:T(2,128)S(1)}, u32[]{:S(2)}) copy-start(f32[2,256]{1,0:T(2,128)S(1)} %get-tuple-element.182) | copy-start | bytes 6148
  46.6 32.4 %copy-start.68 = (f32[512]{0:T(512)}, f32[512]{0:T(512)S(1)}, u32[]{:S(2)}) copy-start(f32[512]{0:T(512)S(1)} %add_rsqrt_fusion.1) | copy-start | bytes 6148
  102.4 6.5 copy-start.70
  130.6 20.2 %copy-start.47 = (bf16[256,512]{1,0:T(8,128)(2,1)}, bf16[256,512]{1,0:T(8,128)(2,1)S(1)}, u32[]{:S(2)}) copy-start(bf16[256,512]{1,0:T(8,128)(2,1)S(1)} %copy.256) | copy-start | bytes 786436
  149.0 42.3 %copy-start.81 = (bf16[2048]{0:T(1024)(128)(2,1)S(1)}, bf16[2048]{0:T(1024)(128)(2,1)}, u32[]{:S(2)}) copy-start(bf16[2048]{0:T(1024)(128)(2,1)} %param.27) | copy-start | bytes 12292
  149.0 42.3 %copy-start.73 = (s32[2,256,6]{1,0,2:T(2,128)S(1)}, s32[2,256,6]{1,0,2:T(2,128)}, u32[]{:S(2)}) copy-start(s32[2,256,6]{1,0,2:T(2,128)} %param.20) | copy-start | bytes 36868
  191.3 52.3 %copy-start.60 = (f32[2048]{0:T(1024)}, f32[2048]{0:T(1024)S(1)}, u32[]{:S(2)}) copy-start(f32[2048]{0:T(1024)S(1)} %convert_element_type.223) | copy-start | bytes 24580
  195.8 5.1 copy-start.65
  227.9 8.5 copy-start.34
  506.6 253.9 %reduce-scatter.5.cloned.1.call-start = ((), (), s32[]{:S(2)}) async-start(), calls=%async_computation.4 | async-start | bytes 12091392 | tf_op jit(solution)/shard_map/reduce_scatter | solution.py:1069
  516.5 6.5 copy-start.93
  519.8 6.5 copy-start.28
  523.1 7.5 slice-start.3
  523.1 7.5 slice-start.4
  542.1 47.2 %copy-start.61 = (f32[2048]{0:T(1024)S(1)}, f32[2048]{0:T(1024)}, u32[]{:S(2)}) copy-start(f32[2048]{0:T(1024)} %copy-done.60) | copy-start | bytes 24580
  590.9 49.9 %copy-start.48 = (bf16[256,512]{1,0:T(8,128)(2,1)S(1)}, bf16[256,512]{1,0:T(8,128)(2,1)}, u32[]{:S(2)}) copy-start(bf16[256,512]{1,0:T(8,128)(2,1)} %copy-done.47) | copy-start | bytes 786436
  669.4 480.8 %all-reduce.4.cloned.1.call-start = ((), (), s32[]{:S(2)}) async-start(), calls=%async_computation.3 | async-start | bytes 4194304 | tf_op jit(solution)/shard_map/psum | solution.py:1058
  669.4 6.0 copy-start.69
  669.5 6.0 copy-start.72
  669.5 6.0 copy-start.75
  669.5 6.0 copy-start.83
  675.3 479.8 %all-gather.8.cloned.1.call-start = ((), (), s32[]{:S(2)}) async-start(), calls=%async_computation.5 | async-start | bytes 12091392 | tf_op jit(solution)/shard_map/all_gather | solution.py:1070
  803.5 7.3 copy-start.6
  804.8 7.8 copy-start.35
  828.1 22.6 %copy-start.7 = (bf16[4,256,1024]{2,1,0:T(8,128)(2,1)S(1)}, bf16[4,256,1024]{2,1,0:T(8,128)(2,1)}, u32[]{:S(2)}) copy-start(bf16[4,256,1024]{2,1,0:T(8,128)(2,1)} %copy-done.6) | copy-start | bytes 6291460
  854.3 5.6 copy-start.51
  866.9 49.3 %copy-start.64 = (f32[64,32]{1,0:T(8,128)S(1)}, f32[64,32]{1,0:T(8,128)}, u32[]{:S(2)}) copy-start(f32[64,32]{1,0:T(8,128)} %get-tuple-element.177) | copy-start | bytes 24580
  866.9 49.4 %copy-start.67 = (f32[512]{0:T(512)S(1)}, f32[512]{0:T(512)}, u32[]{:S(2)}) copy-start(f32[512]{0:T(512)} %copy-done.66) | copy-start | bytes 6148
  866.9 49.5 %copy-start.85 = (f32[128]{0:T(128)S(1)}, f32[128]{0:T(128)}, u32[]{:S(2)}) copy-start(f32[128]{0:T(128)} %mul.528) | copy-start | bytes 1540
  866.9 49.7 %copy-start.13 = (f32[2,64,2048]{2,1,0:T(8,128)S(1)}, f32[2,64,2048]{2,1,0:T(8,128)}, u32[]{:S(2)}) copy-start(f32[2,64,2048]{2,1,0:T(8,128)} %constant_dynamic-slice_fusion) | copy-start | bytes 3145732
  866.9 49.7 %copy-start.33 = (bf16[2048,576]{0,1:T(8,128)(2,1)S(1)}, bf16[2048,576]{0,1:T(8,128)(2,1)}, u32[]{:S(2)}) copy-start(bf16[2048,576]{0,1:T(8,128)(2,1)} %param.23) | copy-start | bytes 7077892
  866.9 49.7 %copy-start.63 = (f32[2048]{0:T(1024)S(1)}, f32[2048]{0:T(1024)}, u32[]{:S(2)}) copy-start(f32[2048]{0:T(1024)} %copy-done.62) | copy-start | bytes 24580
  984.1 5.3 copy-start.52
  984.1 5.3 copy-start.54
  1137.9 6.0 copy-start.31
  1137.9 7.3 copy-start.44
  1167.5 11.0 slice-start
  1167.5 11.0 slice-start.1
  1173.6 4.9 slice-start.2
  (58 other events, 136.2 us)
Sparse Core Ops, SparseCore 0:
  10.2 30.6 all-gather.9
  42.7 64.9 all-gather.11
  109.6 89.8 all-gather.13
  506.7 125.7 reduce-scatter.2
  669.5 91.0 reduce-scatter.4
  763.5 86.6 all-reduce.3
  852.1 65.1 all-gather.7

commit v2 on v1

v2 whole, which is shorter than its diff:
```python
import functools

import jax
import jax.numpy as jnp
from jax import lax
from jax.experimental import pallas as pl
from jax.experimental.pallas import tpu as pltpu
from jax.sharding import PartitionSpec as P

D = 2048
NOPE = 128
ROPE = 64
VDIM = 128
LATENT = 512
TOP = 6
EXP_DEV = 2
LANES = 128
GROUP = ("dp", "context")
EVERY = ("dp", "context", "tensor")
BF16 = jnp.bfloat16
F32 = jnp.float32
MESH = pl.DeviceIdType.MESH
MIB = 1024 * 1024

EPS = 1e-06


def rms_scale(rows):
    return lax.rsqrt(jnp.mean(rows * rows, axis=-1, keepdims=True) + EPS)


def norm_back(grad_out, normed, inverse):
    return inverse * (grad_out - normed * jnp.mean(grad_out * normed, axis=-1, keepdims=True))


def angles(positions, rope_dim):
    frequency = 10000.0 ** (-(jnp.arange(rope_dim // 2).astype(jnp.float32) * 2.0) / rope_dim)
    turned = positions[:, None] * frequency[None, :]
    return (jnp.cos(turned), jnp.sin(turned))


def rotate(vectors, cosine, sine):
    half_dim = vectors.shape[-1] // 2
    front_part = vectors[..., :half_dim]
    back_part = vectors[..., half_dim:]
    return jnp.concatenate(
        [front_part * cosine - back_part * sine, front_part * sine + back_part * cosine], axis=-1
    )


def unrotate(vectors, cosine, sine):
    half_dim = vectors.shape[-1] // 2
    front_part = vectors[..., :half_dim]
    back_part = vectors[..., half_dim:]
    return jnp.concatenate(
        [front_part * cosine + back_part * sine, back_part * cosine - front_part * sine], axis=-1
    )


def mm(left, right):
    return jnp.dot(left, right, preferred_element_type=F32)


def mm_nt(left, right):
    return lax.dot_general(left, right, (((1,), (1,)), ((), ())), preferred_element_type=F32)


def mm_tn(left, right):
    return lax.dot_general(left, right, (((0,), (0,)), ((), ())), preferred_element_type=F32)


def ring(axes, sizes):
    place = 0
    total = 1
    for axis, size in zip(axes, sizes):
        place = place * size + lax.axis_index(axis)
        total *= size

    def coordinates(index):
        found = {}
        for axis, size in reversed(list(zip(axes, sizes))):
            found[axis] = lax.rem(index, size)
            index = lax.div(index, size)
        return found

    return place, total, coordinates


def meet(devices):
    barrier = pltpu.get_barrier_semaphore()
    for device in devices:
        pl.semaphore_signal(barrier, inc=1, device_id=device, device_id_type=MESH)
    pl.semaphore_wait(barrier, len(devices))


def flip(index, mask, bits):
    total = 0
    for bit in range(bits):
        weight = 1 << bit
        ours = lax.rem(lax.div(index, weight), 2)
        theirs = lax.rem(lax.div(mask, weight), 2)
        total = total + lax.rem(ours + theirs, 2) * weight
    return total


def group_layout(axes, sizes):
    place, _, coordinates = ring(axes, sizes)
    return lax.div(place, 2), lax.rem(place, 2), lambda chip, core: coordinates(chip * 2 + core)


def group_sizes(axes):
    sizes = tuple(lax.axis_size(axis) for axis in axes)
    pairs = 1
    for size in sizes:
        pairs *= size
    return sizes, pairs // 2


def add_rows(out, terms, rows):
    def add(index, carry):
        at = pl.ds(pl.multiple_of(index * 16, 16), 16)
        value = terms[0](at).astype(F32)
        for term in terms[1:]:
            value = value + term(at).astype(F32)
        out(at, value)
        return carry

    lax.fori_loop(0, rows // 16, add, 0)


class LineGather:
    def __init__(self, v, axis):
        self.axis, self.size = axis, lax.axis_size(axis)
        dma = pltpu.SemaphoreType.DMA
        self.inputs = [(v, pltpu.VMEM)]
        shape = (v.shape[0], self.size) + v.shape[1:]
        self.outputs = [(jax.ShapeDtypeStruct(shape, v.dtype), pl.ANY)]
        self.scratch = [dma((2, self.size)), dma((2, self.size)), dma]

    def greets(self):
        index = lax.axis_index(self.axis)
        return [
            {self.axis: lax.rem(index + step, self.size)} for step in (1, self.size - 1)
        ]

    def run(self, v_ref, out_ref, send_sem, recv_sem, own_sem):
        index, size = lax.axis_index(self.axis), self.size

        def copy(way, hop, first):
            step = 1 - 2 * way
            source = lax.rem(index - step * (hop - 1) + size, size)
            return pltpu.make_async_remote_copy(
                src_ref=v_ref if first else out_ref.at[:, source],
                dst_ref=out_ref.at[:, source],
                send_sem=send_sem.at[way, hop],
                recv_sem=recv_sem.at[way, hop],
                device_id={self.axis: lax.rem(index + step + size, size)},
                device_id_type=MESH,
            )

        def arrival(way, hop):
            step = 1 - 2 * way
            source = lax.rem(index - step * hop + size, size)
            return pltpu.make_async_remote_copy(
                src_ref=v_ref,
                dst_ref=out_ref.at[:, source],
                send_sem=send_sem.at[way, hop],
                recv_sem=recv_sem.at[way, hop],
                device_id={self.axis: lax.rem(index + step + size, size)},
                device_id_type=MESH,
            )

        def sends(way, hop):
            if way == 0:
                return (index + 1 < size) & (index - hop + 1 >= 0)
            return (index - 1 >= 0) & (index + hop - 1 < size)

        def receives(way, hop):
            return index - hop >= 0 if way == 0 else index + hop < size

        for way in range(2):

            @pl.when(sends(way, 1))
            def _():
                copy(way, 1, True).start()

        own = pltpu.make_async_copy(v_ref, out_ref.at[:, index], own_sem)
        own.start()
        yield
        for hop in range(1, size):
            for way in range(2):

                @pl.when(receives(way, hop))
                def _():
                    arrival(way, hop).wait_recv()

                if hop + 1 < size:

                    @pl.when(sends(way, hop + 1))
                    def _():
                        copy(way, hop + 1, False).start()

            yield
        own.wait()
        for hop in range(1, size):
            for way in range(2):

                @pl.when(sends(way, hop))
                def _():
                    copy(way, hop, hop == 1).wait_send()


class LineScatter:
    def __init__(self, v, axis):
        self.axis, self.size = axis, lax.axis_size(axis)
        lead, total, rows, width = v.shape
        self.lead, self.rows = lead, rows
        if not isinstance(v, jax.ShapeDtypeStruct):
            v = v.reshape(lead, total * rows, width)
        dma = pltpu.SemaphoreType.DMA
        self.inputs = [(v, pltpu.VMEM)]
        self.outputs = [(jax.ShapeDtypeStruct((lead, rows, width), F32), pltpu.VMEM)]
        self.scratch = [
            pltpu.VMEM((2, total, lead, rows, width), v.dtype),
            dma((2, total)),
            dma((2, total)),
        ]

    greets = LineGather.greets

    def run(self, v_ref, out_ref, held, send_sem, recv_sem):
        index, size, rows = lax.axis_index(self.axis), self.size, self.rows

        def block(target):
            return pl.ds(pl.multiple_of(target * rows, rows), rows)

        def ours(lead, target):
            return lambda at: v_ref[
                lead, pl.ds(pl.multiple_of(target * rows + at.start, 16), 16), :
            ]

        def copy(way, target, first):
            step = 1 - 2 * way
            return pltpu.make_async_remote_copy(
                src_ref=v_ref.at[:, block(target)] if first else held.at[way, target],
                dst_ref=held.at[way, target],
                send_sem=send_sem.at[way, target],
                recv_sem=recv_sem.at[way, target],
                device_id={self.axis: lax.rem(index + step + size, size)},
                device_id_type=MESH,
            )

        def start(way):
            return index == 0 if way == 0 else index == size - 1

        def between(way, target):
            return (index > 0) & (index < target) if way == 0 else (index < size - 1) & (index > target)

        def targets(way):
            return range(size - 1, 0, -1) if way == 0 else range(size - 1)

        for way in range(2):

            @pl.when(start(way))
            def _():
                copy(way, targets(way)[0], True).start()

        yield
        def hand_on(way, position):
            target = targets(way)[position]
            if position + 1 < size - 1:

                @pl.when(start(way))
                def _():
                    copy(way, target, True).wait_send()
                    copy(way, targets(way)[position + 1], True).start()

            @pl.when(between(way, target))
            def _():
                copy(way, target, False).wait_recv()
                for lead in range(self.lead):

                    def store(at, value):
                        held[way, target, lead, at, :] = value.astype(BF16)

                    add_rows(
                        store,
                        [
                            lambda at: held[way, target, lead, at, :],
                            ours(lead, target),
                        ],
                        self.rows,
                    )
                copy(way, target, False).start()

        for position in range(size - 1):
            @pl.when(index < size // 2)
            def _():
                hand_on(0, position)
                hand_on(1, position)

            @pl.when(index >= size // 2)
            def _():
                hand_on(1, position)
                hand_on(0, position)

            yield
        for way in range(2):

            @pl.when(jnp.logical_not(start(way)))
            def _():
                copy(way, index, False).wait_recv()

        for lead in range(self.lead):

            def store(at, value, lead=lead):
                out_ref[lead, at, :] = value

            own = [ours(lead, index)]
            right = [lambda at, lead=lead: held[0, index, lead, at, :]]
            left = [lambda at, lead=lead: held[1, index, lead, at, :]]

            @pl.when(index == 0)
            def _():
                add_rows(store, own + left, self.rows)

            @pl.when(index == size - 1)
            def _():
                add_rows(store, own + right, self.rows)

            @pl.when((index > 0) & (index < size - 1))
            def _():
                add_rows(store, own + right + left, self.rows)

        for way in range(2):

            @pl.when(start(way))
            def _():
                copy(way, targets(way)[size - 2], True).wait_send()

            for target in targets(way):

                @pl.when(between(way, target))
                def _():
                    copy(way, target, False).wait_send()


class GroupScatter:
    def __init__(self, v, axes):
        self.axes = axes
        self.sizes, self.pairs = group_sizes(axes)
        tail = v.shape[1:]
        self.across = self.pairs == 4 and tail[0] % 32 == 0
        v = v.reshape((self.pairs, 2) + tail)
        self.rows = tail[0]
        dma = pltpu.SemaphoreType.DMA
        self.inputs = [(v, pl.ANY)]
        self.outputs = [(jax.ShapeDtypeStruct(tail, BF16), pltpu.VMEM)]
        self.scratch = [pltpu.VMEM((self.pairs,) + tail, BF16)] * 4 + [
            pltpu.VMEM((2, tail[0] // 2 if self.across else 16) + tail[1:], BF16),
            dma,
            dma,
            dma,
            dma((self.pairs,)),
            dma((self.pairs,)),
            dma((2,)),
            dma((2,)),
        ]

    def greets(self):
        chip, core, device = group_layout(self.axes, self.sizes)
        bits = self.pairs.bit_length() - 1
        return [device(chip, 1 - core)] + [
            device(flip(chip, mask, bits), core) for mask in range(1, self.pairs)
        ]

    def run(
        self,
        v_ref,
        out_ref,
        mine,
        peer,
        summed,
        held,
        passed,
        load_sem,
        swap_send,
        swap_recv,
        sum_send,
        sum_recv,
        pass_send,
        pass_recv,
    ):
        pairs, rows = self.pairs, self.rows
        bits = pairs.bit_length() - 1
        chip, core, device = group_layout(self.axes, self.sizes)
        swap = pltpu.make_async_remote_copy(
            src_ref=v_ref.at[:, 1 - core],
            dst_ref=peer,
            send_sem=swap_send,
            recv_sem=swap_recv,
            device_id=device(chip, 1 - core),
            device_id_type=MESH,
        )
        swap.start()
        load = pltpu.make_async_copy(v_ref.at[:, core], mine, load_sem)
        load.start()
        yield

        def push(mask):
            return pltpu.make_async_remote_copy(
                src_ref=summed.at[mask],
                dst_ref=held.at[mask],
                send_sem=sum_send.at[mask],
                recv_sem=sum_recv.at[mask],
                device_id=device(flip(chip, mask, bits), core),
                device_id_type=MESH,
            )

        middle = rows // 2
        halves = (pl.ds(0, middle), pl.ds(middle, rows - middle))

        def pass_on(part):
            return pltpu.make_async_remote_copy(
                src_ref=summed.at[3, halves[part]],
                dst_ref=passed.at[part],
                send_sem=pass_send.at[part],
                recv_sem=pass_recv.at[part],
                device_id=device(flip(chip, part + 1, bits), core),
                device_id_type=MESH,
            )

        load.wait()
        swap.wait()
        for mask in range(pairs - 1, -1, -1):
            target = flip(chip, mask, bits)

            def store(at, value, mask=mask):
                summed[mask, at, :] = value.astype(BF16)

            add_rows(
                store,
                [
                    lambda at, target=target: mine[target, at, :],
                    lambda at, target=target: peer[target, at, :],
                ],
                rows,
            )
            if self.across and mask == 3:
                for part in range(2):
                    pass_on(part).start()
            if not self.across and mask:
                push(mask).start()
        yield
        direct = (1, 2) if self.across else range(1, pairs)
        if self.across:
            for part in range(2):
                pass_on(part).wait_recv()
                mask = 2 - part
                start = part * middle

                def store(at, value, mask=mask, start=start):
                    summed[mask, pl.ds(pl.multiple_of(start + at.start, 16), 16), :] = value.astype(
                        BF16
                    )

                add_rows(
                    store,
                    [
                        lambda at, mask=mask, start=start: summed[
                            mask, pl.ds(pl.multiple_of(start + at.start, 16), 16), :
                        ],
                        lambda at, part=part: passed[part, at, :],
                    ],
                    middle,
                )
                push(mask).start()
        yield
        for mask in direct:
            push(mask).wait_recv()

        def finish(at, value):
            out_ref[at, :] = value.astype(BF16)

        add_rows(
            finish,
            [lambda at: summed[0, at, :]]
            + [lambda at, mask=mask: held[mask, at, :] for mask in direct],
            rows,
        )
        yield
        for mask in direct:
            push(mask).wait_send()
        if self.across:
            for part in range(2):
                pass_on(part).wait_send()


class GroupGather:
    def __init__(self, v, axes):
        self.axes = axes
        self.sizes, self.pairs = group_sizes(axes)
        self.rows = v.shape[0]
        self.across = self.pairs == 4 and v.shape[0] % 32 == 0
        dma = pltpu.SemaphoreType.DMA
        self.inputs = [(v, pltpu.VMEM)]
        self.outputs = [(jax.ShapeDtypeStruct((self.pairs, 2) + v.shape, v.dtype), pl.ANY)]
        self.scratch = [dma] + [dma((self.pairs,))] * 4 + [dma((2,))] * 2

    greets = GroupScatter.greets

    def run(
        self,
        v_ref,
        out_ref,
        own_sem,
        push_send,
        push_recv,
        relay_send,
        relay_recv,
        pass_send,
        pass_recv,
    ):
        pairs, rows = self.pairs, self.rows
        bits = pairs.bit_length() - 1
        chip, core, device = group_layout(self.axes, self.sizes)
        middle = rows // 2
        halves = (pl.ds(0, middle), pl.ds(middle, rows - middle))

        def push(mask, source):
            return pltpu.make_async_remote_copy(
                src_ref=v_ref,
                dst_ref=out_ref.at[source, core],
                send_sem=push_send.at[mask],
                recv_sem=push_recv.at[mask],
                device_id=device(flip(chip, mask, bits), core),
                device_id_type=MESH,
            )

        def pass_on(mask, source, part):
            return pltpu.make_async_remote_copy(
                src_ref=out_ref.at[source, core, halves[part]],
                dst_ref=out_ref.at[source, core, halves[part]],
                send_sem=pass_send.at[part],
                recv_sem=pass_recv.at[part],
                device_id=device(flip(chip, mask, bits), core),
                device_id_type=MESH,
            )

        def relay(mask, side):
            source = flip(chip, mask, bits)
            return pltpu.make_async_remote_copy(
                src_ref=v_ref if mask == 0 else out_ref.at[source, side],
                dst_ref=out_ref.at[source, side],
                send_sem=relay_send.at[mask],
                recv_sem=relay_recv.at[mask],
                device_id=device(chip, 1 - core),
                device_id_type=MESH,
            )

        direct = (1, 2) if self.across else tuple(range(1, pairs))
        for mask in direct:
            push(mask, chip).start()
        relay(0, core).start()
        own = pltpu.make_async_copy(v_ref, out_ref.at[chip, core], own_sem)
        own.start()
        yield
        for mask in direct:
            push(mask, flip(chip, mask, bits)).wait_recv()
            if self.across:
                pass_on(3 - mask, flip(chip, mask, bits), mask - 1).start()
            relay(mask, core).start()
        yield
        if self.across:
            for part in range(2):
                pass_on(part + 1, flip(chip, 3, bits), part).wait_recv()
            relay(3, core).start()
        own.wait()
        yield
        for mask in range(pairs):
            relay(mask, 1 - core).wait_recv()
        for mask in range(pairs):
            relay(mask, core).wait_send()
            if mask in direct:
                push(mask, chip).wait_send()
                if self.across:
                    pass_on(3 - mask, flip(chip, mask, bits), mask - 1).wait_send()


class ContextThenLine:
    def __init__(self, values, axes, axis):
        self.first = [GroupScatter(v, axes) for v in values]
        rows, width = values[0].shape[1:]
        total = lax.axis_size(axis)
        self.second = LineScatter(
            jax.ShapeDtypeStruct((len(values), total, rows // total, width), BF16), axis
        )
        self.inputs = [entry for job in self.first for entry in job.inputs]
        self.outputs = self.second.outputs
        self.scratch = [pltpu.VMEM((len(values), rows, width), BF16)]
        self.scratch += [entry for job in self.first for entry in job.scratch]
        self.scratch += self.second.scratch

    def greets(self):
        return [device for job in self.first + [self.second] for device in job.greets()]

    def run(self, *refs):
        refs = list(refs)
        count = len(self.first)
        inputs, out_ref, between, refs = refs[:count], refs[count], refs[count + 1], refs[count + 2 :]
        steps = []
        for number, job in enumerate(self.first):
            used = len(job.scratch)
            steps.append(job.run(inputs[number], between.at[number], *refs[:used]))
            refs = refs[used:]
        for _ in zip(*steps):
            yield
        for step in steps:
            for _ in step:
                pass
        yield from self.second.run(between, out_ref, *refs)


class GroupSum:
    def __init__(self, v, axes):
        self.first = GroupScatter(v, axes)
        self.second = GroupGather(jax.ShapeDtypeStruct(v.shape[1:], BF16), axes)
        self.inputs, self.outputs = self.first.inputs, self.second.outputs
        self.scratch = [pltpu.VMEM(v.shape[1:], BF16)] + self.first.scratch + self.second.scratch
        self.greets = self.first.greets

    def run(self, v_ref, out_ref, between, *refs):
        used = len(self.first.scratch)
        yield from self.first.run(v_ref, between, *refs[:used])
        yield from self.second.run(between, out_ref, *refs[used:])


def exchange_kernel(jobs, *refs):
    refs = list(refs)
    taken = [[], [], []]
    for number, part in enumerate(("inputs", "outputs", "scratch")):
        for job in jobs:
            count = len(getattr(job, part))
            taken[number].append(refs[:count])
            refs = refs[count:]
    meet([device for job in jobs for device in job.greets()])
    running = [
        job.run(*taken[0][at], *taken[1][at], *taken[2][at]) for at, job in enumerate(jobs)
    ]
    while running:
        left = []
        for step in running:
            try:
                next(step)
                left.append(step)
            except StopIteration:
                pass
        running = left


def exchange(jobs, collective_id, micros):
    inputs = [entry for job in jobs for entry in job.inputs]
    outputs = [entry for job in jobs for entry in job.outputs]
    return pl.pallas_call(
        functools.partial(exchange_kernel, jobs),
        out_shape=tuple(shape for shape, _ in outputs),
        in_specs=[pl.BlockSpec(memory_space=space) for _, space in inputs],
        out_specs=tuple(pl.BlockSpec(memory_space=space) for _, space in outputs),
        scratch_shapes=[entry for job in jobs for entry in job.scratch],
        compiler_params=pltpu.CompilerParams(
            collective_id=collective_id, has_side_effects=True, vmem_limit_bytes=56 * MIB
        ),
        cost_estimate=pl.CostEstimate(
            flops=0, bytes_accessed=3_600_000 * micros, transcendentals=0
        ),
        name="exchange_" + "_".join(type(job).__name__ for job in jobs[:3]),
    )(*[value for value, _ in inputs])


def turn(vectors, cosine, sine):
    half_dim = vectors.shape[-1] // 2
    swapped = jnp.concatenate([vectors[:, half_dim:], vectors[:, :half_dim]], axis=1)
    return vectors * cosine + swapped * sine


def head_scores(query, key_nope, key_rope, allowed):
    raw = mm_nt(query[:, :NOPE], key_nope) + mm_nt(query[:, NOPE:], key_rope)
    return jnp.where(allowed, raw * (NOPE + ROPE) ** (-0.5), -1e30)


def allowed_keys(row_ref, column_ref, row_place_ref, column_place_ref):
    return (row_ref[0] == column_ref[0]) & (column_place_ref[...] <= row_place_ref[...])


def attend_kernel(
    x_ref,
    kv_ref,
    row_ref,
    column_ref,
    row_place_ref,
    column_place_ref,
    cos_ref,
    sin_ref,
    query_w,
    up_w,
    out_w,
    part_ref,
    attended_ref,
    query_ref,
    expanded_ref,
    log_ref,
):
    heads = query_w.shape[1] // (NOPE + ROPE)
    allowed = allowed_keys(row_ref, column_ref, row_place_ref, column_place_ref)
    latent = kv_ref[0, :, :LATENT]
    key_rope = kv_ref[0, :, LATENT:]
    query = mm(x_ref[...], query_w[...])
    for head in range(heads):
        start = head * (NOPE + ROPE)
        rope = turn(query[:, start + NOPE : start + NOPE + ROPE], cos_ref[...], sin_ref[...])
        query_ref[0, head, :, :NOPE] = query[:, start : start + NOPE].astype(BF16)
        query_ref[0, head, :, NOPE:] = rope.astype(BF16)
        at = slice(head * (NOPE + VDIM), (head + 1) * (NOPE + VDIM))
        expanded_ref[0, :, at] = mm(latent, up_w[:, at]).astype(BF16)
        key_nope = expanded_ref[0, :, at.start : at.start + NOPE]
        values = expanded_ref[0, :, at.start + NOPE : at.stop]
        scores = head_scores(query_ref[0, head], key_nope, key_rope, allowed)
        top = jnp.max(scores, axis=-1, keepdims=True)
        weights = jnp.where(allowed, jnp.exp(scores - top), 0.0)
        total = jnp.sum(weights, axis=-1, keepdims=True)
        log_ref[0, head] = top + jnp.log(total)
        probs = (weights / total).astype(BF16)
        attended_ref[:, head * VDIM : (head + 1) * VDIM] = mm(probs, values).astype(BF16)
    part_ref[...] = mm(attended_ref[...], out_w[...]).astype(BF16)


def attend_back_kernel(
    grad_ref,
    attended_ref,
    x_ref,
    kv_ref,
    row_ref,
    column_ref,
    row_place_ref,
    column_place_ref,
    cos_ref,
    sin_ref,
    query_ref,
    expanded_ref,
    log_ref,
    query_w,
    up_w,
    out_w,
    kv_grad_ref,
    x_grad_ref,
    query_w_ref,
    up_w_ref,
    out_w_ref,
    query_grad,
    expanded_grad,
):
    heads = query_w.shape[1] // (NOPE + ROPE)
    scale = (NOPE + ROPE) ** (-0.5)
    allowed = allowed_keys(row_ref, column_ref, row_place_ref, column_place_ref)
    latent = kv_ref[0, :, :LATENT]
    key_rope = kv_ref[0, :, LATENT:]
    grad = grad_ref[...]
    attended_grad = mm_nt(grad, out_w[...]).astype(BF16)
    rope_grad = jnp.zeros((kv_ref.shape[1], ROPE), F32)
    for head in range(heads):
        first = head * (NOPE + VDIM)
        key_nope = expanded_ref[0, :, first : first + NOPE]
        values = expanded_ref[0, :, first + NOPE : first + NOPE + VDIM]
        query = query_ref[0, head]
        scores = head_scores(query, key_nope, key_rope, allowed)
        probs = jnp.where(allowed, jnp.exp(scores - log_ref[0, head]), 0.0)
        own_grad = attended_grad[:, head * VDIM : (head + 1) * VDIM]
        probs_grad = mm_nt(own_grad, values)
        moved = probs * (probs_grad - jnp.sum(probs * probs_grad, axis=-1, keepdims=True))
        moved = moved.astype(BF16)
        expanded_grad[:, first : first + NOPE] = (
            scale * mm_tn(moved, query[:, :NOPE])
        ).astype(BF16)
        expanded_grad[:, first + NOPE : first + NOPE + VDIM] = mm_tn(
            probs.astype(BF16), own_grad
        ).astype(BF16)
        rope_grad = rope_grad + mm_tn(moved, query[:, NOPE:])
        start = head * (NOPE + ROPE)
        query_grad[:, start : start + NOPE] = (scale * mm(moved, key_nope)).astype(BF16)
        query_grad[:, start + NOPE : start + NOPE + ROPE] = turn(
            scale * mm(moved, key_rope), cos_ref[...], -sin_ref[...]
        ).astype(BF16)
    kv_grad_ref[0, :, :LATENT] = mm_nt(expanded_grad[...], up_w[...]).astype(BF16)
    kv_grad_ref[0, :, LATENT:] = (scale * rope_grad).astype(BF16)
    x_grad_ref[...] = mm_nt(query_grad[...], query_w[...]).astype(BF16)
    pieces = (
        (query_w_ref, x_ref[...], query_grad[...]),
        (up_w_ref, latent, expanded_grad[...]),
        (out_w_ref, attended_ref[...], grad),
    )

    @pl.when(pl.program_id(0) == 0)
    def _():
        for target, left, right in pieces:
            target[...] = mm_tn(left, right)

    @pl.when(pl.program_id(0) > 0)
    def _():
        for target, left, right in pieces:
            target[...] += mm_tn(left, right)


def attention_specs(micro_count, rows, seq_len, heads):
    per_micro = lambda *shape: pl.BlockSpec((1,) + shape, lambda m: (m,) + (0,) * len(shape))
    rows_of = lambda width: pl.BlockSpec((rows, width), lambda m: (m, 0))
    whole = lambda *shape: pl.BlockSpec(
        shape, lambda m: (0,) * len(shape), pipeline_mode=pl.Buffered(1)
    )
    places = [
        per_micro(rows, 1),
        per_micro(1, seq_len),
        whole(rows, 1),
        whole(1, seq_len),
        whole(rows, ROPE),
        whole(rows, ROPE),
    ]
    weights = [
        whole(D, heads * (NOPE + ROPE)),
        whole(LATENT, heads * (NOPE + VDIM)),
        whole(heads * VDIM, D),
    ]
    kept = [
        rows_of(heads * VDIM),
        per_micro(heads, rows, NOPE + ROPE),
        per_micro(seq_len, heads * (NOPE + VDIM)),
        per_micro(heads, rows, 1),
    ]
    return per_micro, rows_of, whole, places, weights, kept


def attend(x_attn, kv_all, places, weights, micro_count, heads):
    rows, seq_len = x_attn.shape[0] // micro_count, kv_all.shape[1]
    per_micro, rows_of, _, place_specs, weight_specs, kept = attention_specs(
        micro_count, rows, seq_len, heads
    )
    total = micro_count * rows
    return pl.pallas_call(
        attend_kernel,
        grid=(micro_count,),
        in_specs=[rows_of(D), per_micro(seq_len, LATENT + ROPE)] + place_specs + weight_specs,
        out_specs=[rows_of(D)] + kept,
        out_shape=[
            jax.ShapeDtypeStruct((total, D), BF16),
            jax.ShapeDtypeStruct((total, heads * VDIM), BF16),
            jax.ShapeDtypeStruct((micro_count, heads, rows, NOPE + ROPE), BF16),
            jax.ShapeDtypeStruct((micro_count, seq_len, heads * (NOPE + VDIM)), BF16),
            jax.ShapeDtypeStruct((micro_count, heads, rows, 1), F32),
        ],
        compiler_params=pltpu.CompilerParams(vmem_limit_bytes=56 * MIB),
        cost_estimate=pl.CostEstimate(
            flops=9_000_000_000, bytes_accessed=60_000_000, transcendentals=0
        ),
        name="attend",
    )(x_attn, kv_all, *places, *weights)


def attend_back(grad, x_attn, kv_all, places, weights, kept, micro_count, heads):
    rows, seq_len = x_attn.shape[0] // micro_count, kv_all.shape[1]
    per_micro, rows_of, whole, place_specs, weight_specs, kept_specs = attention_specs(
        micro_count, rows, seq_len, heads
    )
    total = micro_count * rows
    return pl.pallas_call(
        attend_back_kernel,
        grid=(micro_count,),
        in_specs=[rows_of(D), kept_specs[0], rows_of(D), per_micro(seq_len, LATENT + ROPE)]
        + place_specs
        + kept_specs[1:]
        + weight_specs,
        out_specs=[per_micro(seq_len, LATENT + ROPE), rows_of(D)] + weight_specs,
        out_shape=[
            jax.ShapeDtypeStruct((micro_count, seq_len, LATENT + ROPE), BF16),
            jax.ShapeDtypeStruct((total, D), BF16),
            jax.ShapeDtypeStruct(weights[0].shape, F32),
            jax.ShapeDtypeStruct(weights[1].shape, F32),
            jax.ShapeDtypeStruct(weights[2].shape, F32),
        ],
        scratch_shapes=[
            pltpu.VMEM((rows, heads * (NOPE + ROPE)), BF16),
            pltpu.VMEM((seq_len, heads * (NOPE + VDIM)), BF16),
        ],
        compiler_params=pltpu.CompilerParams(vmem_limit_bytes=60 * MIB),
        cost_estimate=pl.CostEstimate(
            flops=20_000_000_000, bytes_accessed=100_000_000, transcendentals=0
        ),
        name="attend_back",
    )(grad, kept[0], x_attn, kv_all, *places, *kept[1:], *weights)


PEER_SLOTS = 4


def expert_kernel(
    pairs,
    context_size,
    fe,
    x_ref,
    cot_ref,
    gate_in,
    up_in,
    down_in,
    router_in,
    shared_gate_in,
    shared_up_in,
    shared_down_in,
    out_ref,
    part_ref,
    gate_out,
    up_out,
    down_out,
    router_out,
    shared_out,
    shared_part,
    shared_grads,
    x_all,
    gate_ref,
    up_ref,
    down_ref,
    x_tile,
    cot_tile,
    out_tile,
    grad_tile,
    peer_tile,
    grad_gate,
    grad_up,
    hidden_low,
    gate_acc,
    up_acc,
    down_acc,
    x_send,
    x_recv,
    relay_send,
    relay_recv,
    pass_send,
    pass_recv,
    x_load,
    cot_load,
    out_store,
    swap_send,
    swap_recv,
    sum_send,
    sum_recv,
    weight_load,
    grad_store,
    shared_store,
    acc_store,
    credit,
):
    micro_count, rows = x_ref.shape[0], x_ref.shape[1]
    units = gate_ref.shape[0]
    shared_units = shared_gate_in.shape[0]
    half = units // EXP_DEV
    experts = 2 * pairs * EXP_DEV
    bits = pairs.bit_length() - 1
    steps = micro_count * pairs
    across = pairs == 4
    place = lax.axis_index("dp") * context_size + lax.axis_index("context")
    core = lax.rem(place, 2)
    chip = lax.div(place, 2)

    def device(chip_index, core_index):
        index = chip_index * 2 + core_index
        return {"dp": lax.div(index, context_size), "context": lax.rem(index, context_size)}

    sibling = device(chip, 1 - core)
    meet([sibling] + [device(flip(chip, mask, bits), core) for mask in range(1, pairs)])

    def step_of(step):
        micro = lax.div(step, pairs)
        turn = lax.rem(step, pairs)
        backward = lax.rem(micro, 2)
        return micro, lax.rem(turn + backward, pairs)

    def push_x(micro, mask):
        return pltpu.make_async_remote_copy(
            src_ref=x_ref.at[micro],
            dst_ref=x_all.at[micro, chip, core],
            send_sem=x_send.at[micro, mask],
            recv_sem=x_recv.at[micro, mask],
            device_id=device(flip(chip, mask, bits), core),
            device_id_type=MESH,
        )

    def relay(micro, mask, own=False):
        source = flip(chip, mask, bits)
        return pltpu.make_async_remote_copy(
            src_ref=x_ref.at[micro] if own else x_all.at[micro, source, core],
            dst_ref=x_all.at[micro, source, core],
            send_sem=relay_send.at[micro, mask],
            recv_sem=relay_recv.at[micro, mask],
            device_id=sibling,
            device_id_type=MESH,
        )

    def relay_arrival(micro, mask):
        source = flip(chip, mask, bits)
        return pltpu.make_async_remote_copy(
            src_ref=x_all.at[micro, source, 1 - core],
            dst_ref=x_all.at[micro, source, 1 - core],
            send_sem=relay_send.at[micro, mask],
            recv_sem=relay_recv.at[micro, mask],
            device_id=sibling,
            device_id_type=MESH,
        )

    def x_arrival(micro, mask):
        return pltpu.make_async_remote_copy(
            src_ref=x_ref.at[micro],
            dst_ref=x_all.at[micro, flip(chip, mask, bits), core],
            send_sem=x_send.at[micro, mask],
            recv_sem=x_recv.at[micro, mask],
            device_id=device(flip(chip, mask, bits), core),
            device_id_type=MESH,
        )

    middle = rows // 2
    parts = (pl.ds(0, middle), pl.ds(middle, rows - middle))

    def pass_on(micro, mask, source, part):
        return pltpu.make_async_remote_copy(
            src_ref=x_all.at[micro, source, core, parts[part]],
            dst_ref=x_all.at[micro, source, core, parts[part]],
            send_sem=pass_send.at[micro, part],
            recv_sem=pass_recv.at[micro, part],
            device_id=device(flip(chip, mask, bits), core),
            device_id_type=MESH,
        )

    def half_tile(side):
        return pl.ds(pl.multiple_of(side * rows, rows), rows)

    def load_cot(step):
        micro, mask = step_of(step)
        slot = lax.rem(step, 2)
        source = flip(chip, mask, bits)
        return [
            pltpu.make_async_copy(
                cot_ref.at[2 * source + side, micro],
                cot_tile.at[slot, half_tile(side)],
                cot_load.at[slot, side],
            )
            for side in range(2)
        ]

    def load_own(step):
        slot = lax.rem(step, 2)
        return pltpu.make_async_copy(
            x_ref.at[step_of(step)[0]], x_tile.at[slot, half_tile(core)], x_load.at[slot, 0]
        )

    def load_x(step, number):
        micro, mask = step_of(step)
        slot = lax.rem(step, 2)
        side = core if number == 0 else 1 - core
        return pltpu.make_async_copy(
            x_all.at[micro, flip(chip, mask, bits), side],
            x_tile.at[slot, half_tile(side)],
            x_load.at[slot, number],
        )

    def store(step):
        micro, mask = step_of(step)
        return [
            pltpu.make_async_copy(
                out_tile.at[pl.ds(side * rows, rows)],
                out_ref.at[2 * flip(chip, mask, bits) + side, micro],
                out_store.at[side],
            )
            for side in range(2)
        ]

    def swap(step):
        slot = lax.rem(step, 2)
        held = lax.rem(step, PEER_SLOTS)
        return pltpu.make_async_remote_copy(
            src_ref=grad_tile.at[pl.ds(pl.multiple_of((1 - core) * rows, rows), rows)],
            dst_ref=peer_tile.at[held],
            send_sem=swap_send.at[slot],
            recv_sem=swap_recv.at[held],
            device_id=sibling,
            device_id_type=MESH,
        )

    def push_sum(step):
        micro, mask = step_of(step)
        slot = lax.rem(step, PEER_SLOTS)
        return pltpu.make_async_remote_copy(
            src_ref=peer_tile.at[slot],
            dst_ref=part_ref.at[micro, mask],
            send_sem=sum_send.at[slot],
            recv_sem=sum_recv.at[micro, mask],
            device_id=device(flip(chip, mask, bits), core),
            device_id_type=MESH,
        )

    def keep_sum(step):
        micro, mask = step_of(step)
        slot = lax.rem(step, PEER_SLOTS)
        return pltpu.make_async_copy(
            peer_tile.at[slot], part_ref.at[micro, mask], sum_send.at[slot]
        )

    def wait_sum_sent(step):
        mask = step_of(step)[1]

        @pl.when(mask > 0)
        def _():
            push_sum(step).wait_send()

        @pl.when(mask == 0)
        def _():
            keep_sum(step).wait()

    def fetch(step):
        micro, mask = step_of(step)

        if not across:

            @pl.when(mask > 0)
            def _():
                x_arrival(micro, mask).wait_recv()
                relay(micro, mask).start()

        else:

            @pl.when((mask == 1) | (mask == 2))
            def _():
                x_arrival(micro, mask).wait_recv()
                relay(micro, mask).start()

            for part in range(2):

                @pl.when(mask == part + 1)
                def _():
                    pass_on(micro, 2 - part, flip(chip, part + 1, bits), part).start()

            @pl.when(mask == 3)
            def _():
                for part in range(2):
                    pass_on(micro, part + 1, flip(chip, 3, bits), part).wait_recv()
                relay(micro, mask).start()

        for copy in load_cot(step):
            copy.start()

        @pl.when(mask == 0)
        def _():
            load_own(step).start()

        @pl.when(mask > 0)
        def _():
            load_x(step, 0).start()

    def fetch_relayed(step):
        micro, mask = step_of(step)
        relay_arrival(micro, mask).wait_recv()
        load_x(step, 1).start()

    def finish_sum(step):
        slot = lax.rem(step, 2)
        held = lax.rem(step, PEER_SLOTS)
        swap(step).wait()

        def add(index, carry):
            at = pl.ds(pl.multiple_of(index * 16, 16), 16)
            mine = pl.ds(pl.multiple_of(core * rows + index * 16, 16), 16)
            value = grad_tile[mine, :].astype(F32) + peer_tile[held, at, :].astype(F32)
            peer_tile[held, at, :] = value.astype(BF16)
            return carry

        lax.fori_loop(0, rows // 16, add, 0)

        mask = step_of(step)[1]

        @pl.when(mask > 0)
        def _():
            push_sum(step).start()

        @pl.when(mask == 0)
        def _():
            keep_sum(step).start()

    direct = (1, 2) if across else tuple(range(1, pairs))
    for mask in direct:
        push_x(0, mask).start()
    for micro in range(micro_count):
        relay(micro, 0, own=True).start()

    def weights_in(pieces):
        copies = []
        for number, (source, target, start) in enumerate(pieces):
            copies.append(
                pltpu.make_async_copy(
                    source, target.at[pl.ds(start, source.shape[0])], weight_load.at[number]
                )
            )
        return copies

    shared_weights = weights_in(
        [(shared_gate_in, gate_ref, 0), (shared_up_in, up_ref, 0), (shared_down_in, down_ref, 0)]
    )
    for copy in shared_weights:
        copy.start()
    shared_rows = []
    for micro in range(micro_count):
        at = pl.ds(micro * rows, rows)
        shared_rows.append(
            pltpu.make_async_copy(x_ref.at[micro], x_tile.at[1, at], x_load.at[1, micro])
        )
        shared_rows.append(
            pltpu.make_async_copy(cot_ref.at[place, micro], cot_tile.at[1, at], cot_load.at[1, micro])
        )
    for copy in shared_rows:
        copy.start()
    for target in (gate_ref, up_ref, down_ref):
        target[shared_units:, :] = jnp.zeros((units - shared_units, D), BF16)
    fetch(0)

    chunk = 256 if units % 256 == 0 else LANES
    out_chunk = 512
    slab = half - LANES
    first_lane = fe % LANES
    slab_chunk = slab // chunk * chunk

    def hidden_pass(x, cot, here, start, gate, scale):
        at = slice(start, start + chunk)
        up = mm_nt(x, up_ref[at, :])
        back = mm_nt(cot, down_ref[at, :])
        sig = jax.nn.sigmoid(gate)
        act = gate * sig
        hidden = act * up
        grad_hidden = back if scale is None else back * scale
        scaled = hidden if scale is None else hidden * scale
        hidden_low[here, at] = scaled.astype(BF16)
        grad_gate[here, at] = (grad_hidden * up * (sig * (1.0 + gate * (1.0 - sig)))).astype(BF16)
        grad_up[here, at] = (grad_hidden * act).astype(BF16)
        return hidden * back

    def grad_pass():
        for start in range(0, D, out_chunk):
            at = slice(start, start + out_chunk)
            grad = mm(grad_gate[...], gate_ref[:, at]) + mm(grad_up[...], up_ref[:, at])
            grad_tile[:, at] = grad.astype(BF16)

    def out_pass():
        for start in range(0, D, out_chunk):
            at = slice(start, start + out_chunk)
            out_tile[:, at] = mm(hidden_low[...], down_ref[:, at]).astype(BF16)

    for copy in shared_weights + shared_rows:
        copy.wait()
    row_halves = (slice(0, rows), slice(rows, 2 * rows))
    for here in row_halves:
        x, cot = x_tile[1, here, :D], cot_tile[1, here]
        for start in range(0, units, chunk):
            gate = mm_nt(x, gate_ref[start : start + chunk, :])
            hidden_pass(x, cot, here, start, gate, None)
    grad_pass()
    out_pass()
    expert_weights = weights_in(
        [
            piece
            for number in range(EXP_DEV)
            for piece in (
                (gate_in.at[number], gate_ref, number * half),
                (up_in.at[number], up_ref, number * half),
                (down_in.at[number], down_ref, number * half),
            )
        ]
        + [(router_in, gate_ref, fe)]
    )
    for copy in expert_weights:
        copy.start()
    for target in (gate_ref, up_ref, down_ref):
        for number in range(EXP_DEV):
            first = number * half + fe
            if target is gate_ref and number == 0:
                first += experts
            last = (number + 1) * half
            if last > first:
                target[first:last, :] = jnp.zeros((last - first, D), BF16)
    shared_stores = []
    for micro in range(micro_count):
        at = pl.ds(micro * rows, rows)
        shared_stores.append(
            pltpu.make_async_copy(out_tile.at[at], shared_out.at[micro], shared_store.at[micro, 0])
        )
        shared_stores.append(
            pltpu.make_async_copy(
                grad_tile.at[at], shared_part.at[micro], shared_store.at[micro, 1]
            )
        )
    for copy in shared_stores:
        copy.start()
    fetch_relayed(0)
    for copy in shared_stores:
        copy.wait()
    staged = []
    for which, (left, right) in enumerate(
        ((grad_gate, x_tile[1, :, :D]), (grad_up, x_tile[1, :, :D]), (hidden_low, cot_tile[1]))
    ):
        for start in range(0, units, rows):
            stage = len(staged) % 2 * rows
            if len(staged) >= 2:
                staged[-2].wait()
            out_tile[stage : stage + rows, :] = mm_tn(
                left[:, start : start + rows], right
            ).astype(BF16)
            copy = pltpu.make_async_copy(
                out_tile.at[pl.ds(stage, rows)],
                shared_grads.at[which, pl.ds(start, rows)],
                grad_store.at[len(staged) % 2],
            )
            copy.start()
            staged.append(copy)
    for acc in (gate_acc, up_acc, down_acc):
        acc[...] = jnp.zeros_like(acc)
    for copy in staged[-2:] + expert_weights:
        copy.wait()

    def work(step, carry):
        slot = lax.rem(step, 2)

        for copy in load_cot(step):
            copy.wait()
        for number in range(2):
            load_x(step, number).wait()

        for here in row_halves:
            x = x_tile[slot, here, :D]
            chosen = x_tile[slot, here, D:].astype(F32)
            cot = cot_tile[slot, here]
            lane = lax.broadcasted_iota(jnp.int32, (rows, LANES), 1) - first_lane
            valid = (lane >= 0) & (lane < experts)

            first_gate = mm_nt(x, gate_ref[slab_chunk : slab_chunk + chunk, :])
            slab_gate = first_gate[:, slab - slab_chunk : slab - slab_chunk + LANES]
            logits = jnp.where(valid, slab_gate, -1e30)
            weights = jnp.where(
                valid, jnp.exp(logits - jnp.max(logits, axis=-1, keepdims=True)), 0.0
            )
            router_probs = weights / jnp.sum(weights, axis=-1, keepdims=True)
            named = router_probs * chosen
            picks = [lane == place * EXP_DEV + number for number in range(EXP_DEV)]
            scales = [
                jnp.sum(jnp.where(pick, named, 0.0), axis=-1, keepdims=True) for pick in picks
            ]
            flags = [
                jnp.sum(jnp.where(pick, chosen, 0.0), axis=-1, keepdims=True) for pick in picks
            ]
            dots = [jnp.zeros((rows, 1), F32) for _ in picks]
            column = lax.broadcasted_iota(jnp.int32, (rows, chunk), 1)
            starts = [slab_chunk] + [at for at in range(0, units, chunk) if at != slab_chunk]
            for start in starts:
                if start == slab_chunk:
                    gate = first_gate
                else:
                    gate = mm_nt(x, gate_ref[start : start + chunk, :])
                first, last = start // half, (start + chunk - 1) // half
                scale = scales[first]
                if last > first:
                    scale = jnp.where(column < last * half - start, scales[first], scales[last])
                product = hidden_pass(x, cot, here, start, gate, scale)
                if last > first:
                    split = last * half - start
                    dots[first] = dots[first] + jnp.sum(product[:, :split], axis=-1, keepdims=True)
                    dots[last] = dots[last] + jnp.sum(product[:, split:], axis=-1, keepdims=True)
                else:
                    dots[first] = dots[first] + jnp.sum(product, axis=-1, keepdims=True)
            spread = jnp.zeros((rows, LANES), F32)
            for pick, dot, flag in zip(picks, dots, flags):
                spread = spread + jnp.where(pick, dot * flag, 0.0)
            grad_logits = router_probs * (
                spread - jnp.sum(router_probs * spread, axis=-1, keepdims=True)
            )
            grad_gate[here, slab:half] = jnp.where(
                lane < 0, grad_gate[here, slab:half].astype(F32), grad_logits
            ).astype(BF16)

        @pl.when(step + 1 < steps)
        def _():
            fetch(step + 1)

        @pl.when(step == 1)
        def _():
            for micro in range(1, micro_count):
                for mask in direct:
                    push_x(micro, mask).start()

        @pl.when(step >= 1)
        def _():
            finish_sum(step - 1)

        @pl.when(step >= PEER_SLOTS)
        def _():
            wait_sum_sent(step - PEER_SLOTS)
            pl.semaphore_signal(credit, inc=1, device_id=sibling, device_id_type=MESH)
            pl.semaphore_wait(credit, 1)

        grad_pass()
        swap(step).start()


        @pl.when(step >= 1)
        def _():
            for copy in store(step - 1):
                copy.wait()

        out_pass()
        for copy in store(step):
            copy.start()

        @pl.when(step + 1 < steps)
        def _():
            fetch_relayed(step + 1)

        for acc, left, right in (
            (gate_acc, grad_gate, x_tile),
            (up_acc, grad_up, x_tile),
            (down_acc, hidden_low, cot_tile),
        ):
            for start in range(0, D, out_chunk):
                at = slice(start, start + out_chunk)
                acc[:, at] += mm_tn(left[...], right[slot, :, at])
        return carry


    lax.fori_loop(0, steps, work, 0)
    finals = [
        pltpu.make_async_copy(
            gate_acc.at[pl.ds(fe, experts)], router_out, acc_store.at[EXP_DEV, 0]
        )
    ]
    for number in range(EXP_DEV):
        for which, (acc, target) in enumerate(
            ((gate_acc, gate_out), (up_acc, up_out), (down_acc, down_out))
        ):
            finals.append(
                pltpu.make_async_copy(
                    acc.at[pl.ds(number * half, fe)],
                    target.at[number],
                    acc_store.at[number, which],
                )
            )
    for copy in finals:
        copy.start()
    finish_sum(steps - 1)
    for back in range(PEER_SLOTS, 0, -1):
        wait_sum_sent(steps - back)
    for copy in finals:
        copy.wait()
    for copy in store(steps - 1):
        copy.wait()
    for micro in range(micro_count):
        if across:
            for part in range(2):
                pass_on(micro, 2 - part, flip(chip, part + 1, bits), part).wait_send()
        for mask in range(pairs):
            relay(micro, mask).wait_send()
            if mask in direct:
                push_x(micro, mask).wait_send()
            if mask:
                pltpu.make_async_remote_copy(
                    src_ref=peer_tile.at[0],
                    dst_ref=part_ref.at[micro, mask],
                    send_sem=sum_send.at[0],
                    recv_sem=sum_recv.at[micro, mask],
                    device_id=device(flip(chip, mask, bits), core),
                    device_id_type=MESH,
                ).wait_recv()


def expert_pass(
    x_ext, cot_all, gate_w, up_w, down_w, router_w, shared_gate, shared_up, shared_down, collective_id
):
    micro_count, rows, width = x_ext.shape
    context_size = lax.axis_size("context")
    pairs = lax.axis_size("dp") * context_size // 2
    fe, experts, shared_units = gate_w.shape[1], router_w.shape[0], shared_gate.shape[0]
    half = -(-(fe + experts) // LANES) * LANES
    units = EXP_DEV * half
    dma = pltpu.SemaphoreType.DMA
    wide = jax.ShapeDtypeStruct((EXP_DEV, fe, D), F32)
    own = jax.ShapeDtypeStruct((micro_count, rows, D), BF16)
    return pl.pallas_call(
        functools.partial(expert_kernel, pairs, context_size, fe),
        out_shape=(
            jax.ShapeDtypeStruct((2 * pairs, micro_count, rows, D), BF16),
            jax.ShapeDtypeStruct((micro_count, pairs, rows, D), BF16),
            wide,
            wide,
            wide,
            jax.ShapeDtypeStruct((experts, D), F32),
            own,
            own,
            jax.ShapeDtypeStruct((3, units, D), BF16),
            jax.ShapeDtypeStruct((micro_count, pairs, 2, rows, width), BF16),
        ),
        in_specs=[pl.BlockSpec(memory_space=pl.ANY)] * 9,
        out_specs=(pl.BlockSpec(memory_space=pl.ANY),) * 10,
        scratch_shapes=[
            pltpu.VMEM((units, D), BF16),
            pltpu.VMEM((units, D), BF16),
            pltpu.VMEM((units, D), BF16),
            pltpu.VMEM((2, 2 * rows, width), BF16),
            pltpu.VMEM((2, 2 * rows, D), BF16),
            pltpu.VMEM((2 * rows, D), BF16),
            pltpu.VMEM((2 * rows, D), BF16),
            pltpu.VMEM((PEER_SLOTS, rows, D), BF16),
            pltpu.VMEM((2 * rows, units), BF16),
            pltpu.VMEM((2 * rows, units), BF16),
            pltpu.VMEM((2 * rows, units), BF16),
            pltpu.VMEM((units, D), F32),
            pltpu.VMEM((units, D), F32),
            pltpu.VMEM((units, D), F32),
            dma((micro_count, pairs)),
            dma((micro_count, pairs)),
            dma((micro_count, pairs)),
            dma((micro_count, pairs)),
            dma((micro_count, 2)),
            dma((micro_count, 2)),
            dma((2, 2)),
            dma((2, 2)),
            dma((2,)),
            dma((2,)),
            dma((PEER_SLOTS,)),
            dma((PEER_SLOTS,)),
            dma((micro_count, pairs)),
            dma((3 * EXP_DEV + 1,)),
            dma((2,)),
            dma((micro_count, 2)),
            dma((EXP_DEV + 1, 3)),
            pltpu.SemaphoreType.REGULAR,
        ],
        compiler_params=pltpu.CompilerParams(
            collective_id=collective_id, has_side_effects=True, vmem_limit_bytes=62 * MIB
        ),
        cost_estimate=pl.CostEstimate(
            flops=36 * (pairs * micro_count + 1) * rows * D * units,
            bytes_accessed=500_000_000,
            transcendentals=0,
        ),
        name="expert_pass",
    )(x_ext, cot_all, gate_w, up_w, down_w, router_w, shared_gate, shared_up, shared_down)[:9]


def per_device(
    tokens,
    segments,
    expert_ids,
    norm_attn,
    w_query,
    w_kv_down,
    norm_latent,
    w_kv_up,
    w_out,
    norm_ffn,
    w_router,
    w_shared_gate,
    w_shared_up,
    w_shared_down,
    w_expert_gate,
    w_expert_up,
    w_expert_down,
    cotangent,
):
    micro_count, block_rows = tokens.shape[:2]
    rows = micro_count * block_rows
    seq_len = segments.shape[1]
    context_size = lax.axis_size("context")
    groups = lax.axis_size("dp") * context_size
    tensor_size = lax.axis_size("tensor")
    group_index = lax.axis_index("dp") * context_size + lax.axis_index("context")
    own_rows = block_rows // tensor_size
    own_start = lax.axis_index("tensor") * own_rows
    experts = EXP_DEV * groups
    heads_local = w_query.shape[1] // (NOPE + ROPE)
    fe_local = w_expert_gate.shape[2]
    start_row = lax.axis_index("context") * block_rows
    query_index = start_row + jnp.arange(block_rows)
    key_index = jnp.arange(seq_len)
    cos_block, sin_block = angles(query_index.astype(F32), ROPE)
    cos_query = jnp.tile(cos_block, (micro_count, 1))
    sin_query = jnp.tile(sin_block, (micro_count, 1))
    gain_attn = norm_attn.astype(F32)
    gain_latent = norm_latent.astype(F32)
    gain_ffn = norm_ffn.astype(F32)

    def own(values):
        values = values.reshape((micro_count, block_rows) + values.shape[1:])
        part = lax.dynamic_slice_in_dim(values, own_start, own_rows, axis=1)
        return part.reshape((micro_count * own_rows,) + values.shape[2:])

    def to_owner(values):
        values = values.astype(BF16).reshape(micro_count, tensor_size, own_rows, values.shape[-1])
        return LineScatter(values, "tensor")

    def from_owners(values):
        return LineGather(values.reshape(micro_count, own_rows, values.shape[-1]), "tensor")

    def flat(values):
        return values.reshape(-1, values.shape[-1])

    ff_local = w_shared_gate.shape[1]
    slots = jnp.arange(LANES) - fe_local % LANES
    named = jnp.any(expert_ids[..., None] == slots, axis=2).astype(BF16)

    x_rows = tokens.reshape(rows, D).astype(F32)
    cot_rows = cotangent.reshape(rows, D)
    inv_attn = rms_scale(x_rows)
    normed_attn = x_rows * inv_attn
    x_attn = (normed_attn * gain_attn).astype(BF16)
    kv_raw = mm(x_attn, w_kv_down)
    latent_raw = kv_raw[:, :LATENT]
    inv_latent = rms_scale(latent_raw)
    normed_latent = latent_raw * inv_latent
    latent = (normed_latent * gain_latent).astype(BF16)
    key_rope = rotate(kv_raw[:, LATENT:], cos_query, sin_query).astype(BF16)
    kv_own = jnp.concatenate([latent, key_rope], axis=1)
    kv_all = exchange(
        [GroupGather(part, ("context",)) for part in jnp.split(kv_own, micro_count)], 1, 20
    )
    kv_all = jnp.concatenate([flat(part) for part in kv_all], axis=0)
    kv_all, cot_late = lax.optimization_barrier((kv_all, cotangent))
    cot_all = lax.all_gather(cot_late, GROUP, axis=0)
    kv_all = kv_all.reshape(micro_count, seq_len, LATENT + ROPE)
    seg_query = lax.dynamic_slice_in_dim(segments, start_row, block_rows, axis=1)
    places = (
        seg_query[:, :, None],
        segments[:, None, :],
        query_index[:, None],
        key_index[None, :],
        jnp.tile(cos_block, (1, 2)),
        jnp.concatenate([-sin_block, sin_block], axis=1),
    )
    weights = (w_query, w_kv_up, w_out)
    attn_part, *kept = attend(x_attn, kv_all, places, weights, micro_count, heads_local)
    (attn_sum,) = exchange([to_owner(attn_part)], 2, 40)
    hidden_one = own(x_rows) + flat(attn_sum)
    inv_ffn = rms_scale(hidden_one)
    normed_ffn = hidden_one * inv_ffn
    x_ffn = (normed_ffn * gain_ffn).astype(BF16)
    (x_ffn,) = exchange([from_owners(x_ffn)], 3, 40)
    x_ffn = flat(x_ffn.reshape(rows, D))
    x_ext = jnp.concatenate([x_ffn.reshape(micro_count, block_rows, D), named], axis=-1)

    (
        out_part,
        grad_part,
        gate_grad,
        up_grad,
        down_grad,
        router_grad,
        shared_out,
        shared_part,
        shared_grads,
    ) = expert_pass(
        x_ext,
        cot_all,
        w_expert_gate.transpose(0, 2, 1),
        w_expert_up.transpose(0, 2, 1),
        w_expert_down,
        w_router.T,
        w_shared_gate.T,
        w_shared_up.T,
        w_shared_down,
        4,
    )
    grad_sum = jnp.sum(grad_part.astype(F32), axis=1) + shared_part.astype(F32)
    grad_sum = grad_sum.reshape(rows, D)
    shared_units = shared_grads.shape[1]
    shared_grads = shared_grads.reshape(groups, -1, D)
    shared_grads = lax.psum_scatter(shared_grads, GROUP, scatter_dimension=0, tiled=False)
    out_sum = lax.psum_scatter(out_part, GROUP, scatter_dimension=0, tiled=False)
    (grad_x_ffn,) = exchange([to_owner(grad_sum)], 5, 40)
    grad_x_ffn = flat(grad_x_ffn)

    norm_ffn_grad = jnp.sum(grad_x_ffn * normed_ffn, axis=0)
    grad_one = own(cot_rows).astype(F32) + norm_back(grad_x_ffn * gain_ffn, normed_ffn, inv_ffn)
    (grad_attn_low,) = exchange([from_owners(grad_one.astype(BF16))], 6, 40)
    grad_attn_low = grad_attn_low.reshape(rows, D)
    grad_kv_part, grad_x_heads, query_grad, kv_up_grad, out_grad = attend_back(
        grad_attn_low, x_attn, kv_all, places, weights, kept, micro_count, heads_local
    )
    grad_x_heads, shared_grads = lax.optimization_barrier((grad_x_heads, shared_grads))
    shared_grads = lax.all_gather(shared_grads, GROUP, axis=0, tiled=True)
    router_part = router_grad.T.astype(BF16).reshape(tensor_size, micro_count, own_rows, -1)
    router_part = router_part.transpose(1, 0, 2, 3).reshape(rows, -1)
    late, grad_kv, query_part, kv_up_part, out_grad = exchange(
        [
            to_owner(jnp.concatenate([grad_x_heads, router_part], axis=1)),
            ContextThenLine(
                [
                    grad_kv_part[m].reshape(context_size, block_rows, LATENT + ROPE)
                    for m in range(micro_count)
                ],
                ("context",),
                "tensor",
            ),
            GroupScatter(query_grad.astype(BF16).reshape(groups, D // groups, -1), GROUP),
            GroupScatter(kv_up_grad.astype(BF16).reshape(groups, LATENT // groups, -1), GROUP),
            GroupScatter(out_grad.astype(BF16).reshape(groups, -1, D), GROUP),
        ],
        8,
        50,
    )
    late = flat(late)
    late, out_sum = lax.optimization_barrier((late, out_sum))
    out_sum = out_sum.reshape(rows, D).astype(F32) + shared_out.reshape(rows, D).astype(F32)
    out_sum = out_sum.astype(BF16).reshape(micro_count, tensor_size, own_rows, D)
    out_sum = out_sum.transpose(1, 0, 2, 3)
    out_sum = lax.psum_scatter(out_sum, "tensor", scatter_dimension=0, tiled=False)
    grad_x_heads, router_own = late[:, :D], late[:, D:]
    grad_kv = flat(grad_kv)
    grad_latent, grad_rope_key = grad_kv[:, :LATENT], grad_kv[:, LATENT:]
    normed_latent_own = own(normed_latent)
    norm_latent_grad = jnp.sum(grad_latent * normed_latent_own, axis=0)
    grad_latent_raw = norm_back(grad_latent * gain_latent, normed_latent_own, own(inv_latent))
    grad_kv_raw = jnp.concatenate(
        [grad_latent_raw, unrotate(grad_rope_key, own(cos_query), own(sin_query))], axis=-1
    ).astype(BF16)
    grad_x_attn = grad_x_heads + mm_nt(grad_kv_raw, w_kv_down)
    normed_attn_own = own(normed_attn)
    norm_attn_grad = jnp.sum(grad_x_attn * normed_attn_own, axis=0)
    grad_input = grad_one + norm_back(grad_x_attn * gain_attn, normed_attn_own, own(inv_attn))
    finished, small, router_all, query_grad, kv_up_grad, out_grad = exchange(
        [
            from_owners(jnp.concatenate([grad_input.astype(BF16), grad_kv_raw], axis=1)),
            LineGather(
                jnp.concatenate([norm_attn_grad, norm_ffn_grad, norm_latent_grad]).reshape(
                    1, -1, LANES
                ),
                "tensor",
            ),
            LineGather(router_own.astype(BF16)[None], "tensor"),
            GroupGather(query_part, GROUP),
            GroupGather(kv_up_part, GROUP),
            GroupGather(out_grad, GROUP),
        ],
        9,
        60,
    )
    finished = finished.reshape(rows, -1)
    out_sum, finished = lax.optimization_barrier((out_sum, finished))
    output = (hidden_one + flat(out_sum).astype(F32)).astype(BF16)
    output = lax.all_gather(output, "tensor", axis=0)
    output = output.reshape(tensor_size, micro_count, own_rows, D).transpose(1, 0, 2, 3)
    grad_tokens, grad_kv_raw = finished[:, :D], finished[:, D:]
    kv_width = -(-grad_kv_raw.shape[1] // (16 * groups)) * 16 * groups
    grad_kv_raw = jnp.pad(grad_kv_raw, ((0, 0), (0, kv_width - grad_kv_raw.shape[1])))
    kv_down_grad = mm_tn(grad_kv_raw, x_attn).astype(BF16)
    small = jnp.sum(small, axis=(0, 1)).astype(BF16)
    kv_down_grad, router_grad, small = exchange(
        [
            GroupSum(part.reshape(groups, -1, part.shape[-1]), GROUP)
            for part in (
                kv_down_grad,
                router_all.reshape(groups * 16, -1),
                small.reshape(groups * 16, -1),
            )
        ],
        10,
        35,
    )
    kv_down_grad = kv_down_grad.reshape(-1, D)[: LATENT + ROPE].astype(F32).T
    router_grad = router_grad.reshape(D, experts).astype(F32)
    small = small.reshape(-1).astype(F32)
    return (
        output.reshape(tokens.shape),
        grad_tokens.reshape(tokens.shape),
        small[:D],
        flat(query_grad).reshape(D, -1).astype(F32),
        kv_down_grad,
        small[D + D :],
        kv_up_grad.reshape(LATENT, -1).astype(F32),
        out_grad.reshape(-1, D).astype(F32),
        small[D : D + D],
        router_grad,
        shared_grads[:ff_local].astype(F32).T,
        shared_grads[shared_units : shared_units + ff_local].astype(F32).T,
        shared_grads[2 * shared_units : 2 * shared_units + ff_local].astype(F32),
        gate_grad.transpose(0, 2, 1),
        up_grad.transpose(0, 2, 1),
        down_grad,
    )


def solution(mesh):
    return jax.shard_map(
        per_device,
        mesh=mesh,
        in_specs=(
            P("dp", "context", None),
            P("dp", None),
            P("dp", "context", None),
            P(),
            P(None, "tensor"),
            P(),
            P(),
            P(None, "tensor"),
            P("tensor", None),
            P(),
            P(),
            P(None, "tensor"),
            P(None, "tensor"),
            P("tensor", None),
            P(("dp", "context"), None, "tensor"),
            P(("dp", "context"), None, "tensor"),
            P(("dp", "context"), "tensor", None),
            P("dp", "context", None),
        ),
        out_specs=(
            P("dp", "context", None),
            P("dp", "context", None),
            P(),
            P(None, "tensor"),
            P(),
            P(),
            P(None, "tensor"),
            P("tensor", None),
            P(),
            P(),
            P(None, "tensor"),
            P(None, "tensor"),
            P("tensor", None),
            P(("dp", "context"), None, "tensor"),
            P(("dp", "context"), None, "tensor"),
            P(("dp", "context"), "tensor", None),
        ),
        check_vma=False,
    )
```

time: 1200 us -> 832 us (0.69)
  local copies, waits for them, and re-layouts: 176 us -> 45.9 us
  waiting for transfers between devices: 117 us -> 2.78 us
  matrix products: 111 us -> 7.72 us
  Pallas kernels: 678 us -> 662 us
    reduce_scatter x1 -> x2, waiting for transfers between devices: 85 us -> 0.01 us  [the longest x1 0.01 us: per_device(): lax.psum_scatter(shared_grads, GROUP, scatter_dimension=0, tiled=False)]
    pallas_call x1, Pallas kernels: 257 us -> 210 us  [expert_pass(): pl.pallas_call(functools.partial(expert_kernel, pairs, context_size, fe),...]
    unnamed x213 -> x100, local copies, waits for them, and re-layouts: 62.9 us -> 19.4 us
    pallas_call x11 -> x10, Pallas kernels: 421 us -> 452 us  [the longest x8 392 us: exchange(): pl.pallas_call(functools.partial(exchange_kernel, jobs), out_shape=tuple(...]
    all_gather x4 -> x3, waiting for transfers between devices: 31.7 us -> 1.47 us  [the longest x1 1.47 us: per_device(): output = lax.all_gather(output, 'tensor', axis=0)]
    concatenate x10 -> x3, other arithmetic: 35.1 us -> 7.35 us  [the longest x1 3.44 us: per_device(): kv_all = jnp.concatenate([flat(part) for part in kv_all], axis=0)]
    dot_general x16 -> x0, matrix products: 26.7 us -> none  [the longest x2 8.25 us: per_device(): jnp.einsum('hcl,lhd->chd', probs[m].astype(BF16), head_values, preferred_...]
    slice x8 -> x1, local copies, waits for them, and re-layouts: 26.4 us -> 1.71 us  [per_device(): grad_kv_part[m].reshape(context_size, block_rows, LATENT + ROPE)]
  transfers between devices with their start and end apart: 7 -> 6, of which waited for: 2 -> 1; matrix products, arithmetic and copies ran while one was open for 27% -> 13% of each run, Pallas kernels for 35% -> 52%
where the time goes in v2:
time: 832 us; the launch traced here: 821 us
  Pallas kernels  662 us (80%)
  other arithmetic  87 us (10%)
  local copies, waits for them, and re-layouts  45.9 us (6%)
  between operations  15.1 us (2%)
    pallas_call x8, Pallas kernels, exchange(): pl.pallas_call(functools.partial(exchange_kernel, jobs), out_shape=tuple(...  392 us
    pallas_call x1, Pallas kernels, expert_pass(): pl.pallas_call(functools.partial(expert_kernel, pairs, context_size, fe),...  210 us
    pallas_call x1, Pallas kernels, attend_back(): pl.pallas_call(attend_back_kernel, grid=(micro_count,), in_specs=[rows_of...  38.6 us
    pallas_call x1, Pallas kernels, attend(): pl.pallas_call(attend_kernel, grid=(micro_count,), in_specs=[rows_of(D),...  21.7 us
    unnamed x100, local copies, waits for them, and re-layouts  19.4 us
  transfers between devices with their start and end apart: 6, of which 1 were waited for; matrix products, arithmetic and copies ran while one was open for 13% of the time, Pallas kernels for 52%

profile of v2, /device:TPU:0, one launch (start us, length us, event | category | flops | bytes accessed | tf_op | source)
XLA Modules:
  0.0 820.9 jit_solution(11682768810271378225)
XLA Ops:
  8.1 2.1 multiply_reduce_fusion
  11.9 1.8 fusion.39
  16.9 21.4 %exchange_GroupGather_GroupGather.1 = (bf16[2,2,256,576]{3,2,1,0:T(8,128)(2,1)}, bf16[2,2,256,576]{3,2,1,0:T(8,128)(2,1)}) custom-call(bf16[256,576]{1,0:T(8,128)(2,1)} %get-tuple-element.217.refs_0_, bf16[256,576]{1,0:T(8,128)(2,1)} %get-tuple-element.216.refs_1_), custom_call_target="tpu_custom_call" | custom-call | bytes 72000000 | tf_op jit(solution)/shard_map/exchange_GroupGather_GroupGather/pallas_call | solution.py:664
  38.2 3.4 pad_maximum_fusion
  41.8 2.6 convert_element_type.182
  48.7 21.7 %attend.1 = (bf16[512,2048]{1,0:T(8,128)(2,1)}, bf16[512,512]{1,0:T(8,128)(2,1)}, bf16[2,4,256,192]{3,2,1,0:T(8,128)(2,1)}, bf16[2,1024,1024]{2,1,0:T(8,128)(2,1)}, f32[2,4,256,1]{3,2,1,0:T(8,128)}) custom-call(bf16[512,2048]{1,0:T(8,128)(2,1)} %copy-done.11, bf16[2,1024,576]{2,1,0:T(8,128)(2,1)} %bitcast.190, s32[2,256,1]{2,1,0:T(8,128)} %copy.100.row_ref, ...), custom_call_target="tpu_custom_call" | custom-call | flops 8999999488 | bytes 60000000 | tf_op jit(solution)/shard_map/attend/pallas_call | solution.py:847
  70.4 43.8 %exchange_LineScatter.2 = f32[2,64,2048]{2,1,0:T(8,128)} custom-call(bf16[2,256,2048]{2,1,0:T(8,128)(2,1)} %bitcast.196), custom_call_target="tpu_custom_call" | custom-call | bytes 144000000 | tf_op jit(solution)/shard_map/exchange_LineScatter/pallas_call | solution.py:664
  114.3 2.8 multiply_reduce_fusion.3
  119.0 38.9 %exchange_LineGather.2 = bf16[2,4,64,2048]{3,2,1,0:T(8,128)(2,1)} custom-call(bf16[2,64,2048]{2,1,0:T(8,128)(2,1)} %multiply_convert_fusion.refs_0_), custom_call_target="tpu_custom_call" | custom-call | bytes 144000000 | tf_op jit(solution)/shard_map/exchange_LineGather/pallas_call | solution.py:664
  159.0 3.2 pad_maximum_fusion.1.x_ref
  162.1 210.0 %expert_pass.1 = (bf16[8,2,256,2048]{3,2,1,0:T(8,128)(2,1)}, bf16[2,4,256,2048]{3,2,1,0:T(8,128)(2,1)}, f32[2,352,2048]{2,1,0:T(8,128)}, f32[2,352,2048]{2,1,0:T...) custom-call(bf16[2,256,2176]{2,1,0:T(8,128)(2,1)} %pad_maximum_fusio, ...), custom_call_target="tpu_custom_call" | custom-call | flops 130459631616 | bytes 500000000 | tf_op jit(solution)/shard_map/expert_pass/pallas_call | solution.py:1495
  372.9 6.7 convert_reduce_fusion
  379.7 2.0 add_convert_fusion.1.refs_0_
  381.7 41.5 %exchange_LineScatter.3 = f32[2,64,2048]{2,1,0:T(8,128)} custom-call(bf16[2,256,2048]{2,1,0:T(8,128)(2,1)} %add_convert_fusion.1.refs_0_), custom_call_target="tpu_custom_call" | custom-call | bytes 144000000 | tf_op jit(solution)/shard_map/exchange_LineScatter/pallas_call | solution.py:664
  423.3 2.3 multiply_reduce_fusion.1
  425.6 2.2 add_convert_fusion.3.refs_0_
  427.7 34.9 %exchange_LineGather.3 = bf16[2,4,64,2048]{3,2,1,0:T(8,128)(2,1)} custom-call(bf16[2,64,2048]{2,1,0:T(8,128)(2,1)} %add_convert_fusion.3.refs_0_), custom_call_target="tpu_custom_call" | custom-call | bytes 144000000 | tf_op jit(solution)/shard_map/exchange_LineGather/pallas_call | solution.py:664
  463.2 38.6 %attend_back.1 = (bf16[2,1024,576]{2,1,0:T(8,128)(2,1)}, bf16[512,2048]{1,0:T(8,128)(2,1)}, f32[2048,768]{1,0:T(8,128)}, f32[512,1024]{1,0:T(8,128)}, f32[512,2048]{1,0:T(8,128)}) custom-call(bf16[512,2048]{1,0:T(8,128)(2,1)} %bitcast.195, bf16[512,512]{1,0:T(8,128)(2,1)} %get-tuple-element.66.attended_ref, bf16[512,2048]{1,0:T(8,128)(2,1)} %copy-done.11, ...), custom_call_target="tpu_custom_call" | custom-call | flops 20000000000 | bytes 100000000 | tf_op jit(solution)/shard_map/attend_back/pallas_call | solution.py:873
  501.9 5.1 convert_element_type.201
  507.5 4.2 convert_element_type.203
  513.9 1.7 fusion.36
  515.6 3.1 pad_maximum_fusion.2.refs_0_
  518.8 97.7 %exchange_LineScatter_ContextThenLine_GroupScatter.1 = (f32[2,64,2112]{2,1,0:T(8,128)}, f32[2,64,576]{2,1,0:T(8,128)}, bf16[256,768]{1,0:T(8,128)(2,1)}, bf16[64,1024]{1,0:T(8,128)(2,1)}, bf16[64,2048]{1,0:T(8,128)(2,1)}) custom-call(bf16[2,256,2112]{2,1,0:T(8,128)(2,1)} %pad_maximum_fusion.2.refs_0_, bf16[2,2,256,576]{3,2,1,0:T(8,128)(2,1)} %bitcast.185, ...), custom_call_target="tpu_custom_call" | custom-call | bytes 180000000 | tf_op jit(solution)/shard_map/exchange_LineScatter_ContextThenLine_GroupScatter/pallas_call | solution.py:664
  616.5 3.0 add_convert_fusion
  619.5 1.5 copy.114
  625.6 2.1 dynamic-slice_convert_fusion
  629.4 1.7 fusion.21
  632.2 2.8 fusion.7
  635.1 1.4 fusion.6
  636.5 2.1 concatenate.42
  639.2 1.5 fusion.32.refs_2_
  640.7 71.6 %exchange_LineGather_LineGather_LineGather.1 = (bf16[2,4,64,2624]{3,2,1,0:T(8,128)(2,1)}, f32[1,4,36,128]{3,2,1,0:T(8,128)}, bf16[1,4,128,64]{3,2,1,0:T(8,128)(2...) custom-call(bf16[2,64,2624]{2,1,0:T(8,128)(2,1)} %bitcast.189, ...), custom_call_target="tpu_custom_call" | custom-call | bytes 216000000 | tf_op jit(solution)/shard_map/exchange_LineGather_LineGather_LineGather/pallas_call | solution.py:664
  712.3 1.7 reshape_reshape_reshape.4.refs_1_
  715.7 4.1 bitcast_convert_fusion.1
  719.8 1.9 add_convert_fusion.2
  721.8 2.9 bitcast_convert_fusion.2
  724.7 3.4 bitcast_convert_fusion
  728.2 1.6 slice.74
  730.3 3.1 convolution_convert_fusion
  733.4 42.0 %exchange_GroupSum_GroupSum_GroupSum.1 = (bf16[4,2,80,2048]{3,2,1,0:T(8,128)(2,1)}, bf16[4,2,16,256]{3,2,1,0:T(8,128)(2,1)}, bf16[4,2,16,36]{3,2,1,0:T(8,128)(2,1)}) custom-call(bf16[4,2,80,2048]{3,2,1,0:T(8,128)(2,1)} %bitcast.192, bf16[4,2,16,256]{3,2,1,0:T(8,128)(2,1)} %reshape_reshape_reshape.4.refs_1_, bf16[4,2,16,36]{3,2,1,0:T(8,128)(2,1)} %convert_element_type.216.refs_2_), custom_call_target="tpu_custom_call" | custom-call | bytes 126000000 | tf_op jit(solution)/shard_map/exchange_GroupSum_GroupSum_GroupSum/pallas_call | solution.py:664
  775.4 1.2 reshape.461
  779.6 4.5 convert_bitcast_fusion.2
  784.1 10.5 %slice_convert_fusion = (f32[704,2048]{1,0:T(8,128)}, f32[2048,704]{0,1:T(8,128)}, f32[2048,704]{0,1:T(8,128)}) fusion(bf16[2304,2048]{1,0:T(8,128)(2,1)} %all-gather.7.cloned.1.call-done), kind=kLoop, calls=%fused_computation.12 | loop fusion | flops 4325376 | bytes 25952256 | tf_op jit(solution)/shard_map/convert_element_type | solution.py:1791
  794.6 1.5 all-gather.5.cloned.1.call-done
  796.1 3.2 copy.109
  799.3 6.0 copy.118
  805.3 6.0 copy.119
  811.3 2.5 copy.120
  (173 shorter events, 30.4 us)
Async XLA Ops:
  7.2 3.0 copy-start.2
  7.2 154.9 %all-gather.9.cloned.1.call-start = ((), (), s32[]{:S(2)}) async-start(), calls=%async_computation.8 | async-start | bytes 18874368 | tf_op jit(solution)/shard_map/all_gather | solution.py:1635
  7.3 6.7 copy-start.37
  7.3 6.6 copy-start.39
  8.1 2.7 copy-start.21
  10.2 1.7 copy-start.9
  11.9 1.8 copy-start.11
  11.9 2.0 copy-start.41
  13.9 2.1 copy-start.27
  13.9 2.0 copy-start.24
  14.5 27.3 %copy-start.14 = (f32[256,32]{1,0:T(8,128)}, f32[256,32]{1,0:T(8,128)S(1)}, u32[]{:S(2)}) copy-start(f32[256,32]{1,0:T(8,128)S(1)} %get-tuple-element.226) | copy-start | bytes 98308
  41.7 473.9 %reduce-scatter.4.cloned.1.call-start = ((), (), s32[]{:S(2)}) async-start(), calls=%async_computation.3 | async-start | bytes 10616832 | tf_op jit(solution)/shard_map/reduce_scatter | solution.py:1683
  41.8 2.6 copy-start.31
  70.4 43.8 %copy-start.34 = (bf16[2048]{0:T(1024)(128)(2,1)S(1)}, bf16[2048]{0:T(1024)(128)(2,1)}, u32[]{:S(2)}) copy-start(bf16[2048]{0:T(1024)(128)(2,1)} %param.27) | copy-start | bytes 12292
  114.2 4.8 copy-start.19
  114.3 4.7 copy-start.35
  117.1 40.9 %copy-start.32 = (s32[2,256,6]{1,0,2:T(2,128)S(1)}, s32[2,256,6]{1,0,2:T(2,128)}, u32[]{:S(2)}) copy-start(s32[2,256,6]{1,0,2:T(2,128)} %param.20) | copy-start | bytes 36868
  372.2 244.3 %reduce-scatter.6.cloned.1.call-start = ((), (), s32[]{:S(2)}) async-start(), calls=%async_computation.4 | async-start | bytes 18874368 | tf_op jit(solution)/shard_map/reduce_scatter | solution.py:1684
  372.9 346.9 %reduce-scatter.8.cloned.1.call-start = ((), (), s32[]{:S(2)}) async-start(), calls=%async_computation.5 | async-start | bytes 2621440 | tf_op jit(solution)/shard_map/reduce_scatter | solution.py:1722
  372.9 6.7 copy-start.13
  381.7 41.5 %copy-start.1 = (f32[2,64,2048]{2,1,0:T(8,128)S(1)}, f32[2,64,2048]{2,1,0:T(8,128)}, u32[]{:S(2)}) copy-start(f32[2,64,2048]{2,1,0:T(8,128)} %copy-done) | copy-start | bytes 3145732
  381.7 41.6 %copy-start.20 = (f32[2048]{0:T(1024)S(1)}, f32[2048]{0:T(1024)}, u32[]{:S(2)}) copy-start(f32[2048]{0:T(1024)} %copy-done.19) | copy-start | bytes 24580
  381.7 41.6 %copy-start.30 = (f32[2,64]{1,0:T(2,128)S(1)}, f32[2,64]{1,0:T(2,128)}, u32[]{:S(2)}) copy-start(f32[2,64]{1,0:T(2,128)} %copy-done.29) | copy-start | bytes 1540
  423.3 2.3 copy-start.3
  501.8 5.1 copy-start.23
  507.5 4.3 copy-start.10
  511.8 2.1 copy-start.8
  621.0 2.7 copy-start.38
  621.0 8.4 %copy-start.25 = (f32[512]{0:T(512)S(1)}, f32[512]{0:T(512)}, u32[]{:S(2)}) copy-start(f32[512]{0:T(512)} %copy-done.24) | copy-start | bytes 6148
  621.0 11.1 %copy-start.4 = (f32[2,64,2048]{2,1,0:T(8,128)S(1)}, f32[2,64,2048]{2,1,0:T(8,128)}, u32[]{:S(2)}) copy-start(f32[2,64,2048]{2,1,0:T(8,128)} %get-tuple-element.211) | copy-start | bytes 3145732
  621.0 11.1 %copy-start.22 = (f32[2048]{0:T(1024)S(1)}, f32[2048]{0:T(1024)}, u32[]{:S(2)}) copy-start(f32[2048]{0:T(1024)} %copy-done.21) | copy-start | bytes 24580
  621.0 163.1 %all-gather.7.cloned.1.call-start = ((), (), s32[]{:S(2)}) async-start(), calls=%async_computation.7 | async-start | bytes 10616832 | tf_op jit(solution)/shard_map/all_gather | solution.py:1696
  621.6 174.5 %all-gather.5.cloned.1.call-start = ((), (), s32[]{:S(2)}) async-start(), calls=%async_computation.6 | async-start | bytes 2621440 | tf_op jit(solution)/shard_map/all_gather | solution.py:1756
  629.3 5.7 copy-start.15
  629.3 5.7 copy-start.17
  632.1 2.9 copy-start.5
  632.1 2.9 copy-start.42
  632.2 2.9 copy-start.43
  632.2 2.9 copy-start.44
  635.1 1.4 copy-start.16
  635.1 1.4 copy-start.18
  635.1 3.5 copy-start.26
  635.1 3.5 copy-start.33
  721.7 3.0 copy-start.6
  724.7 3.4 copy-start.7
  728.1 2.3 copy-start.12
  799.3 12.0 %slice-start = ((s8[5767168]{0:T(1024)(128)(4,1)}), s8[4194304]{0:T(1024)(128)(4,1)S(1)}, s32[]{:S(2)}) async-start(s8[5767168]{0:T(1024)(128)(4,1)} %bitcast.180), calls=%async_computation.9 | async-start | bytes 8388608
  805.3 6.0 slice-start.1
  (5 other events, 4.8 us)
Sparse Core Ops, SparseCore 0:
  41.8 90.7 all-gather.8
  372.3 73.6 reduce-scatter.3
  449.5 140.7 reduce-scatter.5
  621.1 59.5 reduce-scatter.7
  682.6 58.1 all-gather.6
  742.9 53.1 all-gather.4

commit v3 on v2

--- a/solution.py
+++ b/solution.py
@@ -346,12 +346,12 @@
 
 
 class GroupScatter:
-    def __init__(self, v, axes):
-        self.axes = axes
+    def __init__(self, v, axes, pick=None):
+        self.axes, self.pick = axes, pick
         self.sizes, self.pairs = group_sizes(axes)
-        tail = v.shape[1:]
+        tail = v.shape[1:] if pick is None else v.shape[2:]
         self.across = self.pairs == 4 and tail[0] % 32 == 0
-        v = v.reshape((self.pairs, 2) + tail)
+        v = v.reshape((self.pairs, 2) + v.shape[1:])
         self.rows = tail[0]
         dma = pltpu.SemaphoreType.DMA
         self.inputs = [(v, pl.ANY)]
@@ -394,8 +394,14 @@
         pairs, rows = self.pairs, self.rows
         bits = pairs.bit_length() - 1
         chip, core, device = group_layout(self.axes, self.sizes)
+
+        def side(which):
+            if self.pick is None:
+                return v_ref.at[:, which]
+            return v_ref.at[:, which, self.pick]
+
         swap = pltpu.make_async_remote_copy(
-            src_ref=v_ref.at[:, 1 - core],
+            src_ref=side(1 - core),
             dst_ref=peer,
             send_sem=swap_send,
             recv_sem=swap_recv,
@@ -403,7 +409,7 @@
             device_id_type=MESH,
         )
         swap.start()
-        load = pltpu.make_async_copy(v_ref.at[:, core], mine, load_sem)
+        load = pltpu.make_async_copy(side(core), mine, load_sem)
         load.start()
         yield
 
@@ -621,6 +627,63 @@
         yield from self.second.run(between, out_ref, *refs)
 
 
+class SumThenShare:
+    def __init__(self, parts, extras, finish, shares, results):
+        self.parts, self.finish = parts, finish
+        self.gathers = [LineGather(share, "tensor") for share in shares]
+        self.counts = (len(extras), len(results))
+        self.inputs = [entry for job in parts for entry in job.inputs]
+        self.inputs += [(extra, pltpu.VMEM) for extra in extras]
+        self.outputs = [entry for job in self.gathers for entry in job.outputs]
+        self.outputs += [(result, pltpu.VMEM) for result in results]
+        self.scratch = [pltpu.VMEM(shape.shape, shape.dtype) for job in parts for shape, _ in job.outputs]
+        self.scratch += [pltpu.VMEM(share.shape, share.dtype) for share in shares]
+        for job in parts + self.gathers:
+            self.scratch += job.scratch
+
+    def greets(self):
+        return [device for job in self.parts + self.gathers[:1] for device in job.greets()]
+
+    def run(self, *refs):
+        refs = list(refs)
+
+        def take(count):
+            taken = refs[:count]
+            del refs[:count]
+            return taken
+
+        part_inputs = [take(len(job.inputs)) for job in self.parts]
+        extras = take(self.counts[0])
+        outputs = take(len(self.gathers))
+        results = take(self.counts[1])
+        sums = take(len(self.parts))
+        shares = take(len(self.gathers))
+        running = [
+            job.run(*inputs, total, *take(len(job.scratch)))
+            for job, inputs, total in zip(self.parts, part_inputs, sums)
+        ]
+        gathers = [
+            job.run(share, output, *take(len(job.scratch)))
+            for job, share, output in zip(self.gathers, shares, outputs)
+        ]
+        yield from side_by_side(running)
+        self.finish(sums, extras, shares, results)
+        yield from side_by_side(gathers)
+
+
+def side_by_side(running):
+    while running:
+        left = []
+        for step in running:
+            try:
+                next(step)
+                left.append(step)
+            except StopIteration:
+                pass
+        running = left
+        yield
+
+
 class GroupSum:
     def __init__(self, v, axes):
         self.first = GroupScatter(v, axes)
@@ -647,15 +710,8 @@
     running = [
         job.run(*taken[0][at], *taken[1][at], *taken[2][at]) for at, job in enumerate(jobs)
     ]
-    while running:
-        left = []
-        for step in running:
-            try:
-                next(step)
-                left.append(step)
-            except StopIteration:
-                pass
-        running = left
+    for _ in side_by_side(running):
+        pass
 
 
 def exchange(jobs, collective_id, micros):
@@ -671,10 +727,13 @@
             collective_id=collective_id, has_side_effects=True, vmem_limit_bytes=56 * MIB
         ),
         cost_estimate=pl.CostEstimate(
-            flops=0, bytes_accessed=3_600_000 * micros, transcendentals=0
+            flops=0, bytes_accessed=360_000 * micros, transcendentals=0
         ),
         name="exchange_" + "_".join(type(job).__name__ for job in jobs[:3]),
     )(*[value for value, _ in inputs])
+
+
+KV_WIDTH = 640
 
 
 def turn(vectors, cosine, sine):
@@ -712,8 +771,8 @@
 ):
     heads = query_w.shape[1] // (NOPE + ROPE)
     allowed = allowed_keys(row_ref, column_ref, row_place_ref, column_place_ref)
-    latent = kv_ref[0, :, :LATENT]
-    key_rope = kv_ref[0, :, LATENT:]
+    latent = kv_ref[:, :LATENT]
+    key_rope = kv_ref[:, LATENT : LATENT + ROPE]
     query = mm(x_ref[...], query_w[...])
     for head in range(heads):
         start = head * (NOPE + ROPE)
@@ -758,15 +817,18 @@
     out_w_ref,
     query_grad,
     expanded_grad,
+    query_w_sum,
+    up_w_sum,
+    out_w_sum,
 ):
     heads = query_w.shape[1] // (NOPE + ROPE)
     scale = (NOPE + ROPE) ** (-0.5)
     allowed = allowed_keys(row_ref, column_ref, row_place_ref, column_place_ref)
-    latent = kv_ref[0, :, :LATENT]
-    key_rope = kv_ref[0, :, LATENT:]
+    latent = kv_ref[:, :LATENT]
+    key_rope = kv_ref[:, LATENT : LATENT + ROPE]
     grad = grad_ref[...]
     attended_grad = mm_nt(grad, out_w[...]).astype(BF16)
-    rope_grad = jnp.zeros((kv_ref.shape[1], ROPE), F32)
+    rope_grad = jnp.zeros((kv_ref.shape[0], ROPE), F32)
     for head in range(heads):
         first = head * (NOPE + VDIM)
         key_nope = expanded_ref[0, :, first : first + NOPE]
@@ -794,20 +856,26 @@
     kv_grad_ref[0, :, LATENT:] = (scale * rope_grad).astype(BF16)
     x_grad_ref[...] = mm_nt(query_grad[...], query_w[...]).astype(BF16)
     pieces = (
-        (query_w_ref, x_ref[...], query_grad[...]),
-        (up_w_ref, latent, expanded_grad[...]),
-        (out_w_ref, attended_ref[...], grad),
+        (query_w_sum, query_w_ref, x_ref[...], query_grad[...]),
+        (up_w_sum, up_w_ref, latent, expanded_grad[...]),
+        (out_w_sum, out_w_ref, attended_ref[...], grad),
     )
-
-    @pl.when(pl.program_id(0) == 0)
+    step = pl.program_id(0)
+
+    @pl.when(step == 0)
     def _():
-        for target, left, right in pieces:
-            target[...] = mm_tn(left, right)
-
-    @pl.when(pl.program_id(0) > 0)
+        for total, _, left, right in pieces:
+            total[...] = mm_tn(left, right)
+
+    @pl.when(step > 0)
     def _():
-        for target, left, right in pieces:
-            target[...] += mm_tn(left, right)
+        for total, _, left, right in pieces:
+            total[...] += mm_tn(left, right)
+
+    @pl.when(step == pl.num_programs(0) - 1)
+    def _():
+        for total, target, _, _ in pieces:
+            target[...] = total[...].astype(BF16)
 
 
 def attention_specs(micro_count, rows, seq_len, heads):
@@ -838,8 +906,12 @@
     return per_micro, rows_of, whole, places, weights, kept
 
 
+def kv_spec(seq_len):
+    return pl.BlockSpec((seq_len, KV_WIDTH), lambda m: (0, m))
+
+
 def attend(x_attn, kv_all, places, weights, micro_count, heads):
-    rows, seq_len = x_attn.shape[0] // micro_count, kv_all.shape[1]
+    rows, seq_len = x_attn.shape[0] // micro_count, kv_all.shape[0]
     per_micro, rows_of, _, place_specs, weight_specs, kept = attention_specs(
         micro_count, rows, seq_len, heads
     )
@@ -847,7 +919,7 @@
     return pl.pallas_call(
         attend_kernel,
         grid=(micro_count,),
-        in_specs=[rows_of(D), per_micro(seq_len, LATENT + ROPE)] + place_specs + weight_specs,
+        in_specs=[rows_of(D), kv_spec(seq_len)] + place_specs + weight_specs,
         out_specs=[rows_of(D)] + kept,
         out_shape=[
             jax.ShapeDtypeStruct((total, D), BF16),
@@ -865,7 +937,7 @@
 
 
 def attend_back(grad, x_attn, kv_all, places, weights, kept, micro_count, heads):
-    rows, seq_len = x_attn.shape[0] // micro_count, kv_all.shape[1]
+    rows, seq_len = x_attn.shape[0] // micro_count, kv_all.shape[0]
     per_micro, rows_of, whole, place_specs, weight_specs, kept_specs = attention_specs(
         micro_count, rows, seq_len, heads
     )
@@ -873,7 +945,7 @@
     return pl.pallas_call(
         attend_back_kernel,
         grid=(micro_count,),
-        in_specs=[rows_of(D), kept_specs[0], rows_of(D), per_micro(seq_len, LATENT + ROPE)]
+        in_specs=[rows_of(D), kept_specs[0], rows_of(D), kv_spec(seq_len)]
         + place_specs
         + kept_specs[1:]
         + weight_specs,
@@ -881,17 +953,20 @@
         out_shape=[
             jax.ShapeDtypeStruct((micro_count, seq_len, LATENT + ROPE), BF16),
             jax.ShapeDtypeStruct((total, D), BF16),
-            jax.ShapeDtypeStruct(weights[0].shape, F32),
-            jax.ShapeDtypeStruct(weights[1].shape, F32),
-            jax.ShapeDtypeStruct(weights[2].shape, F32),
+            jax.ShapeDtypeStruct(weights[0].shape, BF16),
+            jax.ShapeDtypeStruct(weights[1].shape, BF16),
+            jax.ShapeDtypeStruct(weights[2].shape, BF16),
         ],
         scratch_shapes=[
             pltpu.VMEM((rows, heads * (NOPE + ROPE)), BF16),
             pltpu.VMEM((seq_len, heads * (NOPE + VDIM)), BF16),
+            pltpu.VMEM(weights[0].shape, F32),
+            pltpu.VMEM(weights[1].shape, F32),
+            pltpu.VMEM(weights[2].shape, F32),
         ],
         compiler_params=pltpu.CompilerParams(vmem_limit_bytes=60 * MIB),
         cost_estimate=pl.CostEstimate(
-            flops=20_000_000_000, bytes_accessed=100_000_000, transcendentals=0
+            flops=2_000_000_000, bytes_accessed=10_000_000, transcendentals=0
         ),
         name="attend_back",
     )(grad, kept[0], x_attn, kv_all, *places, *kept[1:], *weights)
@@ -1391,7 +1466,7 @@
         def _():
             fetch(step + 1)
 
-        @pl.when(step == 1)
+        @pl.when(step == 0)
         def _():
             for micro in range(1, micro_count):
                 for mask in direct:
@@ -1626,14 +1701,14 @@
     normed_latent = latent_raw * inv_latent
     latent = (normed_latent * gain_latent).astype(BF16)
     key_rope = rotate(kv_raw[:, LATENT:], cos_query, sin_query).astype(BF16)
-    kv_own = jnp.concatenate([latent, key_rope], axis=1)
-    kv_all = exchange(
-        [GroupGather(part, ("context",)) for part in jnp.split(kv_own, micro_count)], 1, 20
-    )
-    kv_all = jnp.concatenate([flat(part) for part in kv_all], axis=0)
+    blank = jnp.zeros((rows, KV_WIDTH - LATENT - ROPE), BF16)
+    kv_own = jnp.concatenate([latent, key_rope, blank], axis=1)
+    kv_own = kv_own.reshape(micro_count, block_rows, KV_WIDTH).transpose(1, 0, 2)
+    kv_own = kv_own.reshape(block_rows, micro_count * KV_WIDTH)
+    (kv_all,) = exchange([GroupGather(kv_own, ("context",))], 1, 20)
     kv_all, cot_late = lax.optimization_barrier((kv_all, cotangent))
     cot_all = lax.all_gather(cot_late, GROUP, axis=0)
-    kv_all = kv_all.reshape(micro_count, seq_len, LATENT + ROPE)
+    kv_all = kv_all.reshape(seq_len, micro_count * KV_WIDTH)
     seg_query = lax.dynamic_slice_in_dim(segments, start_row, block_rows, axis=1)
     places = (
         seg_query[:, :, None],
@@ -1645,13 +1720,29 @@
     )
     weights = (w_query, w_kv_up, w_out)
     attn_part, *kept = attend(x_attn, kv_all, places, weights, micro_count, heads_local)
-    (attn_sum,) = exchange([to_owner(attn_part)], 2, 40)
-    hidden_one = own(x_rows) + flat(attn_sum)
-    inv_ffn = rms_scale(hidden_one)
-    normed_ffn = hidden_one * inv_ffn
-    x_ffn = (normed_ffn * gain_ffn).astype(BF16)
-    (x_ffn,) = exchange([from_owners(x_ffn)], 3, 40)
-    x_ffn = flat(x_ffn.reshape(rows, D))
+    own_shape = (micro_count, own_rows, D)
+    tokens_own = own(tokens.reshape(rows, D)).reshape(own_shape)
+
+    def finish_attention(sums, extras, shares, results):
+        for m in range(micro_count):
+            hidden = extras[0][m].astype(F32) + sums[0][m]
+            results[0][m] = hidden
+            shares[0][m] = (hidden * rms_scale(hidden) * extras[1][...]).astype(BF16)
+
+    x_ffn, hidden_one = exchange(
+        [
+            SumThenShare(
+                [to_owner(attn_part)],
+                [tokens_own, gain_ffn[None]],
+                finish_attention,
+                [jax.ShapeDtypeStruct(own_shape, BF16)],
+                [jax.ShapeDtypeStruct(own_shape, F32)],
+            )
+        ],
+        2,
+        80,
+    )
+    x_ffn = x_ffn.reshape(rows, D)
     x_ext = jnp.concatenate([x_ffn.reshape(micro_count, block_rows, D), named], axis=-1)
 
     (
@@ -1681,97 +1772,153 @@
     shared_units = shared_grads.shape[1]
     shared_grads = shared_grads.reshape(groups, -1, D)
     shared_grads = lax.psum_scatter(shared_grads, GROUP, scatter_dimension=0, tiled=False)
+    cot_own = own(cot_rows).reshape(own_shape)
+
+    def finish_experts(sums, extras, shares, results):
+        hidden, cot, gain = extras
+        gain_grad = jnp.zeros((1, D), F32)
+        for m in range(micro_count):
+            inverse = rms_scale(hidden[m])
+            normed = hidden[m] * inverse
+            grad = sums[0][m]
+            gain_grad = gain_grad + jnp.sum(grad * normed, axis=0, keepdims=True)
+            total = cot[m].astype(F32) + norm_back(grad * gain[...], normed, inverse)
+            results[0][m] = total
+            shares[0][m] = total.astype(BF16)
+        results[1][...] = gain_grad
+
     out_sum = lax.psum_scatter(out_part, GROUP, scatter_dimension=0, tiled=False)
-    (grad_x_ffn,) = exchange([to_owner(grad_sum)], 5, 40)
-    grad_x_ffn = flat(grad_x_ffn)
-
-    norm_ffn_grad = jnp.sum(grad_x_ffn * normed_ffn, axis=0)
-    grad_one = own(cot_rows).astype(F32) + norm_back(grad_x_ffn * gain_ffn, normed_ffn, inv_ffn)
-    (grad_attn_low,) = exchange([from_owners(grad_one.astype(BF16))], 6, 40)
+    grad_attn_low, grad_one, norm_ffn_grad = exchange(
+        [
+            SumThenShare(
+                [to_owner(grad_sum)],
+                [hidden_one, cot_own, gain_ffn[None]],
+                finish_experts,
+                [jax.ShapeDtypeStruct(own_shape, BF16)],
+                [
+                    jax.ShapeDtypeStruct(own_shape, F32),
+                    jax.ShapeDtypeStruct((1, D), F32),
+                ],
+            ),
+        ],
+        5,
+        90,
+    )
     grad_attn_low = grad_attn_low.reshape(rows, D)
     grad_kv_part, grad_x_heads, query_grad, kv_up_grad, out_grad = attend_back(
         grad_attn_low, x_attn, kv_all, places, weights, kept, micro_count, heads_local
     )
     grad_x_heads, shared_grads = lax.optimization_barrier((grad_x_heads, shared_grads))
     shared_grads = lax.all_gather(shared_grads, GROUP, axis=0, tiled=True)
-    router_part = router_grad.T.astype(BF16).reshape(tensor_size, micro_count, own_rows, -1)
-    router_part = router_part.transpose(1, 0, 2, 3).reshape(rows, -1)
-    late, grad_kv, query_part, kv_up_part, out_grad = exchange(
+    router_part = router_grad.T.astype(BF16).reshape(1, tensor_size, -1, LANES)
+    latent_own = own(latent_raw).reshape(micro_count, own_rows, LATENT)
+    turns_own = [
+        own(angle).reshape(micro_count, own_rows, ROPE)
+        for angle in (
+            jnp.tile(cos_query, (1, 2)),
+            jnp.concatenate([sin_query, -sin_query], axis=1),
+        )
+    ]
+
+    def finish_rows(sums, extras, shares, results):
+        x_grad, kv_grad, router = sums
+        x_own, one, ffn_gain_grad, raw, cosine, sine, gain, latent_gain, down_w = extras
+        gain_grad = jnp.zeros((1, D), F32)
+        latent_gain_grad = jnp.zeros((1, LATENT), F32)
+        for m in range(micro_count):
+            inverse = rms_scale(raw[m])
+            normed = raw[m] * inverse
+            grad = kv_grad[m, :, :LATENT]
+            latent_gain_grad = latent_gain_grad + jnp.sum(grad * normed, axis=0, keepdims=True)
+            kv_low = jnp.concatenate(
+                [
+                    norm_back(grad * latent_gain[...], normed, inverse),
+                    turn(kv_grad[m, :, LATENT:], cosine[m], sine[m]),
+                ],
+                axis=1,
+            ).astype(BF16)
+            x = x_own[m].astype(F32)
+            inverse = rms_scale(x)
+            normed = x * inverse
+            grad = x_grad[m] + mm(kv_low, down_w[...])
+            gain_grad = gain_grad + jnp.sum(grad * normed, axis=0, keepdims=True)
+            total = one[m] + norm_back(grad * gain[...], normed, inverse)
+            shares[0][m, :, :D] = total.astype(BF16)
+            shares[0][m, :, D:] = kv_low
+        shares[1][0] = router[0].astype(BF16)
+        shares[2][0, :, :D] = gain_grad
+        shares[2][0, :, D : 2 * D] = ffn_gain_grad[...]
+        shares[2][0, :, 2 * D :] = latent_gain_grad
+
+    finished, router_all, small = exchange(
         [
-            to_owner(jnp.concatenate([grad_x_heads, router_part], axis=1)),
-            ContextThenLine(
+            SumThenShare(
                 [
-                    grad_kv_part[m].reshape(context_size, block_rows, LATENT + ROPE)
-                    for m in range(micro_count)
+                    to_owner(grad_x_heads),
+                    ContextThenLine(
+                        [
+                            grad_kv_part[m].reshape(context_size, block_rows, LATENT + ROPE)
+                            for m in range(micro_count)
+                        ],
+                        ("context",),
+                        "tensor",
+                    ),
+                    LineScatter(router_part, "tensor"),
                 ],
-                ("context",),
-                "tensor",
+                [
+                    tokens_own,
+                    grad_one,
+                    norm_ffn_grad,
+                    latent_own,
+                    *turns_own,
+                    gain_attn[None],
+                    gain_latent[None],
+                    w_kv_down.T,
+                ],
+                finish_rows,
+                [
+                    jax.ShapeDtypeStruct((micro_count, own_rows, D + LATENT + ROPE), BF16),
+                    jax.ShapeDtypeStruct((1,) + router_part.shape[2:], BF16),
+                    jax.ShapeDtypeStruct((1, 1, 2 * D + LATENT), F32),
+                ],
+                [],
             ),
-            GroupScatter(query_grad.astype(BF16).reshape(groups, D // groups, -1), GROUP),
-            GroupScatter(kv_up_grad.astype(BF16).reshape(groups, LATENT // groups, -1), GROUP),
-            GroupScatter(out_grad.astype(BF16).reshape(groups, -1, D), GROUP),
         ],
         8,
-        50,
+        100,
     )
-    late = flat(late)
-    late, out_sum = lax.optimization_barrier((late, out_sum))
-    out_sum = out_sum.reshape(rows, D).astype(F32) + shared_out.reshape(rows, D).astype(F32)
+    finished = finished.reshape(rows, -1)
+    finished, out_sum = lax.optimization_barrier((finished, out_sum))
+    out_sum = out_sum.astype(F32) + shared_out.astype(F32)
     out_sum = out_sum.astype(BF16).reshape(micro_count, tensor_size, own_rows, D)
     out_sum = out_sum.transpose(1, 0, 2, 3)
     out_sum = lax.psum_scatter(out_sum, "tensor", scatter_dimension=0, tiled=False)
-    grad_x_heads, router_own = late[:, :D], late[:, D:]
-    grad_kv = flat(grad_kv)
-    grad_latent, grad_rope_key = grad_kv[:, :LATENT], grad_kv[:, LATENT:]
-    normed_latent_own = own(normed_latent)
-    norm_latent_grad = jnp.sum(grad_latent * normed_latent_own, axis=0)
-    grad_latent_raw = norm_back(grad_latent * gain_latent, normed_latent_own, own(inv_latent))
-    grad_kv_raw = jnp.concatenate(
-        [grad_latent_raw, unrotate(grad_rope_key, own(cos_query), own(sin_query))], axis=-1
-    ).astype(BF16)
-    grad_x_attn = grad_x_heads + mm_nt(grad_kv_raw, w_kv_down)
-    normed_attn_own = own(normed_attn)
-    norm_attn_grad = jnp.sum(grad_x_attn * normed_attn_own, axis=0)
-    grad_input = grad_one + norm_back(grad_x_attn * gain_attn, normed_attn_own, own(inv_attn))
-    finished, small, router_all, query_grad, kv_up_grad, out_grad = exchange(
-        [
-            from_owners(jnp.concatenate([grad_input.astype(BF16), grad_kv_raw], axis=1)),
-            LineGather(
-                jnp.concatenate([norm_attn_grad, norm_ffn_grad, norm_latent_grad]).reshape(
-                    1, -1, LANES
-                ),
-                "tensor",
-            ),
-            LineGather(router_own.astype(BF16)[None], "tensor"),
-            GroupGather(query_part, GROUP),
-            GroupGather(kv_up_part, GROUP),
-            GroupGather(out_grad, GROUP),
-        ],
-        9,
-        60,
-    )
-    finished = finished.reshape(rows, -1)
-    out_sum, finished = lax.optimization_barrier((out_sum, finished))
-    output = (hidden_one + flat(out_sum).astype(F32)).astype(BF16)
-    output = lax.all_gather(output, "tensor", axis=0)
-    output = output.reshape(tensor_size, micro_count, own_rows, D).transpose(1, 0, 2, 3)
     grad_tokens, grad_kv_raw = finished[:, :D], finished[:, D:]
     kv_width = -(-grad_kv_raw.shape[1] // (16 * groups)) * 16 * groups
     grad_kv_raw = jnp.pad(grad_kv_raw, ((0, 0), (0, kv_width - grad_kv_raw.shape[1])))
     kv_down_grad = mm_tn(grad_kv_raw, x_attn).astype(BF16)
-    small = jnp.sum(small, axis=(0, 1)).astype(BF16)
-    kv_down_grad, router_grad, small = exchange(
+    small = jnp.sum(small, axis=(0, 1, 2)).astype(BF16)
+    query_grad, kv_up_grad, out_grad, kv_down_grad, router_grad, small = exchange(
         [
             GroupSum(part.reshape(groups, -1, part.shape[-1]), GROUP)
             for part in (
+                query_grad,
+                kv_up_grad,
+                out_grad,
                 kv_down_grad,
                 router_all.reshape(groups * 16, -1),
                 small.reshape(groups * 16, -1),
             )
         ],
         10,
-        35,
+        80,
     )
+    query_grad, kv_up_grad, out_grad, kv_down_grad, out_sum, shared_grads = lax.optimization_barrier(
+        (query_grad, kv_up_grad, out_grad, kv_down_grad, out_sum, shared_grads)
+    )
+    output = (hidden_one + out_sum.astype(F32)).astype(BF16)
+    output = lax.all_gather(output, "tensor", axis=0)
+    output = output.transpose(1, 0, 2, 3)
     kv_down_grad = kv_down_grad.reshape(-1, D)[: LATENT + ROPE].astype(F32).T
     router_grad = router_grad.reshape(D, experts).astype(F32)
     small = small.reshape(-1).astype(F32)

time: 832 us -> 813 us (0.977)
  other arithmetic: 87 us -> 48.8 us
  waiting for transfers between devices: 2.78 us -> 23.9 us
  Pallas kernels: 662 us -> 671 us
    all_gather x1, waiting for transfers between devices: 1.47 us -> 22.6 us  [per_device(): output = lax.all_gather(output, 'tensor', axis=0)]
    convert_element_type x11 -> x2, other arithmetic: 21.6 us -> 2.1 us  [the longest x1 2.09 us: per_device(): output = (hidden_one + out_sum.astype(F32)).astype(BF16)]
    pallas_call x8 -> x5, Pallas kernels: 392 us -> 411 us  [exchange(): pl.pallas_call(functools.partial(exchange_kernel, jobs), out_shape=tuple(...]
    pallas_call x1, Pallas kernels: 210 us -> 200 us  [expert_pass(): pl.pallas_call(functools.partial(expert_kernel, pairs, context_size, fe),...]
    unnamed x100 -> x73, local copies, waits for them, and re-layouts: 19.4 us -> 20.2 us
  transfers between devices with their start and end apart: 6 -> 6, of which waited for: 1 -> 1; matrix products, arithmetic and copies ran while one was open for 13% -> 8% of each run, Pallas kernels for 52% -> 55%
where the time goes in v3:
time: 813 us; the launch traced here: 808 us
  Pallas kernels  671 us (83%)
  other arithmetic  48.8 us (6%)
  local copies, waits for them, and re-layouts  45.6 us (6%)
  waiting for transfers between devices  23.9 us (3%)
  between operations  14.9 us (2%)
    pallas_call x5, Pallas kernels, exchange(): pl.pallas_call(functools.partial(exchange_kernel, jobs), out_shape=tuple(...  411 us
    pallas_call x1, Pallas kernels, expert_pass(): pl.pallas_call(functools.partial(expert_kernel, pairs, context_size, fe),...  200 us
    pallas_call x1, Pallas kernels, attend_back(): pl.pallas_call(attend_back_kernel, grid=(micro_count,), in_specs=[rows_of...  37.3 us
    all_gather x1, waiting for transfers between devices, per_device(): output = lax.all_gather(output, 'tensor', axis=0)  22.6 us
    pallas_call x1, Pallas kernels, attend(): pl.pallas_call(attend_kernel, grid=(micro_count,), in_specs=[rows_of(D),...  21.7 us
    unnamed x73, local copies, waits for them, and re-layouts  20.2 us
  transfers between devices with their start and end apart: 6, of which 1 were waited for; matrix products, arithmetic and copies ran while one was open for 8% of the time, Pallas kernels for 55%

profile of v3, /device:TPU:0, one launch (start us, length us, event | category | flops | bytes accessed | tf_op | source)
XLA Modules:
  0.0 808.4 jit_solution(11997081124976162191)
XLA Ops:
  7.3 0.8 convert_element_type.124
  8.1 2.1 multiply_reduce_fusion
  10.2 0.7 convert_element_type.122
  12.9 1.1 copy-done.7
  14.0 1.4 fusion.9
  15.4 1.1 fusion.7
  17.2 1.7 copy.97
  18.9 0.9 copy.113
  19.8 21.8 %exchange_GroupGather.1 = bf16[2,2,256,1280]{3,2,1,0:T(8,128)(2,1)} custom-call(bf16[256,1280]{1,0:T(8,128)(2,1)} %bitcast.104), custom_call_target="tpu_custom_call" | custom-call | bytes 7200000 | tf_op jit(solution)/shard_map/exchange_GroupGather/pallas_call | solution.py:720
  43.6 0.9 copy.99.row_ref
  44.5 0.8 copy.100.cos_ref
  45.9 0.7 pad_maximum_fusion.1.sin_ref
  46.7 0.8 constant_dynamic-slice_fusion.3.refs_1_.refs_4_
  48.1 21.7 %attend.1 = (bf16[512,2048]{1,0:T(8,128)(2,1)}, bf16[512,512]{1,0:T(8,128)(2,1)}, bf16[2,4,256,192]{3,2,1,0:T(8,128)(2,1)}, bf16[2,1024,1024]{2,1,0:T(8,128)(2,1)}, f32[2,4,256,1]{3,2,1,0:T(8,128)}) custom-call(bf16[512,2048]{1,0:T(8,128)(2,1)} %copy-done.1, bf16[1024,1280]{1,0:T(8,128)(2,1)} %bitcast.89, s32[2,256,1]{2,1,0:T(8,128)} %copy.99.row_ref, ...), custom_call_target="tpu_custom_call" | custom-call | flops 8999999488 | bytes 60000000 | tf_op jit(solution)/shard_map/attend/pallas_call | solution.py:919
  69.8 80.1 %exchange_SumThenShare.3 = (bf16[2,4,64,2048]{3,2,1,0:T(8,128)(2,1)}, f32[2,64,2048]{2,1,0:T(8,128)}) custom-call(bf16[2,256,2048]{2,1,0:T(8,128)(2,1)} %bitcast.112, bf16[2,64,2048]{2,1,0:T(8,128)(2,1)} %constant_dynamic-slice_fusion.3.refs_1_.refs_4_, f32[1,2048]{1,0:T(1,128)} %bitcast.127), custom_call_target="tpu_custom_call" | custom-call | bytes 28800000 | tf_op jit(solution)/shard_map/exchange_SumThenShare/pallas_call | solution.py:720
  149.9 3.2 pad_maximum_fusion.x_ref
  153.0 200.4 %expert_pass.1 = (bf16[8,2,256,2048]{3,2,1,0:T(8,128)(2,1)}, bf16[2,4,256,2048]{3,2,1,0:T(8,128)(2,1)}, f32[2,352,2048]{2,1,0:T(8,128)}, f32[2,352,2048]{2,1,0:T...) custom-call(bf16[2,256,2176]{2,1,0:T(8,128)(2,1)} %pad_maximum_fusio, ...), custom_call_target="tpu_custom_call" | custom-call | flops 130459631616 | bytes 500000000 | tf_op jit(solution)/shard_map/expert_pass/pallas_call | solution.py:1570
  354.5 0.7 copy.110.refs_8_
  355.7 0.7 fusion.3.refs_9_
  356.4 0.7 constant_dynamic-slice_fusion.1.refs_7_
  357.1 1.9 constant_dynamic-slice_fusion.2.refs_2_
  359.3 1.0 reshape_reshape.31.refs_3_
  360.2 7.4 convert_reduce_fusion
  367.7 2.0 add_convert_fusion.1.refs_0_
  369.7 74.4 %exchange_SumThenShare.4 = (bf16[2,4,64,2048]{3,2,1,0:T(8,128)(2,1)}, f32[2,64,2048]{2,1,0:T(8,128)}, f32[1,2048]{1,0:T(1,128)}) custom-call(bf16[2,256,2048]{2,1,0:T(8,128)(2,1)} %add_convert_fusion.1.refs_0_, f32[2,64,2048]{2,1,0:T(8,128)} %get-tuple-element.63.refs_1_, bf16[2,64,2048]{2,1,0:T(8,128)(2,1)} %constant_dynamic-slice_fusion.2.refs_2_, ...), custom_call_target="tpu_custom_call" | custom-call | bytes 32400000 | tf_op jit(solution)/shard_map/exchange_SumThenShare/pallas_call | solution.py:720
  444.7 37.3 %attend_back.1 = (bf16[2,1024,576]{2,1,0:T(8,128)(2,1)}, bf16[512,2048]{1,0:T(8,128)(2,1)}, bf16[2048,768]{1,0:T(8,128)(2,1)}, bf16[512,1024]{1,0:T(8,128)(2,1)}, bf16[512,2048]{1,0:T(8,128)(2,1)}) custom-call(bf16[512,2048]{1,0:T(8,128)(2,1)} %bitcast.117, bf16[512,512]{1,0:T(8,128)(2,1)} %get-tuple-element.69.attended_ref, bf16[512,2048]{1,0:T(8,128)(2,1)} %copy-done.1, ...), custom_call_target="tpu_custom_call" | custom-call | flops 2000000000 | bytes 10000000 | tf_op jit(solution)/shard_map/attend_back/pallas_call | solution.py:945
  482.0 3.6 fusion.6
  485.6 109.1 %exchange_SumThenShare.5 = (bf16[2,4,64,2624]{3,2,1,0:T(8,128)(2,1)}, bf16[1,4,64,128]{3,2,1,0:T(8,128)(2,1)}, f32[1,4,1,4608]{3,2,1,0:T(1,128)}) custom-call(bf16[2,256,2048]{2,1,0:T(8,128)(2,1)} %bitcast.111, bf16[2,2,256,576]{3,2,1,0:T(8,128)(2,1)} %bitcast.99, bf16[2,2,256,576]{3,2,1,0:T(8,128)(2,1)} %bitcast.98, ...), custom_call_target="tpu_custom_call" | custom-call | bytes 36000000 | tf_op jit(solution)/shard_map/exchange_SumThenShare/pallas_call | solution.py:720
  594.7 2.4 add_convert_fusion
  597.1 1.5 copy.115
  599.5 0.7 convert_element_type.136.refs_5_
  601.0 1.6 slice.51
  603.1 3.1 convolution_convert_fusion
  606.2 125.8 %exchange_GroupSum_GroupSum_GroupSum.1 = (bf16[4,2,256,768]{3,2,1,0:T(8,128)(2,1)}, bf16[4,2,64,1024]{3,2,1,0:T(8,128)(2,1)}, bf16[4,2,64,2048]{3,2,1,0:T(8,128)...) custom-call(bf16[4,2,256,768]{3,2,1,0:T(8,128)(2,1)} %bitcast.100, ...), custom_call_target="tpu_custom_call" | custom-call | bytes 28800000 | tf_op jit(solution)/shard_map/exchange_GroupSum_GroupSum_GroupSum/pallas_call | solution.py:720
  732.1 1.0 reshape.209
  733.6 1.2 reshape.213
  734.8 1.0 copy.109
  736.4 2.1 add_convert_fusion.2
  738.5 2.8 bitcast_convert_fusion.2
  741.3 2.7 bitcast_convert_fusion.1
  744.0 2.8 convert_bitcast_fusion.2
  747.1 3.4 bitcast_convert_fusion
  750.5 10.5 %slice_convert_fusion = (f32[704,2048]{1,0:T(8,128)}, f32[2048,704]{0,1:T(8,128)}, f32[2048,704]{0,1:T(8,128)}) fusion(bf16[2304,2048]{1,0:T(8,128)(2,1)} %all-gather.6.cloned.1.call-done), kind=kLoop, calls=%fused_computation.12 | loop fusion | flops 4325376 | bytes 25952256 | tf_op jit(solution)/shard_map/convert_element_type | solution.py:1938
  761.0 22.6 %all-gather.10.cloned.1.call-done = bf16[8,64,2048]{2,1,0:T(8,128)(2,1)} async-done(((bf16[2,64,2048]{2,1,0:T(8,128)(2,1)}), bf16[8,64,2048]{2,1,0:T(8,128)(2,1)}) %all-gather.10.cloned.1.call-update) | async-done | bytes 2097168 | tf_op jit(solution)/shard_map/all_gather | solution.py:1920
  783.6 3.2 copy.108
  786.7 6.0 copy.119
  792.8 6.0 copy.120
  798.8 2.5 copy.121
  (122 shorter events, 12.0 us)
Async XLA Ops:
  7.2 5.1 copy-start
  7.2 145.8 %all-gather.8.cloned.1.call-start = ((), (), s32[]{:S(2)}) async-start(), calls=%async_computation.7 | async-start | bytes 18874368 | tf_op jit(solution)/shard_map/all_gather | solution.py:1710
  8.1 8.6 %copy-start.26 = (f32[512]{0:T(512)}, f32[512]{0:T(512)S(1)}, u32[]{:S(2)}) copy-start(f32[512]{0:T(512)S(1)} %convert_element_type.124) | copy-start | bytes 6148
  10.9 2.0 copy-start.23
  11.4 1.5 copy-start.16
  11.4 34.5 %copy-start.14 = (f32[256,32]{1,0:T(8,128)}, f32[256,32]{1,0:T(8,128)S(1)}, u32[]{:S(2)}) copy-start(f32[256,32]{1,0:T(8,128)S(1)} %get-tuple-element.197) | copy-start | bytes 98308
  11.5 0.7 copy-start.20
  12.2 4.5 copy-start.18
  12.2 3.2 copy-start.8
  12.3 1.7 copy-start.7
  14.0 1.4 copy-start.1
  19.8 22.0 %copy-start.27 = (s32[2,1024]{1,0:T(2,128)S(1)}, s32[2,1024]{1,0:T(2,128)}, u32[]{:S(2)}) copy-start(s32[2,1024]{1,0:T(2,128)} %param.19) | copy-start | bytes 24580
  19.8 22.6 %copy-start.29 = (bf16[2048]{0:T(1024)(128)(2,1)S(1)}, bf16[2048]{0:T(1024)(128)(2,1)}, u32[]{:S(2)}) copy-start(bf16[2048]{0:T(1024)(128)(2,1)} %param.27) | copy-start | bytes 12292
  19.8 23.2 %copy-start.28 = (s32[2,256,6]{1,0,2:T(2,128)S(1)}, s32[2,256,6]{1,0,2:T(2,128)}, u32[]{:S(2)}) copy-start(s32[2,256,6]{1,0,2:T(2,128)} %param.20) | copy-start | bytes 36868
  19.8 24.7 %copy-start.21 = (f32[256,32]{0,1:T(8,128)S(1)}, f32[256,32]{0,1:T(8,128)}, u32[]{:S(2)}) copy-start(f32[256,32]{0,1:T(8,128)} %copy-done.20) | copy-start | bytes 98308
  19.8 26.1 %copy-start.17 = (f32[256,32]{1,0:T(8,128)S(1)}, f32[256,32]{1,0:T(8,128)}, u32[]{:S(2)}) copy-start(f32[256,32]{1,0:T(8,128)} %copy-done.16) | copy-start | bytes 98308
  41.7 443.9 %reduce-scatter.4.cloned.1.call-start = ((), (), s32[]{:S(2)}) async-start(), calls=%async_computation.3 | async-start | bytes 10616832 | tf_op jit(solution)/shard_map/reduce_scatter | solution.py:1774
  353.4 241.3 %reduce-scatter.6.cloned.1.call-start = ((), (), s32[]{:S(2)}) async-start(), calls=%async_computation.4 | async-start | bytes 18874368 | tf_op jit(solution)/shard_map/reduce_scatter | solution.py:1790
  353.4 0.8 copy-start.19
  353.5 1.8 copy-start.4
  354.1 1.5 copy-start.15
  354.2 1.5 copy-start.9
  354.2 382.2 %reduce-scatter.8.cloned.1.call-start = ((), (), s32[]{:S(2)}) async-start(), calls=%async_computation.5 | async-start | bytes 2621440 | tf_op jit(solution)/shard_map/reduce_scatter | solution.py:1895
  354.3 4.7 copy-start.22
  360.2 7.5 copy-start.13
  485.6 109.1 %copy-start.11 = (bf16[2,256,2048]{2,1,0:T(8,128)(2,1)S(1)}, bf16[2,256,2048]{2,1,0:T(8,128)(2,1)}, u32[]{:S(2)}) copy-start(bf16[2,256,2048]{2,1,0:T(8,128)(2,1)} %get-tuple-element.93) | copy-start | bytes 6291460
  598.5 0.9 copy-start.24
  598.5 1.7 copy-start.25
  598.5 2.4 copy-start.6
  598.5 137.8 %all-gather.6.cloned.1.call-start = ((), (), s32[]{:S(2)}) async-start(), calls=%async_computation.6 | async-start | bytes 10616832 | tf_op jit(solution)/shard_map/all_gather | solution.py:1812
  599.1 184.4 %all-gather.10.cloned.1.call-start = ((), (), s32[]{:S(2)}) async-start(), calls=%async_computation.8 | async-start | bytes 2621440 | tf_op jit(solution)/shard_map/all_gather | solution.py:1920
  600.9 2.3 copy-start.2
  732.1 4.3 copy-start.3
  736.4 4.9 copy-start.12
  741.3 2.7 copy-start.10
  744.0 3.1 copy-start.5
  786.7 12.0 %slice-start = ((s8[5767168]{0:T(1024)(128)(4,1)}), s8[4194304]{0:T(1024)(128)(4,1)S(1)}, s32[]{:S(2)}) async-start(s8[5767168]{0:T(1024)(128)(4,1)} %bitcast.94), calls=%async_computation.9 | async-start | bytes 8388608
  792.8 6.0 slice-start.1
Sparse Core Ops, SparseCore 0:
  41.8 90.6 all-gather.7
  353.5 76.9 reduce-scatter.3
  434.1 129.8 reduce-scatter.5
  598.7 43.0 reduce-scatter.7
  643.6 91.9 all-gather.5
  738.6 44.9 all-gather.9

commit v4 on v3

--- a/solution.py
+++ b/solution.py
@@ -343,6 +343,30 @@
                 @pl.when(between(way, target))
                 def _():
                     copy(way, target, False).wait_send()
+
+
+class LineScatterSum(LineScatter):
+    def __init__(self, parts, one, axis):
+        lead, self.count, all_rows, width = parts.shape
+        total = lax.axis_size(axis)
+        self.all_rows = all_rows
+        super().__init__(
+            jax.ShapeDtypeStruct((lead, total, all_rows // total, width), BF16), axis
+        )
+        self.inputs = [(parts, pltpu.VMEM), (one, pltpu.VMEM)]
+        self.scratch = [pltpu.VMEM((lead, all_rows, width), BF16)] + self.scratch
+
+    def run(self, parts_ref, one_ref, out_ref, summed, *refs):
+        for lead in range(self.lead):
+
+            def store(at, value, lead=lead):
+                summed[lead, at, :] = value.astype(BF16)
+
+            terms = [lambda at, lead=lead: one_ref[lead, at, :]]
+            for number in range(self.count):
+                terms.append(lambda at, lead=lead, number=number: parts_ref[lead, number, at, :])
+            add_rows(store, terms, self.all_rows)
+        yield from super().run(summed, out_ref, *refs)
 
 
 class GroupScatter:
@@ -594,16 +618,16 @@
 
 
 class ContextThenLine:
-    def __init__(self, values, axes, axis):
-        self.first = [GroupScatter(v, axes) for v in values]
-        rows, width = values[0].shape[1:]
+    def __init__(self, value, count, axes, axis):
+        self.first = [GroupScatter(value, axes, pick=number) for number in range(count)]
+        rows, width = value.shape[2:]
         total = lax.axis_size(axis)
         self.second = LineScatter(
-            jax.ShapeDtypeStruct((len(values), total, rows // total, width), BF16), axis
+            jax.ShapeDtypeStruct((count, total, rows // total, width), BF16), axis
         )
         self.inputs = [entry for job in self.first for entry in job.inputs]
         self.outputs = self.second.outputs
-        self.scratch = [pltpu.VMEM((len(values), rows, width), BF16)]
+        self.scratch = [pltpu.VMEM((count, rows, width), BF16)]
         self.scratch += [entry for job in self.first for entry in job.scratch]
         self.scratch += self.second.scratch
 
@@ -852,8 +876,13 @@
         query_grad[:, start + NOPE : start + NOPE + ROPE] = turn(
             scale * mm(moved, key_rope), cos_ref[...], -sin_ref[...]
         ).astype(BF16)
-    kv_grad_ref[0, :, :LATENT] = mm_nt(expanded_grad[...], up_w[...]).astype(BF16)
-    kv_grad_ref[0, :, LATENT:] = (scale * rope_grad).astype(BF16)
+    latent_grad = mm_nt(expanded_grad[...], up_w[...]).astype(BF16)
+    rope_grad = (scale * rope_grad).astype(BF16)
+    rows = x_ref.shape[0]
+    for block in range(kv_grad_ref.shape[0]):
+        at = slice(block * rows, (block + 1) * rows)
+        kv_grad_ref[block, 0, :, :LATENT] = latent_grad[at]
+        kv_grad_ref[block, 0, :, LATENT:] = rope_grad[at]
     x_grad_ref[...] = mm_nt(query_grad[...], query_w[...]).astype(BF16)
     pieces = (
         (query_w_sum, query_w_ref, x_ref[...], query_grad[...]),
@@ -949,9 +978,13 @@
         + place_specs
         + kept_specs[1:]
         + weight_specs,
-        out_specs=[per_micro(seq_len, LATENT + ROPE), rows_of(D)] + weight_specs,
+        out_specs=[
+            pl.BlockSpec((seq_len // rows, 1, rows, LATENT + ROPE), lambda m: (0, m, 0, 0)),
+            rows_of(D),
+        ]
+        + weight_specs,
         out_shape=[
-            jax.ShapeDtypeStruct((micro_count, seq_len, LATENT + ROPE), BF16),
+            jax.ShapeDtypeStruct((seq_len // rows, micro_count, rows, LATENT + ROPE), BF16),
             jax.ShapeDtypeStruct((total, D), BF16),
             jax.ShapeDtypeStruct(weights[0].shape, BF16),
             jax.ShapeDtypeStruct(weights[1].shape, BF16),
@@ -1767,8 +1800,6 @@
         w_shared_down,
         4,
     )
-    grad_sum = jnp.sum(grad_part.astype(F32), axis=1) + shared_part.astype(F32)
-    grad_sum = grad_sum.reshape(rows, D)
     shared_units = shared_grads.shape[1]
     shared_grads = shared_grads.reshape(groups, -1, D)
     shared_grads = lax.psum_scatter(shared_grads, GROUP, scatter_dimension=0, tiled=False)
@@ -1791,7 +1822,7 @@
     grad_attn_low, grad_one, norm_ffn_grad = exchange(
         [
             SumThenShare(
-                [to_owner(grad_sum)],
+                [LineScatterSum(grad_part, shared_part, "tensor")],
                 [hidden_one, cot_own, gain_ffn[None]],
                 finish_experts,
                 [jax.ShapeDtypeStruct(own_shape, BF16)],
@@ -1856,12 +1887,7 @@
                 [
                     to_owner(grad_x_heads),
                     ContextThenLine(
-                        [
-                            grad_kv_part[m].reshape(context_size, block_rows, LATENT + ROPE)
-                            for m in range(micro_count)
-                        ],
-                        ("context",),
-                        "tensor",
+                        grad_kv_part, micro_count, ("context",), "tensor"
                     ),
                     LineScatter(router_part, "tensor"),
                 ],
@@ -1913,8 +1939,10 @@
         10,
         80,
     )
-    query_grad, kv_up_grad, out_grad, kv_down_grad, out_sum, shared_grads = lax.optimization_barrier(
-        (query_grad, kv_up_grad, out_grad, kv_down_grad, out_sum, shared_grads)
+    query_grad, kv_up_grad, out_grad, kv_down_grad, out_sum, shared_grads, one = (
+        lax.optimization_barrier(
+            (query_grad, kv_up_grad, out_grad, kv_down_grad, out_sum, shared_grads, F32(1.0))
+        )
     )
     output = (hidden_one + out_sum.astype(F32)).astype(BF16)
     output = lax.all_gather(output, "tensor", axis=0)
@@ -1922,6 +1950,7 @@
     kv_down_grad = kv_down_grad.reshape(-1, D)[: LATENT + ROPE].astype(F32).T
     router_grad = router_grad.reshape(D, experts).astype(F32)
     small = small.reshape(-1).astype(F32)
+    gate_grad, up_grad, down_grad = gate_grad * one, up_grad * one, down_grad * one
     return (
         output.reshape(tokens.shape),
         grad_tokens.reshape(tokens.shape),

time: 813 us -> 793 us (0.975)
  local copies, waits for them, and re-layouts: 45.6 us -> 27.1 us
  waiting for transfers between devices: 23.9 us -> 10.1 us
    unnamed x73 -> x68, local copies, waits for them, and re-layouts: 20.2 us -> 5.31 us
    all_gather x1, waiting for transfers between devices: 22.6 us -> 8.38 us  [per_device(): output = lax.all_gather(output, 'tensor', axis=0)]
    transpose x0 -> x1, other arithmetic: none -> 11.3 us  [per_device(): up_grad.transpose(0, 2, 1)]
  transfers between devices with their start and end apart: 6 -> 6, of which waited for: 1 -> 2; matrix products, arithmetic and copies ran while one was open for 8% -> 8% of each run, Pallas kernels for 55% -> 58%
where the time goes in v4:
time: 793 us; the launch traced here: 788 us
  Pallas kernels  676 us (85%)
  other arithmetic  54.7 us (7%)
  local copies, waits for them, and re-layouts  27.1 us (3%)
  between operations  14.8 us (2%)
  waiting for transfers between devices  10.1 us (1%)
    pallas_call x5, Pallas kernels, exchange(): pl.pallas_call(functools.partial(exchange_kernel, jobs), out_shape=tuple(...  417 us
    pallas_call x1, Pallas kernels, expert_pass(): pl.pallas_call(functools.partial(expert_kernel, pairs, context_size, fe),...  200 us
    pallas_call x1, Pallas kernels, attend_back(): pl.pallas_call(attend_back_kernel, grid=(micro_count,), in_specs=[rows_of...  37.3 us
    pallas_call x1, Pallas kernels, attend(): pl.pallas_call(attend_kernel, grid=(micro_count,), in_specs=[rows_of(D),...  21.7 us
  transfers between devices with their start and end apart: 6, of which 2 were waited for; matrix products, arithmetic and copies ran while one was open for 8% of the time, Pallas kernels for 58%

profile of v4, /device:TPU:0, one launch (start us, length us, event | category | flops | bytes accessed | tf_op | source)
XLA Modules:
  0.0 787.9 jit_solution(2234729199822106913)
XLA Ops:
  7.3 0.8 convert_element_type.114
  8.1 2.1 multiply_reduce_fusion
  10.2 0.7 convert_element_type.112
  12.9 1.1 copy-done.9
  14.0 1.4 fusion.8
  15.4 1.1 fusion.6
  17.2 1.7 copy.97
  18.9 0.9 copy.113
  19.8 21.8 %exchange_GroupGather.1 = bf16[2,2,256,1280]{3,2,1,0:T(8,128)(2,1)} custom-call(bf16[256,1280]{1,0:T(8,128)(2,1)} %bitcast.103), custom_call_target="tpu_custom_call" | custom-call | bytes 7200000 | tf_op jit(solution)/shard_map/exchange_GroupGather/pallas_call | solution.py:744
  41.7 0.6 broadcast_in_dim.16.column_ref
  43.6 0.9 copy.99.row_ref
  44.5 0.8 copy.100.cos_ref
  45.3 0.7 iota_add_fusion.row_place_ref
  45.9 0.7 pad_maximum_fusion.1.sin_ref
  46.7 0.8 constant_dynamic-slice_fusion.3.refs_1_.refs_4_
  48.1 21.7 %attend.1 = (bf16[512,2048]{1,0:T(8,128)(2,1)}, bf16[512,512]{1,0:T(8,128)(2,1)}, bf16[2,4,256,192]{3,2,1,0:T(8,128)(2,1)}, bf16[2,1024,1024]{2,1,0:T(8,128)(2,1)}, f32[2,4,256,1]{3,2,1,0:T(8,128)}) custom-call(bf16[512,2048]{1,0:T(8,128)(2,1)} %copy-done.1, bf16[1024,1280]{1,0:T(8,128)(2,1)} %bitcast.92, s32[2,256,1]{2,1,0:T(8,128)} %copy.99.row_ref, ...), custom_call_target="tpu_custom_call" | custom-call | flops 8999999488 | bytes 60000000 | tf_op jit(solution)/shard_map/attend/pallas_call | solution.py:948
  69.8 80.0 %exchange_SumThenShare.3 = (bf16[2,4,64,2048]{3,2,1,0:T(8,128)(2,1)}, f32[2,64,2048]{2,1,0:T(8,128)}) custom-call(bf16[2,256,2048]{2,1,0:T(8,128)(2,1)} %bitcast.111, bf16[2,64,2048]{2,1,0:T(8,128)(2,1)} %constant_dynamic-slice_fusion.3.refs_1_.refs_4_, f32[1,2048]{1,0:T(1,128)} %bitcast.126), custom_call_target="tpu_custom_call" | custom-call | bytes 28800000 | tf_op jit(solution)/shard_map/exchange_SumThenShare/pallas_call | solution.py:744
  149.8 3.2 pad_maximum_fusion.x_ref
  153.0 200.3 %expert_pass.1 = (bf16[8,2,256,2048]{3,2,1,0:T(8,128)(2,1)}, bf16[2,4,256,2048]{3,2,1,0:T(8,128)(2,1)}, f32[2,352,2048]{2,1,0:T(8,128)}, f32[2,352,2048]{2,1,0:T...) custom-call(bf16[2,256,2176]{2,1,0:T(8,128)(2,1)} %pad_maximum_fusio, ...), custom_call_target="tpu_custom_call" | custom-call | flops 130459631616 | bytes 500000000 | tf_op jit(solution)/shard_map/expert_pass/pallas_call | solution.py:1603
  353.4 0.7 reduce-scatter.6.cloned.1.call-update
  354.5 0.7 copy.110.refs_8_
  355.6 0.7 fusion.3.refs_9_
  356.3 0.7 constant_dynamic-slice_fusion.1.refs_7_
  357.0 1.9 constant_dynamic-slice_fusion.2.refs_3_
  359.2 1.0 reshape_reshape.30.refs_3_
  360.2 81.8 %exchange_SumThenShare.4 = (bf16[2,4,64,2048]{3,2,1,0:T(8,128)(2,1)}, f32[2,64,2048]{2,1,0:T(8,128)}, f32[1,2048]{1,0:T(1,128)}) custom-call(bf16[2,4,256,2048]{3,2,1,0:T(8,128)(2,1)} %get-tuple-element.67.refs_0_, bf16[2,256,2048]{2,1,0:T(8,128)(2,1)} %get-tuple-element.68.refs_1_, f32[2,64,2048]{2,1,0:T(8,128)} %get-tuple-element.64.refs_2_, ...), custom_call_target="tpu_custom_call" | custom-call | bytes 32400000 | tf_op jit(solution)/shard_map/exchange_SumThenShare/pallas_call | solution.py:744
  442.6 37.3 %attend_back.1 = (bf16[4,2,256,576]{3,2,1,0:T(8,128)(2,1)}, bf16[512,2048]{1,0:T(8,128)(2,1)}, bf16[2048,768]{1,0:T(8,128)(2,1)}, bf16[512,1024]{1,0:T(8,128)(2,1)}, bf16[512,2048]{1,0:T(8,128)(2,1)}) custom-call(bf16[512,2048]{1,0:T(8,128)(2,1)} %bitcast.116, bf16[512,512]{1,0:T(8,128)(2,1)} %get-tuple-element.70.attended_ref, bf16[512,2048]{1,0:T(8,128)(2,1)} %copy-done.1, ...), custom_call_target="tpu_custom_call" | custom-call | flops 2000000000 | bytes 10000000 | tf_op jit(solution)/shard_map/attend_back/pallas_call | solution.py:974
  480.0 110.1 %exchange_SumThenShare.5 = (bf16[2,4,64,2624]{3,2,1,0:T(8,128)(2,1)}, bf16[1,4,64,128]{3,2,1,0:T(8,128)(2,1)}, f32[1,4,1,4608]{3,2,1,0:T(1,128)}) custom-call(bf16[2,256,2048]{2,1,0:T(8,128)(2,1)} %bitcast.110, bf16[2,2,2,256,576]{4,3,2,1,0:T(8,128)(2,1)} %bitcast.90, bf16[2,2,2,256,576]{4,3,2,1,0:T(8,128)(2,1)} %bitcast.91, ...), custom_call_target="tpu_custom_call" | custom-call | bytes 36000000 | tf_op jit(solution)/shard_map/exchange_SumThenShare/pallas_call | solution.py:744
  590.1 2.4 add_convert_fusion
  592.5 1.5 copy.115
  594.9 0.7 convert_element_type.123.refs_5_
  595.6 0.7 reshape_reshape_reshape.4.refs_4_
  596.4 1.6 slice.43
  598.5 3.1 convolution_convert_fusion
  601.6 123.3 %exchange_GroupSum_GroupSum_GroupSum.1 = (bf16[4,2,256,768]{3,2,1,0:T(8,128)(2,1)}, bf16[4,2,64,1024]{3,2,1,0:T(8,128)(2,1)}, bf16[4,2,64,2048]{3,2,1,0:T(8,128)...) custom-call(bf16[4,2,256,768]{3,2,1,0:T(8,128)(2,1)} %bitcast.99, ...), custom_call_target="tpu_custom_call" | custom-call | bytes 28800000 | tf_op jit(solution)/shard_map/exchange_GroupSum_GroupSum_GroupSum/pallas_call | solution.py:744
  724.9 1.0 reshape.213
  726.5 1.2 reshape.217
  727.6 1.0 copy.109
  729.6 1.9 add_convert_fusion.1
  731.6 4.6 convert_bitcast_fusion.2
  736.2 3.9 bitcast_convert_fusion
  740.2 2.7 bitcast_convert_fusion.1
  742.9 1.6 bitcast_convert_fusion.2
  744.5 3.0 broadcast_multiply_fusion
  747.5 10.5 %slice_convert_fusion = (f32[704,2048]{1,0:T(8,128)}, f32[2048,704]{0,1:T(8,128)}, f32[2048,704]{0,1:T(8,128)}) fusion(bf16[2304,2048]{1,0:T(8,128)(2,1)} %all-gather.6.cloned.1.call-done), kind=kLoop, calls=%fused_computation.13 | loop fusion | flops 4325376 | bytes 25952256 | tf_op jit(solution)/shard_map/convert_element_type | solution.py:1967
  758.0 11.3 %multiply_bitcast_fusion = (f32[2,2048,352]{1,2,0:T(8,128)}, f32[2,2048,352]{1,2,0:T(8,128)}) fusion(f32[2,352,2048]{2,1,0:T(8,128)} %get-tuple-element.106, f32[]{:T(128)} %constant.41.clone.1, f32[2,352,2048]{2,1,0:T(8,128)} %get-tuple-element.104), kind=kLoop, calls=%fused_computation.2 | loop fusion | flops 2883584 | bytes 23068676 | tf_op jit(solution)/shard_map/transpose | solution.py:1969
  769.3 8.4 %all-gather.10.cloned.1.call-done = bf16[8,64,2048]{2,1,0:T(8,128)(2,1)} async-done(((bf16[2,64,2048]{2,1,0:T(8,128)(2,1)}), bf16[8,64,2048]{2,1,0:T(8,128)(2,1)}) %all-gather.10.cloned.1.call-update) | async-done | bytes 2097168 | tf_op jit(solution)/shard_map/all_gather | solution.py:1948
  777.7 3.2 copy.108
  (116 shorter events, 9.5 us)
Async XLA Ops:
  7.2 5.1 copy-start
  7.2 145.8 %all-gather.8.cloned.1.call-start = ((), (), s32[]{:S(2)}) async-start(), calls=%async_computation.7 | async-start | bytes 18874368 | tf_op jit(solution)/shard_map/all_gather | solution.py:1743
  8.1 8.6 %copy-start.25 = (f32[512]{0:T(512)}, f32[512]{0:T(512)S(1)}, u32[]{:S(2)}) copy-start(f32[512]{0:T(512)S(1)} %convert_element_type.114) | copy-start | bytes 6148
  10.9 2.0 copy-start.22
  11.4 1.4 copy-start.14
  11.4 34.5 %copy-start.12 = (f32[256,32]{1,0:T(8,128)}, f32[256,32]{1,0:T(8,128)S(1)}, u32[]{:S(2)}) copy-start(f32[256,32]{1,0:T(8,128)S(1)} %get-tuple-element.197) | copy-start | bytes 98308
  11.5 0.6 copy-start.19
  12.1 4.5 copy-start.17
  12.2 3.2 copy-start.7
  12.3 1.7 copy-start.9
  14.0 1.4 copy-start.1
  19.8 22.0 %copy-start.26 = (s32[2,1024]{1,0:T(2,128)S(1)}, s32[2,1024]{1,0:T(2,128)}, u32[]{:S(2)}) copy-start(s32[2,1024]{1,0:T(2,128)} %param.19) | copy-start | bytes 24580
  19.8 22.6 %copy-start.28 = (bf16[2048]{0:T(1024)(128)(2,1)S(1)}, bf16[2048]{0:T(1024)(128)(2,1)}, u32[]{:S(2)}) copy-start(bf16[2048]{0:T(1024)(128)(2,1)} %param.27) | copy-start | bytes 12292
  19.8 23.2 %copy-start.27 = (s32[2,256,6]{1,0,2:T(2,128)S(1)}, s32[2,256,6]{1,0,2:T(2,128)}, u32[]{:S(2)}) copy-start(s32[2,256,6]{1,0,2:T(2,128)} %param.20) | copy-start | bytes 36868
  19.8 24.7 %copy-start.20 = (f32[256,32]{0,1:T(8,128)S(1)}, f32[256,32]{0,1:T(8,128)}, u32[]{:S(2)}) copy-start(f32[256,32]{0,1:T(8,128)} %copy-done.19) | copy-start | bytes 98308
  19.8 26.1 %copy-start.15 = (f32[256,32]{1,0:T(8,128)S(1)}, f32[256,32]{1,0:T(8,128)}, u32[]{:S(2)}) copy-start(f32[256,32]{1,0:T(8,128)} %copy-done.14) | copy-start | bytes 98308
  41.7 438.3 %reduce-scatter.4.cloned.1.call-start = ((), (), s32[]{:S(2)}) async-start(), calls=%async_computation.3 | async-start | bytes 10616832 | tf_op jit(solution)/shard_map/reduce_scatter | solution.py:1805
  353.3 236.8 %reduce-scatter.6.cloned.1.call-start = ((), (), s32[]{:S(2)}) async-start(), calls=%async_computation.4 | async-start | bytes 18874368 | tf_op jit(solution)/shard_map/reduce_scatter | solution.py:1821
  353.4 0.8 copy-start.18
  353.4 1.8 copy-start.4
  354.1 1.5 copy-start.13
  354.1 1.5 copy-start.8
  354.1 375.1 %reduce-scatter.8.cloned.1.call-start = ((), (), s32[]{:S(2)}) async-start(), calls=%async_computation.5 | async-start | bytes 2621440 | tf_op jit(solution)/shard_map/reduce_scatter | solution.py:1921
  354.2 4.7 copy-start.21
  480.0 110.1 %copy-start.10 = (bf16[2,256,2048]{2,1,0:T(8,128)(2,1)S(1)}, bf16[2,256,2048]{2,1,0:T(8,128)(2,1)}, u32[]{:S(2)}) copy-start(bf16[2,256,2048]{2,1,0:T(8,128)(2,1)} %get-tuple-element.94) | copy-start | bytes 6291460
  593.9 0.9 copy-start.23
  593.9 1.7 copy-start.24
  593.9 2.4 copy-start.6
  593.9 135.7 %all-gather.6.cloned.1.call-start = ((), (), s32[]{:S(2)}) async-start(), calls=%async_computation.6 | async-start | bytes 10616832 | tf_op jit(solution)/shard_map/all_gather | solution.py:1843
  594.5 183.1 %all-gather.10.cloned.1.call-start = ((), (), s32[]{:S(2)}) async-start(), calls=%async_computation.8 | async-start | bytes 2621440 | tf_op jit(solution)/shard_map/all_gather | solution.py:1948
  596.3 2.3 copy-start.2
  724.9 4.7 copy-start.3
  731.6 4.6 copy-start.5
  736.2 3.9 copy-start.11
  736.2 8.3 %slice-start = ((s8[5767168]{0:T(1024)(128)(4,1)}), s8[4194304]{0:T(1024)(128)(4,1)S(1)}, s32[]{:S(2)}) async-start(s8[5767168]{0:T(1024)(128)(4,1)} %bitcast.97), calls=%async_computation.9 | async-start | bytes 8388608
  740.2 2.7 copy-start.16
  740.2 4.3 slice-start.1
Sparse Core Ops, SparseCore 0:
  41.8 90.6 all-gather.7
  353.4 76.9 reduce-scatter.3
  434.0 129.8 reduce-scatter.5
  594.1 43.2 reduce-scatter.7
  639.2 90.3 all-gather.5
  731.7 45.8 all-gather.9

commit v5 on v4

--- a/solution.py
+++ b/solution.py
@@ -1417,16 +1417,17 @@
     for which, (left, right) in enumerate(
         ((grad_gate, x_tile[1, :, :D]), (grad_up, x_tile[1, :, :D]), (hidden_low, cot_tile[1]))
     ):
-        for start in range(0, units, rows):
+        for start in range(0, shared_units, rows):
             stage = len(staged) % 2 * rows
+            count = min(rows, shared_units - start)
             if len(staged) >= 2:
                 staged[-2].wait()
             out_tile[stage : stage + rows, :] = mm_tn(
                 left[:, start : start + rows], right
             ).astype(BF16)
             copy = pltpu.make_async_copy(
-                out_tile.at[pl.ds(stage, rows)],
-                shared_grads.at[which, pl.ds(start, rows)],
+                out_tile.at[pl.ds(stage, count)],
+                shared_grads.at[which, pl.ds(start, count)],
                 grad_store.at[len(staged) % 2],
             )
             copy.start()
@@ -1611,7 +1612,7 @@
             jax.ShapeDtypeStruct((experts, D), F32),
             own,
             own,
-            jax.ShapeDtypeStruct((3, units, D), BF16),
+            jax.ShapeDtypeStruct((3, shared_units, D), BF16),
             jax.ShapeDtypeStruct((micro_count, pairs, 2, rows, width), BF16),
         ),
         in_specs=[pl.BlockSpec(memory_space=pl.ANY)] * 9,

time: 793 us -> 769 us (0.970)
  Pallas kernels: 676 us -> 654 us
    pallas_call x5, Pallas kernels: 417 us -> 395 us  [exchange(): pl.pallas_call(functools.partial(exchange_kernel, jobs), out_shape=tuple(...]
  transfers between devices with their start and end apart: 6 -> 6, of which waited for: 2 -> 1; matrix products, arithmetic and copies ran while one was open for 8% -> 9% of each run, Pallas kernels for 58% -> 57%
where the time goes in v5:
time: 769 us; the launch traced here: 764 us
  Pallas kernels  654 us (85%)
  other arithmetic  54.7 us (7%)
  local copies, waits for them, and re-layouts  26.8 us (3%)
  between operations  14.9 us (2%)
  waiting for transfers between devices  9.27 us (1%)
    pallas_call x5, Pallas kernels, exchange(): pl.pallas_call(functools.partial(exchange_kernel, jobs), out_shape=tuple(...  395 us
    pallas_call x1, Pallas kernels, expert_pass(): pl.pallas_call(functools.partial(expert_kernel, pairs, context_size, fe),...  200 us
    pallas_call x1, Pallas kernels, attend_back(): pl.pallas_call(attend_back_kernel, grid=(micro_count,), in_specs=[rows_of...  36.9 us
    pallas_call x1, Pallas kernels, attend(): pl.pallas_call(attend_kernel, grid=(micro_count,), in_specs=[rows_of(D),...  21.7 us
  transfers between devices with their start and end apart: 6, of which 1 were waited for; matrix products, arithmetic and copies ran while one was open for 9% of the time, Pallas kernels for 57%

profile of v5, /device:TPU:0, one launch (start us, length us, event | category | flops | bytes accessed | tf_op | source)
XLA Modules:
  0.0 764.5 jit_solution(4138704720378530778)
XLA Ops:
  7.3 0.8 convert_element_type.114
  8.1 2.1 multiply_reduce_fusion
  10.2 0.7 convert_element_type.112
  12.9 1.1 copy-done.9
  14.0 1.4 fusion.8
  15.4 1.1 fusion.6
  17.2 1.7 copy.97
  18.9 0.9 copy.113
  19.8 21.8 %exchange_GroupGather.1 = bf16[2,2,256,1280]{3,2,1,0:T(8,128)(2,1)} custom-call(bf16[256,1280]{1,0:T(8,128)(2,1)} %bitcast.103), custom_call_target="tpu_custom_call" | custom-call | bytes 7200000 | tf_op jit(solution)/shard_map/exchange_GroupGather/pallas_call | solution.py:744
  41.7 0.6 broadcast_in_dim.16.column_ref
  43.6 0.9 copy.99.row_ref
  44.5 0.8 copy.100.cos_ref
  45.2 0.7 iota_add_fusion.row_place_ref
  45.9 0.7 pad_maximum_fusion.1.sin_ref
  46.7 0.8 constant_dynamic-slice_fusion.3.refs_1_.refs_4_
  48.1 21.7 %attend.1 = (bf16[512,2048]{1,0:T(8,128)(2,1)}, bf16[512,512]{1,0:T(8,128)(2,1)}, bf16[2,4,256,192]{3,2,1,0:T(8,128)(2,1)}, bf16[2,1024,1024]{2,1,0:T(8,128)(2,1)}, f32[2,4,256,1]{3,2,1,0:T(8,128)}) custom-call(bf16[512,2048]{1,0:T(8,128)(2,1)} %copy-done.1, bf16[1024,1280]{1,0:T(8,128)(2,1)} %bitcast.92, s32[2,256,1]{2,1,0:T(8,128)} %copy.99.row_ref, ...), custom_call_target="tpu_custom_call" | custom-call | flops 8999999488 | bytes 60000000 | tf_op jit(solution)/shard_map/attend/pallas_call | solution.py:948
  69.8 80.0 %exchange_SumThenShare.3 = (bf16[2,4,64,2048]{3,2,1,0:T(8,128)(2,1)}, f32[2,64,2048]{2,1,0:T(8,128)}) custom-call(bf16[2,256,2048]{2,1,0:T(8,128)(2,1)} %bitcast.111, bf16[2,64,2048]{2,1,0:T(8,128)(2,1)} %constant_dynamic-slice_fusion.3.refs_1_.refs_4_, f32[1,2048]{1,0:T(1,128)} %bitcast.126), custom_call_target="tpu_custom_call" | custom-call | bytes 28800000 | tf_op jit(solution)/shard_map/exchange_SumThenShare/pallas_call | solution.py:744
  149.8 3.2 pad_maximum_fusion.x_ref
  153.0 200.1 %expert_pass.1 = (bf16[8,2,256,2048]{3,2,1,0:T(8,128)(2,1)}, bf16[2,4,256,2048]{3,2,1,0:T(8,128)(2,1)}, f32[2,352,2048]{2,1,0:T(8,128)}, f32[2,352,2048]{2,1,0:T...) custom-call(bf16[2,256,2176]{2,1,0:T(8,128)(2,1)} %pad_maximum_fusio, ...), custom_call_target="tpu_custom_call" | custom-call | flops 130459631616 | bytes 500000000 | tf_op jit(solution)/shard_map/expert_pass/pallas_call | solution.py:1604
  353.2 0.7 reduce-scatter.6.cloned.1.call-update
  353.9 1.9 constant_dynamic-slice_fusion.2.refs_3_
  355.8 78.8 %exchange_SumThenShare.4 = (bf16[2,4,64,2048]{3,2,1,0:T(8,128)(2,1)}, f32[2,64,2048]{2,1,0:T(8,128)}, f32[1,2048]{1,0:T(1,128)}) custom-call(bf16[2,4,256,2048]{3,2,1,0:T(8,128)(2,1)} %get-tuple-element.67.refs_0_, bf16[2,256,2048]{2,1,0:T(8,128)(2,1)} %get-tuple-element.68.refs_1_, f32[2,64,2048]{2,1,0:T(8,128)} %get-tuple-element.64.refs_2_, ...), custom_call_target="tpu_custom_call" | custom-call | bytes 32400000 | tf_op jit(solution)/shard_map/exchange_SumThenShare/pallas_call | solution.py:744
  435.3 36.9 %attend_back.1 = (bf16[4,2,256,576]{3,2,1,0:T(8,128)(2,1)}, bf16[512,2048]{1,0:T(8,128)(2,1)}, bf16[2048,768]{1,0:T(8,128)(2,1)}, bf16[512,1024]{1,0:T(8,128)(2,1)}, bf16[512,2048]{1,0:T(8,128)(2,1)}) custom-call(bf16[512,2048]{1,0:T(8,128)(2,1)} %bitcast.116, bf16[512,512]{1,0:T(8,128)(2,1)} %get-tuple-element.70.attended_ref, bf16[512,2048]{1,0:T(8,128)(2,1)} %copy-done.1, ...), custom_call_target="tpu_custom_call" | custom-call | flops 2000000000 | bytes 10000000 | tf_op jit(solution)/shard_map/attend_back/pallas_call | solution.py:974
  472.6 0.7 copy.110.refs_8_
  473.7 0.7 fusion.3.refs_9_
  474.4 0.7 constant_dynamic-slice_fusion.1.refs_7_
  475.5 1.0 reshape_reshape.30.refs_3_
  476.4 112.0 %exchange_SumThenShare.5 = (bf16[2,4,64,2624]{3,2,1,0:T(8,128)(2,1)}, bf16[1,4,64,128]{3,2,1,0:T(8,128)(2,1)}, f32[1,4,1,4608]{3,2,1,0:T(1,128)}) custom-call(bf16[2,256,2048]{2,1,0:T(8,128)(2,1)} %bitcast.110, bf16[2,2,2,256,576]{4,3,2,1,0:T(8,128)(2,1)} %bitcast.90, bf16[2,2,2,256,576]{4,3,2,1,0:T(8,128)(2,1)} %bitcast.91, ...), custom_call_target="tpu_custom_call" | custom-call | bytes 36000000 | tf_op jit(solution)/shard_map/exchange_SumThenShare/pallas_call | solution.py:744
  588.5 2.4 add_convert_fusion
  590.9 1.5 copy.115
  592.5 0.7 convert_element_type.123.refs_5_
  593.3 0.7 reshape_reshape_reshape.4.refs_4_
  594.0 1.6 slice.43
  596.2 3.1 convolution_convert_fusion
  599.3 102.6 %exchange_GroupSum_GroupSum_GroupSum.1 = (bf16[4,2,256,768]{3,2,1,0:T(8,128)(2,1)}, bf16[4,2,64,1024]{3,2,1,0:T(8,128)(2,1)}, bf16[4,2,64,2048]{3,2,1,0:T(8,128)...) custom-call(bf16[4,2,256,768]{3,2,1,0:T(8,128)(2,1)} %bitcast.99, ...), custom_call_target="tpu_custom_call" | custom-call | bytes 28800000 | tf_op jit(solution)/shard_map/exchange_GroupSum_GroupSum_GroupSum/pallas_call | solution.py:744
  701.9 1.0 reshape.213
  703.4 1.2 reshape.217
  704.6 1.0 copy.109
  706.1 1.9 add_convert_fusion.1
  708.1 4.6 convert_bitcast_fusion.2
  712.7 3.9 bitcast_convert_fusion
  716.7 2.7 bitcast_convert_fusion.1
  719.4 1.6 bitcast_convert_fusion.2
  721.0 3.0 broadcast_multiply_fusion
  724.0 10.5 %slice_convert_fusion = (f32[704,2048]{1,0:T(8,128)}, f32[2048,704]{0,1:T(8,128)}, f32[2048,704]{0,1:T(8,128)}) fusion(bf16[2112,2048]{1,0:T(8,128)(2,1)} %all-gather.6.cloned.1.call-done), kind=kLoop, calls=%fused_computation.13 | loop fusion | flops 4325376 | bytes 25952256 | tf_op jit(solution)/shard_map/convert_element_type | solution.py:1968
  734.5 11.3 %multiply_bitcast_fusion = (f32[2,2048,352]{1,2,0:T(8,128)}, f32[2,2048,352]{1,2,0:T(8,128)}) fusion(f32[2,352,2048]{2,1,0:T(8,128)} %get-tuple-element.106, f32[]{:T(128)} %constant.41.clone.1, f32[2,352,2048]{2,1,0:T(8,128)} %get-tuple-element.104), kind=kLoop, calls=%fused_computation.2 | loop fusion | flops 2883584 | bytes 23068676 | tf_op jit(solution)/shard_map/transpose | solution.py:1970
  745.8 8.5 %all-gather.10.cloned.1.call-done = bf16[8,64,2048]{2,1,0:T(8,128)(2,1)} async-done(((bf16[2,64,2048]{2,1,0:T(8,128)(2,1)}), bf16[8,64,2048]{2,1,0:T(8,128)(2,1)}) %all-gather.10.cloned.1.call-update) | async-done | bytes 2097168 | tf_op jit(solution)/shard_map/all_gather | solution.py:1949
  754.3 3.2 copy.108
  (116 shorter events, 8.2 us)
Async XLA Ops:
  7.2 5.1 copy-start
  7.2 145.8 %all-gather.8.cloned.1.call-start = ((), (), s32[]{:S(2)}) async-start(), calls=%async_computation.7 | async-start | bytes 18874368 | tf_op jit(solution)/shard_map/all_gather | solution.py:1744
  8.1 8.6 %copy-start.25 = (f32[512]{0:T(512)}, f32[512]{0:T(512)S(1)}, u32[]{:S(2)}) copy-start(f32[512]{0:T(512)S(1)} %convert_element_type.114) | copy-start | bytes 6148
  10.9 2.0 copy-start.22
  11.4 1.4 copy-start.14
  11.4 34.5 %copy-start.12 = (f32[256,32]{1,0:T(8,128)}, f32[256,32]{1,0:T(8,128)S(1)}, u32[]{:S(2)}) copy-start(f32[256,32]{1,0:T(8,128)S(1)} %get-tuple-element.197) | copy-start | bytes 98308
  11.5 0.6 copy-start.19
  12.1 4.5 copy-start.17
  12.2 3.2 copy-start.7
  12.3 1.7 copy-start.9
  14.0 1.4 copy-start.1
  19.8 22.0 %copy-start.26 = (s32[2,1024]{1,0:T(2,128)S(1)}, s32[2,1024]{1,0:T(2,128)}, u32[]{:S(2)}) copy-start(s32[2,1024]{1,0:T(2,128)} %param.19) | copy-start | bytes 24580
  19.8 22.6 %copy-start.28 = (bf16[2048]{0:T(1024)(128)(2,1)S(1)}, bf16[2048]{0:T(1024)(128)(2,1)}, u32[]{:S(2)}) copy-start(bf16[2048]{0:T(1024)(128)(2,1)} %param.27) | copy-start | bytes 12292
  19.8 23.2 %copy-start.27 = (s32[2,256,6]{1,0,2:T(2,128)S(1)}, s32[2,256,6]{1,0,2:T(2,128)}, u32[]{:S(2)}) copy-start(s32[2,256,6]{1,0,2:T(2,128)} %param.20) | copy-start | bytes 36868
  19.8 24.7 %copy-start.20 = (f32[256,32]{0,1:T(8,128)S(1)}, f32[256,32]{0,1:T(8,128)}, u32[]{:S(2)}) copy-start(f32[256,32]{0,1:T(8,128)} %copy-done.19) | copy-start | bytes 98308
  19.8 26.1 %copy-start.15 = (f32[256,32]{1,0:T(8,128)S(1)}, f32[256,32]{1,0:T(8,128)}, u32[]{:S(2)}) copy-start(f32[256,32]{1,0:T(8,128)} %copy-done.14) | copy-start | bytes 98308
  41.7 430.6 %reduce-scatter.4.cloned.1.call-start = ((), (), s32[]{:S(2)}) async-start(), calls=%async_computation.3 | async-start | bytes 9732096 | tf_op jit(solution)/shard_map/reduce_scatter | solution.py:1806
  353.1 235.3 %reduce-scatter.6.cloned.1.call-start = ((), (), s32[]{:S(2)}) async-start(), calls=%async_computation.4 | async-start | bytes 18874368 | tf_op jit(solution)/shard_map/reduce_scatter | solution.py:1822
  353.9 352.3 %all-gather.6.cloned.1.call-start = ((), (), s32[]{:S(2)}) async-start(), calls=%async_computation.6 | async-start | bytes 9732096 | tf_op jit(solution)/shard_map/all_gather | solution.py:1844
  435.3 37.1 %copy-start.18 = (f32[4,8,2,256]{3,1,2,0:T(8,128)S(1)}, f32[4,8,2,256]{3,1,2,0:T(8,128)}, u32[]{:S(2)}) copy-start(f32[4,8,2,256]{3,1,2,0:T(8,128)} %copy-done.17) | copy-start | bytes 196612
  435.3 38.1 %copy-start.4 = (f32[512,512]{0,1:T(8,128)S(1)}, f32[512,512]{0,1:T(8,128)}, u32[]{:S(2)}) copy-start(f32[512,512]{0,1:T(8,128)} %get-tuple-element.193) | copy-start | bytes 3145732
  472.2 1.5 copy-start.13
  472.2 1.5 copy-start.8
  472.3 2.9 copy-start.21
  472.3 233.8 %reduce-scatter.8.cloned.1.call-start = ((), (), s32[]{:S(2)}) async-start(), calls=%async_computation.5 | async-start | bytes 2621440 | tf_op jit(solution)/shard_map/reduce_scatter | solution.py:1922
  476.4 112.1 %copy-start.10 = (bf16[2,256,2048]{2,1,0:T(8,128)(2,1)S(1)}, bf16[2,256,2048]{2,1,0:T(8,128)(2,1)}, u32[]{:S(2)}) copy-start(bf16[2,256,2048]{2,1,0:T(8,128)(2,1)} %get-tuple-element.94) | copy-start | bytes 6291460
  590.9 1.6 copy-start.23
  590.9 2.4 copy-start.24
  590.9 3.0 copy-start.6
  592.4 161.9 %all-gather.10.cloned.1.call-start = ((), (), s32[]{:S(2)}) async-start(), calls=%async_computation.8 | async-start | bytes 2621440 | tf_op jit(solution)/shard_map/all_gather | solution.py:1949
  593.9 2.3 copy-start.2
  701.8 4.3 copy-start.3
  708.1 4.6 copy-start.5
  712.7 3.9 copy-start.11
  712.7 8.3 %slice-start = ((s8[5767168]{0:T(1024)(128)(4,1)}), s8[4194304]{0:T(1024)(128)(4,1)S(1)}, s32[]{:S(2)}) async-start(s8[5767168]{0:T(1024)(128)(4,1)} %bitcast.97), calls=%async_computation.9 | async-start | bytes 8388608
  716.7 2.7 copy-start.16
  716.7 4.3 slice-start.1
Sparse Core Ops, SparseCore 0:
  41.8 90.6 all-gather.7
  353.3 73.0 reduce-scatter.3
  430.4 129.9 reduce-scatter.5
  562.3 64.6 all-gather.5
  629.8 53.6 reduce-scatter.7
  708.2 45.9 all-gather.9
